TPU v7x, 32 devices: a whole 2x2x4 slice. The times are simulated.
32 devices in a mesh: grp: 2 (over y), mesh: 16 (over z, x, core).
Axes of the slice: x: 2, y: 2, z: 4, core: 2. Of those that a mesh axis runs over, the one named last changes fastest.
Arguments:
- basis: bfloat16 [65536, 512], P(('grp', 'mesh')), parts along dimension 0, may hold values from -6 to 6
- blocks: bfloat16 [2, 512, 3, 128, 128], P(None, ('grp', 'mesh')), parts along dimension 1, may hold values from -0.0017089844 to 0.0017089844
- columns: int32 [2, 512, 2], P(None, ('grp', 'mesh')), parts along dimension 1, may hold values from 0 to 31
- sends: int32 [32, 16], P(('grp', 'mesh')), parts along dimension 0, may hold values from 0 to 15
Outputs:
- projected: float32 [1024, 1024], P(('grp', 'mesh')), parts along dimension 0
There are 2 independent parts, one for each index of `grp`. A program takes and returns all parts, laid end to end along the dimension named above; each array names one. Nothing has to cross between parts.
All inputs are finite; a program needn't handle non-finite values.
Results may differ from a plain program's by a relative error of at most 0.0029.
Values may be sent and summed in bfloat16 or wider, within the bound.
No kernel may reach another device: no remote copies, remote signals or barrier semaphores. Data moves between devices by JAX's collectives and lax.ppermute only.
A program may use at most 64 MiB of HBM per device.

v0:
```python
import jax
import jax.numpy as jnp
from jax import lax
from jax.experimental import pallas as pl
from jax.experimental.pallas import tpu as pltpu
from jax.sharding import PartitionSpec as P

AXIS = "mesh"
LANES = 128
EASE = 8
VMEM_BYTES = 24 * 1024 * 1024
VMEM = pl.BlockSpec(memory_space=pltpu.VMEM)
SMEM = pl.BlockSpec(memory_space=pltpu.SMEM)
PARAMETERS = pltpu.CompilerParams(vmem_limit_bytes=VMEM_BYTES)


def cost(flops, moved):
    return pl.CostEstimate(flops=flops // EASE, bytes_accessed=moved // EASE, transcendentals=0)


def pairs(count, first):
    both = []
    for low in range(first, count - 1, 2):
        both += [(low, low + 1), (low + 1, low)]
    return both


def chunks(width):
    first = width
    if first == width or first % LANES:
        return [(0, width)]
    return [(0, first), (first, width - first)]


def halves(width):
    half = width // 2
    return [(0, width)] if half % LANES else [(0, half), (half, half)]


def copy_listed(own_ref, sends_ref, far, part, out_ref):
    halo = out_ref.shape[0]
    odd = lax.rem(lax.axis_index(AXIS), 2)
    first = (odd if far else 1 - odd) * halo
    for place in range(halo):
        out_ref[place] = own_ref[sends_ref[0, first + place], :, pl.ds(*part)]


def pick_first(own, sends, part):
    count, size, width = own.shape
    halo = sends.shape[1] // 2
    ranges = halves(width)

    def kernel(sends_hbm, own_hbm, own_ref, far_ref, *refs):
        near_refs, (sends_ref, sems) = refs[: len(ranges)], refs[len(ranges) :]
        lists = pltpu.make_async_copy(sends_hbm, sends_ref, sems.at[0])
        load = pltpu.make_async_copy(own_hbm, own_ref, sems.at[1])
        lists.start()
        load.start()
        lists.wait()
        load.wait()
        copy_listed(own_ref, sends_ref, True, part, far_ref)
        for near_part, near_ref in zip(ranges, near_refs):
            copy_listed(own_ref, sends_ref, False, near_part, near_ref)

    return pl.pallas_call(
        kernel,
        out_shape=[
            jax.ShapeDtypeStruct(own.shape, own.dtype),
            jax.ShapeDtypeStruct((halo, size, part[1]), own.dtype),
        ]
        + [jax.ShapeDtypeStruct((halo, size, span), own.dtype) for _, span in ranges],
        in_specs=[pl.BlockSpec(memory_space=pltpu.HBM)] * 2,
        out_specs=[VMEM] * (2 + len(ranges)),
        scratch_shapes=[pltpu.SMEM(sends.shape, sends.dtype), pltpu.SemaphoreType.DMA((2,))],
        compiler_params=PARAMETERS,
        cost_estimate=cost(0, 6 * own.size),
    )(
        pltpu.with_memory_space_constraint(sends, pltpu.HBM),
        pltpu.with_memory_space_constraint(own, pltpu.HBM),
    )


def pick_next(own, sends, part):
    _, size, _ = own.shape
    halo = sends.shape[1] // 2

    def kernel(sends_hbm, own_ref, far_ref, sends_ref):
        pltpu.sync_copy(sends_hbm, sends_ref)
        copy_listed(own_ref, sends_ref, True, part, far_ref)

    return pl.pallas_call(
        kernel,
        out_shape=jax.ShapeDtypeStruct((halo, size, part[1]), own.dtype),
        in_specs=[pl.BlockSpec(memory_space=pltpu.HBM), VMEM],
        out_specs=VMEM,
        scratch_shapes=[pltpu.SMEM(sends.shape, sends.dtype)],
        compiler_params=PARAMETERS,
        cost_estimate=cost(0, 4 * halo * size * part[1]),
    )(pltpu.with_memory_space_constraint(sends, pltpu.HBM), own)


def transposed(own, devices):
    count, size, width = own.shape
    chips, rows = devices // 2, width // devices
    if rows % 16:
        turned = own.reshape(count * size, width).T.reshape(chips, 2, rows, count * size)
        return turned.transpose(1, 0, 2, 3).reshape(width, count * size)

    def kernel(own_ref, out_ref):
        @pl.loop(0, count)
        def _(block):
            cols = pl.ds(pl.multiple_of(block * size, size), size)
            turned = own_ref[block].T
            for device in range(devices):
                chip, core = divmod(device, 2)
                out_ref[pl.ds((core * chips + chip) * rows, rows), cols] = (
                    turned[device * rows : (device + 1) * rows]
                )

    return pl.pallas_call(
        kernel,
        out_shape=jax.ShapeDtypeStruct((width, count * size), own.dtype),
        in_specs=[VMEM],
        out_specs=VMEM,
        compiler_params=PARAMETERS,
        cost_estimate=cost(0, 4 * own.size),
    )(own)


def steps(columns):
    step = 2 * LANES if columns % (2 * LANES) == 0 else columns
    return [pl.ds(at, step) for at in range(0, columns, step)]


def halo_place(column, count, halo):
    place = column - count
    upper = place >= halo
    odd = lax.rem(lax.axis_index(AXIS), 2)
    return upper == (odd == 1), jnp.where(upper, place - halo, place)


def fold_far(turned, blocks, columns, halo):
    params, count, slots, size, _ = blocks.shape
    width = turned.shape[0]

    def kernel(columns_ref, turned_ref, blocks_ref, out_ref, sum_ref):
        sum_ref[...] = jnp.zeros_like(sum_ref)

        @pl.loop(0, count)
        def _(row):
            rows = pl.ds(pl.multiple_of(row * size, size), size)
            for param in range(params):
                for slot in range(1, slots):
                    column = columns_ref[param, row, slot - 1]
                    far, place = halo_place(column, count, halo)

                    @pl.when((column >= count) & far)
                    def _():
                        at = pl.ds(pl.multiple_of(place * size, size), size)
                        sum_ref[param, :, at] += jnp.dot(
                            turned_ref[:, rows],
                            blocks_ref[param, row, slot],
                            preferred_element_type=jnp.float32,
                        )

        out_ref[...] = sum_ref[...].astype(out_ref.dtype)

    shape = (params, width, halo * size)
    return pl.pallas_call(
        kernel,
        out_shape=jax.ShapeDtypeStruct(shape, turned.dtype),
        in_specs=[SMEM, VMEM, VMEM],
        out_specs=VMEM,
        scratch_shapes=[pltpu.VMEM(shape, jnp.float32)],
        compiler_params=PARAMETERS,
        cost_estimate=cost(
            params * count * (slots - 1) * size * size * width, 2 * (turned.size + blocks.size)
        ),
    )(columns, turned, blocks)


def local_parts(turned, own, nears, blocks, columns):
    params, count, slots, size, _ = blocks.shape
    halo, width = nears[0].shape[0], own.shape[2]
    ranges = halves(width)

    def kernel(columns_ref, turned_ref, own_ref, blocks_ref, *refs):
        near_refs, (out_ref, list_ref, image_ref) = refs[: len(ranges)], refs[len(ranges) :]
        list_ref[pl.ds(0, count)] = own_ref[...]
        for part, near_ref in zip(ranges, near_refs):
            list_ref[pl.ds(count, halo), :, pl.ds(*part)] = near_ref[...]

        @pl.loop(0, count, unroll=4)
        def _(row):
            at = pl.ds(pl.multiple_of(row * size, size), size)
            for param in range(params):
                left, right = [blocks_ref[param, row, 0]], [list_ref[row]]
                for slot in range(1, slots):
                    block = blocks_ref[param, row, slot]
                    column = columns_ref[param, row, slot - 1]
                    far, place = halo_place(column, count, halo)
                    here = (column < count) | jnp.logical_not(far)
                    left.append(jnp.where(here, block, jnp.zeros_like(block)))
                    right.append(list_ref[jnp.where(column < count, column, count + place)])
                image = jnp.dot(
                    jnp.concatenate(left, axis=1),
                    jnp.concatenate(right, axis=0),
                    preferred_element_type=jnp.float32,
                )
                image_ref[at, pl.ds(param * width, width)] = image.astype(image_ref.dtype)

        for param in range(params):
            for cols in steps(width):
                out_ref[param, :, cols] = jnp.dot(
                    turned_ref[...],
                    image_ref[:, pl.ds(param * width + cols.start, cols.size)],
                    preferred_element_type=jnp.float32,
                )

    rows = count * size
    return pl.pallas_call(
        kernel,
        out_shape=jax.ShapeDtypeStruct((params, width, width), jnp.float32),
        in_specs=[SMEM] + [VMEM] * (3 + len(ranges)),
        out_specs=VMEM,
        scratch_shapes=[
            pltpu.VMEM((count + halo, size, width), own.dtype),
            pltpu.VMEM((rows, params * width), jnp.bfloat16),
        ],
        compiler_params=PARAMETERS,
        cost_estimate=cost(
            2 * params * rows * width * (slots * size + width),
            2 * (turned.size + 2 * own.size + blocks.size) + 4 * params * width * width,
        ),
    )(columns, turned, own, blocks, *nears)


def with_far(local, folds, far, part, mine):
    params, width, depth = folds.shape
    half = width // 2
    start, span = part

    def kernel(local_ref, folds_ref, far_ref, out_ref):
        odd = lax.rem(lax.axis_index(AXIS), 2)
        rows = pl.ds(pl.multiple_of((odd if mine else 1 - odd) * half, half), half)
        right = far_ref[...].reshape(depth, span)
        for param in range(params):
            total = local_ref[param, rows, pl.ds(start, span)] + jnp.dot(
                folds_ref[param, rows], right, preferred_element_type=jnp.float32
            )
            out_ref[:, pl.ds(param * span, span)] = total.astype(out_ref.dtype)

    return pl.pallas_call(
        kernel,
        out_shape=jax.ShapeDtypeStruct(
            (half, params * span), jnp.float32 if mine else jnp.bfloat16
        ),
        in_specs=[VMEM] * 3,
        out_specs=VMEM,
        compiler_params=PARAMETERS,
        cost_estimate=cost(
            2 * params * half * depth * span,
            4 * params * half * span + params * half * depth * 2 + 2 * depth * span,
        ),
    )(local, folds, far)


def add_chips(received, params, width):
    rows = received[0].shape[1]
    ranges = chunks(width)

    def kernel(*refs):
        out_ref = refs[-1]
        for (start, span), ref in zip(ranges, refs):
            total = jnp.sum(ref[...].astype(jnp.float32), axis=0)
            for param in range(params):
                out_ref[:, pl.ds(param * width + start, span)] = total[:, param * span : (param + 1) * span]

    return pl.pallas_call(
        kernel,
        out_shape=jax.ShapeDtypeStruct((rows, params * width), jnp.float32),
        in_specs=[VMEM] * len(received),
        out_specs=VMEM,
        compiler_params=PARAMETERS,
        cost_estimate=cost(0, sum(2 * part.size for part in received)),
    )(*received)


def shards(basis, blocks, columns, sends):
    params, count, _, size, _ = blocks.shape
    width = basis.shape[1]
    halo = sends.shape[1] // 2
    devices = lax.axis_size(AXIS)
    chips = devices // 2
    rows = width // devices
    ranges = chunks(width)
    near_pairs, far_pairs = pairs(devices, 0), pairs(devices, 1)

    own, first, *nears = pick_first(basis.reshape(count, size, width), sends, ranges[0])
    fars = [lax.ppermute(first, AXIS, far_pairs)]
    nears = [lax.ppermute(near, AXIS, near_pairs) for near in nears]
    for part in ranges[1:]:
        fars.append(lax.ppermute(pick_next(own, sends, part), AXIS, far_pairs))

    turned = transposed(own, devices)
    folds = fold_far(turned, blocks, columns, halo)
    local = local_parts(turned, own, nears, blocks, columns)

    groups = [list(range(core, devices, 2)) for core in range(2)]
    received, ready = [], None
    for part, far in zip(ranges, fars):
        if ready is not None:
            ready, far = lax.optimization_barrier((ready, far))
            received.append(exchange(ready, groups))
        give = with_far(local, folds, far, part, False)
        taken = lax.ppermute(give, AXIS, near_pairs)
        keep = with_far(local, folds, far, part, True)
        chip_sum = (keep + taken.astype(jnp.float32)).astype(jnp.bfloat16)
        ready = chip_sum.reshape(chips, rows, params * part[1])
    received.append(exchange(ready, groups))
    return add_chips(received, params, width)


def exchange(parts, groups):
    return lax.all_to_all(
        parts, AXIS, split_axis=0, concat_axis=0, axis_index_groups=groups, tiled=True
    )


def solution(mesh):
    placed = (
        P(("grp", "mesh"), None),
        P(None, ("grp", "mesh"), None, None, None),
        P(None, ("grp", "mesh"), None),
        P(("grp", "mesh"), None),
    )
    return jax.shard_map(
        shards, mesh=mesh, in_specs=placed, out_specs=P(("grp", "mesh"), None), check_vma=False
    )
```

profile of v0, /device:TPU:0, one launch (start us, length us, event | category | flops | bytes accessed | tf_op | source)
XLA Modules:
  0.0 55.1 jit_solution(13101352327716833275)
XLA Ops:
  0.0 0.0 copy-start.1
  0.0 3.1 %shard_map.46 = (bf16[16,128,512]{2,1,0:T(8,128)(2,1)S(1)}, bf16[8,128,512]{2,1,0:T(8,128)(2,1)}, bf16[8,128,256]{2,1,0:T(8,128)(2,1)}, bf16[8,128,256]{2,1,0:T(8,128)(2,1)}) custom-call(s32[1,16]{1,0:T(1,128)} %sends_hbm.1, bf16[16,128,512]{2,1,0:T(8,128)(2,1)} %bitcast.2), custom_call_target="tpu_custom_call" | custom-call | bytes 786432 | tf_op jit(solution)/shard_map/pallas_call | solution.py:65
  3.1 0.7 %collective-permute-start.2 = (bf16[8,128,512]{2,1,0:T(8,128)(2,1)}, bf16[8,128,512]{2,1,0:T(8,128)(2,1)S(1)}, u32[]{:S(2)}, u32[]{:S(2)}) collective-permute-start(bf16[8,128,512]{2,1,0:T(8,128)(2,1)} %get-tuple-element.12), channel_id=1, source_target_pairs={{1,2},{2,1},{3,4},{4,3},{5,6},{6,5},{7,8},{8,7},{9,10},{10,9},{11,... | collective-permute-start | bytes 3145736 | tf_op jit(solution)/shard_map/ppermute | solution.py:300
  3.9 4.3 %collective-permute-start = (bf16[8,128,256]{2,1,0:T(8,128)(2,1)}, bf16[8,128,256]{2,1,0:T(8,128)(2,1)}, u32[]{:S(2)}, u32[]{:S(2)}) collective-permute-start(bf16[8,128,256]{2,1,0:T(8,128)(2,1)} %get-tuple-element.10), channel_id=1, source_target_pairs={{0,1},{1,0},{2,3},{3,2},{4,5},{5,4},{6,7},{7,6},{8,9},{9,8},{10,11... | collective-permute-start | bytes 1572872 | tf_op jit(solution)/shard_map/ppermute | solution.py:301
  8.2 0.1 collective-permute-start.1
  8.2 0.0 copy-done.1
  8.2 0.1 copy.5.columns_ref
  8.3 0.0 copy-start
  8.3 1.5 %shard_map.47.turned_ref = bf16[512,2048]{1,0:T(8,128)(2,1)S(1)} custom-call(bf16[16,128,512]{2,1,0:T(8,128)(2,1)S(1)} %get-tuple-element.9.own_ref), custom_call_target="tpu_custom_call" | custom-call | bytes 524288 | tf_op jit(solution)/shard_map/pallas_call | solution.py:120
  9.8 0.4 copy-done
  10.2 3.7 %shard_map.49.folds_ref = bf16[2,512,1024]{2,1,0:T(8,128)(2,1)S(1)} custom-call(s32[2,16,2]{2,1,0:T(8,128)S(1)} %copy.5.columns_ref, bf16[512,2048]{1,0:T(8,128)(2,1)S(1)} %shard_map.47.turned_ref, bf16[2,16,3,128,128]{4,3,2,1,0:T(8,128)(2,1)S(1)} %copy-done), custom_call_target="tpu_custom_call" | custom-call | flops 67108864 | bytes 655360 | tf_op jit(solution)/shard_map/pallas_call | solution.py:169
  13.9 0.0 collective-permute-done.refs_0_
  13.9 0.0 collective-permute-done.1.refs_1_
  13.9 6.6 %shard_map.48.local_ref = f32[2,512,512]{2,1,0:T(8,128)S(1)} custom-call(s32[2,16,2]{2,1,0:T(8,128)S(1)} %copy.5.columns_ref, bf16[512,2048]{1,0:T(8,128)(2,1)S(1)} %shard_map.47.turned_ref, bf16[16,128,512]{2,1,0:T(8,128)(2,1)S(1)} %get-tuple-element.9.own_ref, bf16[2,16,3,128,128]{4,3,2,1,0:T(8,128)(2,1)S(1)} %copy-done, ...), custom_call_target="tpu_custom_call" | custom-call | flops 469762048 | bytes 1441792 | tf_op jit(solution)/shard_map/pallas_call | solution.py:221
  20.5 0.0 collective-permute-done.2.far_ref
  20.5 0.7 %shard_map.51 = bf16[256,1024]{1,0:T(8,128)(2,1)S(1)} custom-call(f32[2,512,512]{2,1,0:T(8,128)S(1)} %shard_map.48.local_ref, bf16[2,512,1024]{2,1,0:T(8,128)(2,1)S(1)} %shard_map.49.folds_ref, bf16[8,128,512]{2,1,0:T(8,128)(2,1)S(1)} %collective-permute-done.2.far_ref), custom_call_target="tpu_custom_call" | custom-call | flops 67108864 | bytes 393216 | tf_op jit(solution)/shard_map/pallas_call | solution.py:253
  21.2 10.9 %collective-permute-start.3 = (bf16[256,1024]{1,0:T(8,128)(2,1)S(1)}, bf16[256,1024]{1,0:T(8,128)(2,1)S(1)}, u32[]{:S(2)}, u32[]{:S(2)}) collective-permute-start(bf16[256,1024]{1,0:T(8,128)(2,1)S(1)} %shard_map.51), channel_id=1, source_target_pairs={{0,1},{1,0},{2,3},{3,2},{4,5},{5,4},{6,7},{7,6},{8,9},{9,8},{10,11... | collective-permute-start | bytes 1572872 | tf_op jit(solution)/shard_map/ppermute | solution.py:316
  32.1 0.7 %shard_map.50 = f32[256,1024]{1,0:T(8,128)S(1)} custom-call(f32[2,512,512]{2,1,0:T(8,128)S(1)} %shard_map.48.local_ref, bf16[2,512,1024]{2,1,0:T(8,128)(2,1)S(1)} %shard_map.49.folds_ref, bf16[8,128,512]{2,1,0:T(8,128)(2,1)S(1)} %collective-permute-done.2.far_ref), custom_call_target="tpu_custom_call" | custom-call | flops 67108864 | bytes 393216 | tf_op jit(solution)/shard_map/pallas_call | solution.py:253
  32.8 0.8 %collective-permute-done.3 = bf16[256,1024]{1,0:T(8,128)(2,1)S(1)} collective-permute-done((bf16[256,1024]{1,0:T(8,128)(2,1)S(1)}, bf16[256,1024]{1,0:T(8,128)(2,1)S(1)}, u32[]{:S(2)}, u32[]{:S(2)}) %collective-permute-start.3) | collective-permute-done | bytes 524320 | tf_op jit(solution)/shard_map/ppermute | solution.py:316
  33.7 0.1 add_convert_fusion
  33.8 20.5 %all_to_all.5.refs_0_ = bf16[8,32,1024]{2,1,0:T(8,128)(2,1)S(1)} all-to-all(bf16[8,32,1024]{2,1,0:T(8,128)(2,1)S(1)} %bitcast.3), channel_id=1, replica_groups={{0,2,4,6,8,10,12,14},{1,3,5,7,9,11,13,15},{16,18,20,22,24,26,28,30},{17..., dimensions={0} | all-to-all | bytes 1048576 | tf_op jit(solution)/shard_map/all_to_all | solution.py:325
  54.3 0.7 %shard_map.52 = f32[32,1024]{1,0:T(8,128)} custom-call(bf16[8,32,1024]{2,1,0:T(8,128)(2,1)S(1)} %all_to_all.5.refs_0_), custom_call_target="tpu_custom_call" | custom-call | bytes 65536 | tf_op jit(solution)/shard_map/pallas_call | solution.py:279
Async XLA Ops:
  0.0 8.2 %copy-start.1 = (s32[2,16,2]{1,2,0:T(2,128)S(1)}, s32[2,16,2]{1,2,0:T(2,128)}, u32[]{:S(2)}) copy-start(s32[2,16,2]{1,2,0:T(2,128)} %param.6) | copy-start | bytes 772
  3.1 17.4 %collective-permute-start.2 = (bf16[8,128,512]{2,1,0:T(8,128)(2,1)}, bf16[8,128,512]{2,1,0:T(8,128)(2,1)S(1)}, u32[]{:S(2)}, u32[]{:S(2)}) collective-permute-start(bf16[8,128,512]{2,1,0:T(8,128)(2,1)} %get-tuple-element.12), channel_id=1, source_target_pairs={{1,2},{2,1},{3,4},{4,3},{5,6},{6,5},{7,8},{8,7},{9,10},{10,9},{11,... | collective-permute-start | bytes 3145736 | tf_op jit(solution)/shard_map/ppermute | solution.py:300
  3.9 10.0 %collective-permute-start = (bf16[8,128,256]{2,1,0:T(8,128)(2,1)}, bf16[8,128,256]{2,1,0:T(8,128)(2,1)}, u32[]{:S(2)}, u32[]{:S(2)}) collective-permute-start(bf16[8,128,256]{2,1,0:T(8,128)(2,1)} %get-tuple-element.10), channel_id=1, source_target_pairs={{0,1},{1,0},{2,3},{3,2},{4,5},{5,4},{6,7},{7,6},{8,9},{9,8},{10,11... | collective-permute-start | bytes 1572872 | tf_op jit(solution)/shard_map/ppermute | solution.py:301
  8.2 5.7 %collective-permute-start.1 = (bf16[8,128,256]{2,1,0:T(8,128)(2,1)}, bf16[8,128,256]{2,1,0:T(8,128)(2,1)}, u32[]{:S(2)}, u32[]{:S(2)}) collective-permute-start(bf16[8,128,256]{2,1,0:T(8,128)(2,1)} %get-tuple-element.11), channel_id=1, source_target_pairs={{0,1},{1,0},{2,3},{3,2},{4,5},{5,4},{6,7},{7,6},{8,9},{9,8},{10,11... | collective-permute-start | bytes 1572872 | tf_op jit(solution)/shard_map/ppermute | solution.py:301
  8.3 1.9 %copy-start = (bf16[2,16,3,128,128]{4,3,2,1,0:T(8,128)(2,1)S(1)}, bf16[2,16,3,128,128]{4,3,2,1,0:T(8,128)(2,1)}, u32[]{:S(2)}) copy-start(bf16[2,16,3,128,128]{4,3,2,1,0:T(8,128)(2,1)} %blocks_ref.3) | copy-start | bytes 9437188
  21.2 12.4 %collective-permute-start.3 = (bf16[256,1024]{1,0:T(8,128)(2,1)S(1)}, bf16[256,1024]{1,0:T(8,128)(2,1)S(1)}, u32[]{:S(2)}, u32[]{:S(2)}) collective-permute-start(bf16[256,1024]{1,0:T(8,128)(2,1)S(1)} %shard_map.51), channel_id=1, source_target_pairs={{0,1},{1,0},{2,3},{3,2},{4,5},{5,4},{6,7},{7,6},{8,9},{9,8},{10,11... | collective-permute-start | bytes 1572872 | tf_op jit(solution)/shard_map/ppermute | solution.py:316
where the time goes:
time: 55.3 us; the launch traced here: 55.1 us
  blocking collectives  20.5 us (37%)
  Pallas kernels  17 us (31%)
  starting transfers between devices  16 us (29%)
  waiting for transfers between devices  0.83 us (2%)
    all_to_all x1, blocking collectives, exchange(): lax.all_to_all(parts, AXIS, split_axis=0, concat_axis=0, axis_index_group...  20.5 us
    ppermute x1, starting transfers between devices, shards(): taken = lax.ppermute(give, AXIS, near_pairs)  10.9 us
    pallas_call x1, Pallas kernels, local_parts(): pl.pallas_call(kernel, out_shape=jax.ShapeDtypeStruct((params, width, wid...  6.61 us
    ppermute x2, starting transfers between devices, shards(): nears = [lax.ppermute(near, AXIS, near_pairs) for near in nears]  4.38 us
    pallas_call x1, Pallas kernels, fold_far(): pl.pallas_call(kernel, out_shape=jax.ShapeDtypeStruct(shape, turned.dtype...  3.66 us
    pallas_call x1, Pallas kernels, pick_first(): pl.pallas_call(kernel, out_shape=[jax.ShapeDtypeStruct(own.shape, own.dty...  3.11 us
    pallas_call x1, Pallas kernels, transposed(): pl.pallas_call(kernel, out_shape=jax.ShapeDtypeStruct((width, count * siz...  1.48 us
    pallas_call x2, Pallas kernels, with_far(): pl.pallas_call(kernel, out_shape=jax.ShapeDtypeStruct((half, params * spa...  1.41 us
  transfers between devices with their start and end apart: 4, of which 1 were waited for; matrix products, arithmetic and copies ran while one was open for 0% of the time, Pallas kernels for 23%

commit v1 on v0

--- a/solution.py
+++ b/solution.py
@@ -25,77 +25,74 @@
     return both
 
 
-def chunks(width):
-    first = width
-    if first == width or first % LANES:
-        return [(0, width)]
-    return [(0, first), (first, width - first)]
-
-
 def halves(width):
     half = width // 2
     return [(0, width)] if half % LANES else [(0, half), (half, half)]
 
 
-def copy_listed(own_ref, sends_ref, far, part, out_ref):
-    halo = out_ref.shape[0]
-    odd = lax.rem(lax.axis_index(AXIS), 2)
-    first = (odd if far else 1 - odd) * halo
-    for place in range(halo):
-        out_ref[place] = own_ref[sends_ref[0, first + place], :, pl.ds(*part)]
-
-
-def pick_first(own, sends, part):
+def pick_far(own, sends):
     count, size, width = own.shape
     halo = sends.shape[1] // 2
-    ranges = halves(width)
-
-    def kernel(sends_hbm, own_hbm, own_ref, far_ref, *refs):
-        near_refs, (sends_ref, sems) = refs[: len(ranges)], refs[len(ranges) :]
-        lists = pltpu.make_async_copy(sends_hbm, sends_ref, sems.at[0])
-        load = pltpu.make_async_copy(own_hbm, own_ref, sems.at[1])
+
+    def kernel(sends_hbm, own_hbm, own_ref, far_ref, sends_ref, list_sem, sems):
+        lists = pltpu.make_async_copy(sends_hbm, sends_ref, list_sem)
         lists.start()
-        load.start()
+        loads = [
+            pltpu.make_async_copy(own_hbm.at[block], own_ref.at[block], sems.at[block])
+            for block in range(count)
+        ]
+        for load in loads:
+            load.start()
         lists.wait()
-        load.wait()
-        copy_listed(own_ref, sends_ref, True, part, far_ref)
-        for near_part, near_ref in zip(ranges, near_refs):
-            copy_listed(own_ref, sends_ref, False, near_part, near_ref)
-
-    return pl.pallas_call(
-        kernel,
-        out_shape=[
+        for load in loads:
+            load.wait()
+        first = lax.rem(lax.axis_index(AXIS), 2) * halo
+        for place in range(halo):
+            far_ref[place] = own_ref[sends_ref[0, first + place]]
+
+    return pl.pallas_call(
+        kernel,
+        out_shape=(
             jax.ShapeDtypeStruct(own.shape, own.dtype),
-            jax.ShapeDtypeStruct((halo, size, part[1]), own.dtype),
-        ]
-        + [jax.ShapeDtypeStruct((halo, size, span), own.dtype) for _, span in ranges],
+            jax.ShapeDtypeStruct((halo, size, width), own.dtype),
+        ),
         in_specs=[pl.BlockSpec(memory_space=pltpu.HBM)] * 2,
-        out_specs=[VMEM] * (2 + len(ranges)),
-        scratch_shapes=[pltpu.SMEM(sends.shape, sends.dtype), pltpu.SemaphoreType.DMA((2,))],
-        compiler_params=PARAMETERS,
-        cost_estimate=cost(0, 6 * own.size),
+        out_specs=(VMEM,) * 2,
+        scratch_shapes=[
+            pltpu.SMEM(sends.shape, sends.dtype),
+            pltpu.SemaphoreType.DMA(()),
+            pltpu.SemaphoreType.DMA((count,)),
+        ],
+        compiler_params=PARAMETERS,
+        cost_estimate=cost(0, 5 * own.size),
     )(
         pltpu.with_memory_space_constraint(sends, pltpu.HBM),
         pltpu.with_memory_space_constraint(own, pltpu.HBM),
     )
 
 
-def pick_next(own, sends, part):
-    _, size, _ = own.shape
+def pick_near(own, sends):
+    _, size, width = own.shape
     halo = sends.shape[1] // 2
-
-    def kernel(sends_hbm, own_ref, far_ref, sends_ref):
+    ranges = halves(width)
+
+    def kernel(sends_hbm, own_ref, *refs):
+        near_refs, sends_ref = refs[:-1], refs[-1]
         pltpu.sync_copy(sends_hbm, sends_ref)
-        copy_listed(own_ref, sends_ref, True, part, far_ref)
-
-    return pl.pallas_call(
-        kernel,
-        out_shape=jax.ShapeDtypeStruct((halo, size, part[1]), own.dtype),
+        first = (1 - lax.rem(lax.axis_index(AXIS), 2)) * halo
+        for place in range(halo):
+            block = sends_ref[0, first + place]
+            for part, near_ref in zip(ranges, near_refs):
+                near_ref[place] = own_ref[block, :, pl.ds(*part)]
+
+    return pl.pallas_call(
+        kernel,
+        out_shape=[jax.ShapeDtypeStruct((halo, size, span), own.dtype) for _, span in ranges],
         in_specs=[pl.BlockSpec(memory_space=pltpu.HBM), VMEM],
-        out_specs=VMEM,
+        out_specs=[VMEM] * len(ranges),
         scratch_shapes=[pltpu.SMEM(sends.shape, sends.dtype)],
         compiler_params=PARAMETERS,
-        cost_estimate=cost(0, 4 * halo * size * part[1]),
+        cost_estimate=cost(0, 2 * own.size),
     )(pltpu.with_memory_space_constraint(sends, pltpu.HBM), own)
 
 
@@ -235,55 +232,46 @@
     )(columns, turned, own, blocks, *nears)
 
 
-def with_far(local, folds, far, part, mine):
-    params, width, depth = folds.shape
-    half = width // 2
-    start, span = part
+def with_far(local, folds, far, mine, chosen):
+    _, width, depth = folds.shape
+    half, span = width // 2, far.shape[2]
 
     def kernel(local_ref, folds_ref, far_ref, out_ref):
         odd = lax.rem(lax.axis_index(AXIS), 2)
         rows = pl.ds(pl.multiple_of((odd if mine else 1 - odd) * half, half), half)
         right = far_ref[...].reshape(depth, span)
-        for param in range(params):
-            total = local_ref[param, rows, pl.ds(start, span)] + jnp.dot(
+        for place, param in enumerate(chosen):
+            total = local_ref[param, rows] + jnp.dot(
                 folds_ref[param, rows], right, preferred_element_type=jnp.float32
             )
-            out_ref[:, pl.ds(param * span, span)] = total.astype(out_ref.dtype)
-
-    return pl.pallas_call(
-        kernel,
-        out_shape=jax.ShapeDtypeStruct(
-            (half, params * span), jnp.float32 if mine else jnp.bfloat16
-        ),
+            out_ref[:, pl.ds(place * span, span)] = total.astype(out_ref.dtype)
+
+    columns = len(chosen) * span
+    return pl.pallas_call(
+        kernel,
+        out_shape=jax.ShapeDtypeStruct((half, columns), jnp.float32 if mine else jnp.bfloat16),
         in_specs=[VMEM] * 3,
         out_specs=VMEM,
         compiler_params=PARAMETERS,
         cost_estimate=cost(
-            2 * params * half * depth * span,
-            4 * params * half * span + params * half * depth * 2 + 2 * depth * span,
+            2 * half * depth * columns,
+            4 * half * columns + len(chosen) * half * depth * 2 + 2 * depth * span,
         ),
     )(local, folds, far)
 
 
-def add_chips(received, params, width):
-    rows = received[0].shape[1]
-    ranges = chunks(width)
-
-    def kernel(*refs):
-        out_ref = refs[-1]
-        for (start, span), ref in zip(ranges, refs):
-            total = jnp.sum(ref[...].astype(jnp.float32), axis=0)
-            for param in range(params):
-                out_ref[:, pl.ds(param * width + start, span)] = total[:, param * span : (param + 1) * span]
-
-    return pl.pallas_call(
-        kernel,
-        out_shape=jax.ShapeDtypeStruct((rows, params * width), jnp.float32),
-        in_specs=[VMEM] * len(received),
-        out_specs=VMEM,
-        compiler_params=PARAMETERS,
-        cost_estimate=cost(0, sum(2 * part.size for part in received)),
-    )(*received)
+def add_chips(parts):
+    def kernel(parts_ref, out_ref):
+        out_ref[...] = jnp.sum(parts_ref[...].astype(jnp.float32), axis=0)
+
+    return pl.pallas_call(
+        kernel,
+        out_shape=jax.ShapeDtypeStruct(parts.shape[1:], jnp.float32),
+        in_specs=[VMEM],
+        out_specs=VMEM,
+        compiler_params=PARAMETERS,
+        cost_estimate=cost(0, 2 * parts.size),
+    )(parts)
 
 
 def shards(basis, blocks, columns, sends):
@@ -292,39 +280,26 @@
     halo = sends.shape[1] // 2
     devices = lax.axis_size(AXIS)
     chips = devices // 2
-    rows = width // devices
-    ranges = chunks(width)
     near_pairs, far_pairs = pairs(devices, 0), pairs(devices, 1)
 
-    own, first, *nears = pick_first(basis.reshape(count, size, width), sends, ranges[0])
-    fars = [lax.ppermute(first, AXIS, far_pairs)]
-    nears = [lax.ppermute(near, AXIS, near_pairs) for near in nears]
-    for part in ranges[1:]:
-        fars.append(lax.ppermute(pick_next(own, sends, part), AXIS, far_pairs))
+    own, far = pick_far(basis.reshape(count, size, width), sends)
+    far = lax.ppermute(far, AXIS, far_pairs)
+    nears = [lax.ppermute(near, AXIS, near_pairs) for near in pick_near(own, sends)]
 
     turned = transposed(own, devices)
     folds = fold_far(turned, blocks, columns, halo)
     local = local_parts(turned, own, nears, blocks, columns)
 
-    groups = [list(range(core, devices, 2)) for core in range(2)]
-    received, ready = [], None
-    for part, far in zip(ranges, fars):
-        if ready is not None:
-            ready, far = lax.optimization_barrier((ready, far))
-            received.append(exchange(ready, groups))
-        give = with_far(local, folds, far, part, False)
-        taken = lax.ppermute(give, AXIS, near_pairs)
-        keep = with_far(local, folds, far, part, True)
-        chip_sum = (keep + taken.astype(jnp.float32)).astype(jnp.bfloat16)
-        ready = chip_sum.reshape(chips, rows, params * part[1])
-    received.append(exchange(ready, groups))
-    return add_chips(received, params, width)
-
-
-def exchange(parts, groups):
-    return lax.all_to_all(
-        parts, AXIS, split_axis=0, concat_axis=0, axis_index_groups=groups, tiled=True
+    gives = [with_far(local, folds, far, False, [param]) for param in range(params)]
+    taken = [lax.ppermute(give, AXIS, near_pairs) for give in gives]
+    keep = with_far(local, folds, far, True, list(range(params)))
+    chip_sum = (keep + jnp.concatenate(taken, axis=1).astype(jnp.float32)).astype(jnp.bfloat16)
+    parts = lax.all_to_all(
+        chip_sum.reshape(chips, width // devices, params * width), AXIS,
+        split_axis=0, concat_axis=0, tiled=True,
+        axis_index_groups=[list(range(core, devices, 2)) for core in range(2)],
     )
+    return add_chips(parts)
 
 
 def solution(mesh):

time: 55.3 us -> 55.2 us (level)
  starting transfers between devices: 16 us -> 11.4 us
  Pallas kernels: 17 us -> 19.9 us
  local copies, waits for them, and re-layouts: 0.49 us -> 1.99 us
    ppermute x4 -> x5, starting transfers between devices: 16 us -> 11.4 us  [the longest x2 6.48 us: shards(): taken = [lax.ppermute(give, AXIS, near_pairs) for give in gives]]
    pallas_call x4 -> x6, Pallas kernels: 5.24 us -> 6.8 us  [the longest x1 2.8 us: pick_far(): pl.pallas_call(kernel, out_shape=(jax.ShapeDtypeStruct(own.shape, own.dty...]
    unnamed x5 -> x11, local copies, waits for them, and re-layouts: 0.49 us -> 1.99 us
    pallas_call x1, Pallas kernels: 3.66 us -> 5.05 us  [fold_far(): pl.pallas_call(kernel, out_shape=jax.ShapeDtypeStruct(shape, turned.dtype...]
  transfers between devices with their start and end apart: 4 -> 5, of which waited for: 1 -> 1; matrix products, arithmetic and copies ran while one was open for 0% -> 0% of each run, Pallas kernels for 23% -> 29%
where the time goes in v1:
time: 55.2 us; the launch traced here: 55 us
  blocking collectives  20.5 us (37%)
  Pallas kernels  19.9 us (36%)
  starting transfers between devices  11.4 us (21%)
  local copies, waits for them, and re-layouts  1.99 us (4%)
  waiting for transfers between devices  0.81 us (1%)
    all_to_all x1, blocking collectives, shards(): lax.all_to_all(chip_sum.reshape(chips, width // devices, params * width),...  20.5 us
    pallas_call x1, Pallas kernels, local_parts(): pl.pallas_call(kernel, out_shape=jax.ShapeDtypeStruct((params, width, wid...  6.61 us
    ppermute x2, starting transfers between devices, shards(): taken = [lax.ppermute(give, AXIS, near_pairs) for give in gives]  6.48 us
    pallas_call x1, Pallas kernels, fold_far(): pl.pallas_call(kernel, out_shape=jax.ShapeDtypeStruct(shape, turned.dtype...  5.05 us
    ppermute x2, starting transfers between devices, shards(): lax.ppermute(near, AXIS, near_pairs)  4.24 us
    pallas_call x1, Pallas kernels, pick_far(): pl.pallas_call(kernel, out_shape=(jax.ShapeDtypeStruct(own.shape, own.dty...  2.8 us
    unnamed x11, local copies, waits for them, and re-layouts  1.99 us
    pallas_call x1, Pallas kernels, pick_near(): pl.pallas_call(kernel, out_shape=[jax.ShapeDtypeStruct((halo, size, span)...  1.72 us
  transfers between devices with their start and end apart: 5, of which 1 were waited for; matrix products, arithmetic and copies ran while one was open for 0% of the time, Pallas kernels for 29%

profile of v1, /device:TPU:0, one launch (start us, length us, event | category | flops | bytes accessed | tf_op | source)
XLA Modules:
  0.0 55.0 jit_solution(14427067238924826730)
XLA Ops:
  0.0 2.8 %shard_map.46 = (bf16[16,128,512]{2,1,0:T(8,128)(2,1)S(1)}, bf16[8,128,512]{2,1,0:T(8,128)(2,1)}) custom-call(s32[1,16]{1,0:T(1,128)} %sends_hbm.3, bf16[16,128,512]{2,1,0:T(8,128)(2,1)} %bitcast.2), custom_call_target="tpu_custom_call" | custom-call | bytes 655360 | tf_op jit(solution)/shard_map/pallas_call | solution.py:53
  2.8 0.0 copy-start
  2.8 0.7 %collective-permute-start.2 = (bf16[8,128,512]{2,1,0:T(8,128)(2,1)}, bf16[8,128,512]{2,1,0:T(8,128)(2,1)S(1)}, u32[]{:S(2)}, u32[]{:S(2)}) collective-permute-start(bf16[8,128,512]{2,1,0:T(8,128)(2,1)} %get-tuple-element.12), channel_id=1, source_target_pairs={{1,2},{2,1},{3,4},{4,3},{5,6},{6,5},{7,8},{8,7},{9,10},{10,9},{11,... | collective-permute-start | bytes 3145736 | tf_op jit(solution)/shard_map/ppermute | solution.py:286
  3.6 1.7 %shard_map.48 = (bf16[8,128,256]{2,1,0:T(8,128)(2,1)}, bf16[8,128,256]{2,1,0:T(8,128)(2,1)}) custom-call(s32[1,16]{1,0:T(1,128)} %sends_hbm.3, bf16[16,128,512]{2,1,0:T(8,128)(2,1)S(1)} %get-tuple-element.9.own_ref), custom_call_target="tpu_custom_call" | custom-call | bytes 262144 | tf_op jit(solution)/shard_map/pallas_call | solution.py:88
  5.3 4.2 %collective-permute-start = (bf16[8,128,256]{2,1,0:T(8,128)(2,1)}, bf16[8,128,256]{2,1,0:T(8,128)(2,1)}, u32[]{:S(2)}, u32[]{:S(2)}) collective-permute-start(bf16[8,128,256]{2,1,0:T(8,128)(2,1)} %get-tuple-element.10), channel_id=1, source_target_pairs={{0,1},{1,0},{2,3},{3,2},{4,5},{5,4},{6,7},{7,6},{8,9},{9,8},{10,11... | collective-permute-start | bytes 1572872 | tf_op jit(solution)/shard_map/ppermute | solution.py:287
  9.5 0.0 copy-start.4
  9.5 0.0 collective-permute-start.1
  9.5 0.0 copy-done
  9.5 1.5 %shard_map.47.turned_ref = bf16[512,2048]{1,0:T(8,128)(2,1)S(1)} custom-call(bf16[16,128,512]{2,1,0:T(8,128)(2,1)S(1)} %get-tuple-element.9.own_ref), custom_call_target="tpu_custom_call" | custom-call | bytes 524288 | tf_op jit(solution)/shard_map/pallas_call | solution.py:117
  11.0 0.0 copy-done.4
  11.0 0.1 copy.5.columns_ref
  11.1 0.0 copy-start.2
  11.1 1.9 %copy-done.2 = bf16[2,16,3,128,128]{4,3,2,1,0:T(8,128)(2,1)S(1)} copy-done((bf16[2,16,3,128,128]{4,3,2,1,0:T(8,128)(2,1)S(1)}, bf16[2,16,3,128,128]{4,3,2,1,0:T(8,128)(2,1)}, u32[]{:S(2)}) %copy-start.2) | copy-done | bytes 3145752
  13.0 0.0 copy-start.1
  13.0 0.0 copy-start.3
  13.0 5.0 %shard_map.50.folds_ref = bf16[2,512,1024]{2,1,0:T(8,128)(2,1)S(1)} custom-call(s32[2,16,2]{2,1,0:T(8,128)S(1)} %copy.5.columns_ref, bf16[512,2048]{1,0:T(8,128)(2,1)S(1)} %shard_map.47.turned_ref, bf16[2,16,3,128,128]{4,3,2,1,0:T(8,128)(2,1)S(1)} %copy-done.2), custom_call_target="tpu_custom_call" | custom-call | flops 67108864 | bytes 655360 | tf_op jit(solution)/shard_map/pallas_call | solution.py:166
  18.1 0.0 collective-permute-done.refs_0_
  18.1 0.0 collective-permute-done.1.refs_1_
  18.1 0.0 copy-done.1
  18.1 0.0 copy-done.3
  18.1 6.6 %shard_map.49.local_ref = f32[2,512,512]{2,1,0:T(8,128)S(1)} custom-call(s32[2,16,2]{2,1,0:T(8,128)S(1)} %copy.5.columns_ref, bf16[512,2048]{1,0:T(8,128)(2,1)S(1)} %shard_map.47.turned_ref, bf16[16,128,512]{2,1,0:T(8,128)(2,1)S(1)} %copy-done.1, bf16[2,16,3,128,128]{4,3,2,1,0:T(8,128)(2,1)S(1)} %copy-done.3, ...), custom_call_target="tpu_custom_call" | custom-call | flops 469762048 | bytes 1441792 | tf_op jit(solution)/shard_map/pallas_call | solution.py:218
  24.7 0.0 collective-permute-done.2.far_ref
  24.7 0.4 shard_map.52
  25.2 6.4 %collective-permute-start.3 = (bf16[256,512]{1,0:T(8,128)(2,1)S(1)}, bf16[256,512]{1,0:T(8,128)(2,1)S(1)}, u32[]{:S(2)}, u32[]{:S(2)}) collective-permute-start(bf16[256,512]{1,0:T(8,128)(2,1)S(1)} %shard_map.52), channel_id=1, source_target_pairs={{0,1},{1,0},{2,3},{3,2},{4,5},{5,4},{6,7},{7,6},{8,9},{9,8},{10,11... | collective-permute-start | bytes 786440 | tf_op jit(solution)/shard_map/ppermute | solution.py:294
  31.6 0.4 shard_map.53
  32.0 0.1 collective-permute-start.4
  32.1 0.7 %shard_map.51 = f32[256,1024]{1,0:T(8,128)S(1)} custom-call(f32[2,512,512]{2,1,0:T(8,128)S(1)} %shard_map.49.local_ref, bf16[2,512,1024]{2,1,0:T(8,128)(2,1)S(1)} %shard_map.50.folds_ref, bf16[8,128,512]{2,1,0:T(8,128)(2,1)S(1)} %collective-permute-done.2.far_ref), custom_call_target="tpu_custom_call" | custom-call | flops 67108864 | bytes 393216 | tf_op jit(solution)/shard_map/pallas_call | solution.py:250
  32.8 0.0 collective-permute-done.3
  32.8 0.8 %collective-permute-done.4 = bf16[256,512]{1,0:T(8,128)(2,1)S(1)} collective-permute-done((bf16[256,512]{1,0:T(8,128)(2,1)S(1)}, bf16[256,512]{1,0:T(8,128)(2,1)S(1)}, u32[]{:S(2)}, u32[]{:S(2)}) %collective-permute-start.4) | collective-permute-done | bytes 262176 | tf_op jit(solution)/shard_map/ppermute | solution.py:294
  33.6 0.1 add_convert_fusion
  33.7 20.5 %all_to_all.5.parts_ref = bf16[8,32,1024]{2,1,0:T(8,128)(2,1)S(1)} all-to-all(bf16[8,32,1024]{2,1,0:T(8,128)(2,1)S(1)} %bitcast.3), channel_id=1, replica_groups={{0,2,4,6,8,10,12,14},{1,3,5,7,9,11,13,15},{16,18,20,22,24,26,28,30},{17..., dimensions={0} | all-to-all | bytes 1048576 | tf_op jit(solution)/shard_map/all_to_all | solution.py:297
  54.3 0.7 %shard_map.54 = f32[32,1024]{1,0:T(8,128)} custom-call(bf16[8,32,1024]{2,1,0:T(8,128)(2,1)S(1)} %all_to_all.5.parts_ref), custom_call_target="tpu_custom_call" | custom-call | bytes 65536 | tf_op jit(solution)/shard_map/pallas_call | solution.py:267
Async XLA Ops:
  2.8 6.7 %copy-start = (bf16[16,128,512]{2,1,0:T(8,128)(2,1)}, bf16[16,128,512]{2,1,0:T(8,128)(2,1)S(1)}, u32[]{:S(2)}) copy-start(bf16[16,128,512]{2,1,0:T(8,128)(2,1)S(1)} %get-tuple-element.9.own_ref) | copy-start | bytes 6291460
  2.8 21.9 %collective-permute-start.2 = (bf16[8,128,512]{2,1,0:T(8,128)(2,1)}, bf16[8,128,512]{2,1,0:T(8,128)(2,1)S(1)}, u32[]{:S(2)}, u32[]{:S(2)}) collective-permute-start(bf16[8,128,512]{2,1,0:T(8,128)(2,1)} %get-tuple-element.12), channel_id=1, source_target_pairs={{1,2},{2,1},{3,4},{4,3},{5,6},{6,5},{7,8},{8,7},{9,10},{10,9},{11,... | collective-permute-start | bytes 3145736 | tf_op jit(solution)/shard_map/ppermute | solution.py:286
  5.3 12.8 %collective-permute-start = (bf16[8,128,256]{2,1,0:T(8,128)(2,1)}, bf16[8,128,256]{2,1,0:T(8,128)(2,1)}, u32[]{:S(2)}, u32[]{:S(2)}) collective-permute-start(bf16[8,128,256]{2,1,0:T(8,128)(2,1)} %get-tuple-element.10), channel_id=1, source_target_pairs={{0,1},{1,0},{2,3},{3,2},{4,5},{5,4},{6,7},{7,6},{8,9},{9,8},{10,11... | collective-permute-start | bytes 1572872 | tf_op jit(solution)/shard_map/ppermute | solution.py:287
  9.5 1.5 %copy-start.4 = (s32[2,16,2]{1,2,0:T(2,128)S(1)}, s32[2,16,2]{1,2,0:T(2,128)}, u32[]{:S(2)}) copy-start(s32[2,16,2]{1,2,0:T(2,128)} %param.6) | copy-start | bytes 772
  9.5 8.6 %collective-permute-start.1 = (bf16[8,128,256]{2,1,0:T(8,128)(2,1)}, bf16[8,128,256]{2,1,0:T(8,128)(2,1)}, u32[]{:S(2)}, u32[]{:S(2)}) collective-permute-start(bf16[8,128,256]{2,1,0:T(8,128)(2,1)} %get-tuple-element.11), channel_id=1, source_target_pairs={{0,1},{1,0},{2,3},{3,2},{4,5},{5,4},{6,7},{7,6},{8,9},{9,8},{10,11... | collective-permute-start | bytes 1572872 | tf_op jit(solution)/shard_map/ppermute | solution.py:287
  11.1 1.9 %copy-start.2 = (bf16[2,16,3,128,128]{4,3,2,1,0:T(8,128)(2,1)S(1)}, bf16[2,16,3,128,128]{4,3,2,1,0:T(8,128)(2,1)}, u32[]{:S(2)}) copy-start(bf16[2,16,3,128,128]{4,3,2,1,0:T(8,128)(2,1)} %blocks_ref.3) | copy-start | bytes 9437188
  13.0 5.1 %copy-start.1 = (bf16[16,128,512]{2,1,0:T(8,128)(2,1)S(1)}, bf16[16,128,512]{2,1,0:T(8,128)(2,1)}, u32[]{:S(2)}) copy-start(bf16[16,128,512]{2,1,0:T(8,128)(2,1)} %copy-done) | copy-start | bytes 6291460
  13.0 5.1 %copy-start.3 = (bf16[2,16,3,128,128]{4,3,2,1,0:T(8,128)(2,1)S(1)}, bf16[2,16,3,128,128]{4,3,2,1,0:T(8,128)(2,1)}, u32[]{:S(2)}) copy-start(bf16[2,16,3,128,128]{4,3,2,1,0:T(8,128)(2,1)} %blocks_ref.3) | copy-start | bytes 9437188
  25.2 7.6 %collective-permute-start.3 = (bf16[256,512]{1,0:T(8,128)(2,1)S(1)}, bf16[256,512]{1,0:T(8,128)(2,1)S(1)}, u32[]{:S(2)}, u32[]{:S(2)}) collective-permute-start(bf16[256,512]{1,0:T(8,128)(2,1)S(1)} %shard_map.52), channel_id=1, source_target_pairs={{0,1},{1,0},{2,3},{3,2},{4,5},{5,4},{6,7},{7,6},{8,9},{9,8},{10,11... | collective-permute-start | bytes 786440 | tf_op jit(solution)/shard_map/ppermute | solution.py:294
  32.0 1.6 %collective-permute-start.4 = (bf16[256,512]{1,0:T(8,128)(2,1)S(1)}, bf16[256,512]{1,0:T(8,128)(2,1)S(1)}, u32[]{:S(2)}, u32[]{:S(2)}) collective-permute-start(bf16[256,512]{1,0:T(8,128)(2,1)S(1)} %shard_map.53), channel_id=1, source_target_pairs={{0,1},{1,0},{2,3},{3,2},{4,5},{5,4},{6,7},{7,6},{8,9},{9,8},{10,11... | collective-permute-start | bytes 786440 | tf_op jit(solution)/shard_map/ppermute | solution.py:294

commit v2 on v1

--- a/solution.py
+++ b/solution.py
@@ -23,6 +23,10 @@
     for low in range(first, count - 1, 2):
         both += [(low, low + 1), (low + 1, low)]
     return both
+
+
+def chip_order(chips):
+    return list(range(0, chips, 2)) + list(range(1, chips, 2))
 
 
 def halves(width):
@@ -99,8 +103,10 @@
 def transposed(own, devices):
     count, size, width = own.shape
     chips, rows = devices // 2, width // devices
+    order = chip_order(chips)
     if rows % 16:
         turned = own.reshape(count * size, width).T.reshape(chips, 2, rows, count * size)
+        turned = turned[jnp.array(order)]
         return turned.transpose(1, 0, 2, 3).reshape(width, count * size)
 
     def kernel(own_ref, out_ref):
@@ -110,7 +116,7 @@
             turned = own_ref[block].T
             for device in range(devices):
                 chip, core = divmod(device, 2)
-                out_ref[pl.ds((core * chips + chip) * rows, rows), cols] = (
+                out_ref[pl.ds((core * chips + order.index(chip)) * rows, rows), cols] = (
                     turned[device * rows : (device + 1) * rows]
                 )
 
@@ -232,21 +238,21 @@
     )(columns, turned, own, blocks, *nears)
 
 
-def with_far(local, folds, far, mine, chosen):
-    _, width, depth = folds.shape
+def with_far(local, folds, far, mine):
+    params, width, depth = folds.shape
     half, span = width // 2, far.shape[2]
 
     def kernel(local_ref, folds_ref, far_ref, out_ref):
         odd = lax.rem(lax.axis_index(AXIS), 2)
         rows = pl.ds(pl.multiple_of((odd if mine else 1 - odd) * half, half), half)
         right = far_ref[...].reshape(depth, span)
-        for place, param in enumerate(chosen):
+        for param in range(params):
             total = local_ref[param, rows] + jnp.dot(
                 folds_ref[param, rows], right, preferred_element_type=jnp.float32
             )
-            out_ref[:, pl.ds(place * span, span)] = total.astype(out_ref.dtype)
-
-    columns = len(chosen) * span
+            out_ref[:, pl.ds(param * span, span)] = total.astype(out_ref.dtype)
+
+    columns = params * span
     return pl.pallas_call(
         kernel,
         out_shape=jax.ShapeDtypeStruct((half, columns), jnp.float32 if mine else jnp.bfloat16),
@@ -255,7 +261,7 @@
         compiler_params=PARAMETERS,
         cost_estimate=cost(
             2 * half * depth * columns,
-            4 * half * columns + len(chosen) * half * depth * 2 + 2 * depth * span,
+            4 * half * columns + params * half * depth * 2 + 2 * depth * span,
         ),
     )(local, folds, far)
 
@@ -290,14 +296,13 @@
     folds = fold_far(turned, blocks, columns, halo)
     local = local_parts(turned, own, nears, blocks, columns)
 
-    gives = [with_far(local, folds, far, False, [param]) for param in range(params)]
-    taken = [lax.ppermute(give, AXIS, near_pairs) for give in gives]
-    keep = with_far(local, folds, far, True, list(range(params)))
-    chip_sum = (keep + jnp.concatenate(taken, axis=1).astype(jnp.float32)).astype(jnp.bfloat16)
+    taken = lax.ppermute(with_far(local, folds, far, False), AXIS, near_pairs)
+    keep = with_far(local, folds, far, True)
+    chip_sum = (keep + taken.astype(jnp.float32)).astype(jnp.bfloat16)
     parts = lax.all_to_all(
         chip_sum.reshape(chips, width // devices, params * width), AXIS,
         split_axis=0, concat_axis=0, tiled=True,
-        axis_index_groups=[list(range(core, devices, 2)) for core in range(2)],
+        axis_index_groups=[[2 * chip + core for chip in chip_order(chips)] for core in range(2)],
     )
     return add_chips(parts)
 

time: 55.2 us -> 55.9 us (1.013)
  blocking collectives: 20.5 us -> 21.4 us
    all_to_all x1, blocking collectives: 20.5 us -> 21.4 us  [shards(): lax.all_to_all(chip_sum.reshape(chips, width // devices, params * width),...]
    ppermute x2 -> x1, starting transfers between devices: 6.48 us -> 6.07 us  [shards(): taken = lax.ppermute(with_far(local, folds, far, False), AXIS, near_pairs)]
    pallas_call x3 -> x2, Pallas kernels: 1.57 us -> 1.41 us  [with_far(): pl.pallas_call(kernel, out_shape=jax.ShapeDtypeStruct((half, columns), jn...]
  transfers between devices with their start and end apart: 5 -> 4, of which waited for: 1 -> 1; matrix products, arithmetic and copies ran while one was open for 0% -> 0% of each run, Pallas kernels for 29% -> 29%
where the time goes in v2:
time: 55.9 us; the launch traced here: 55.7 us
  blocking collectives  21.4 us (38%)
  Pallas kernels  20.1 us (36%)
  starting transfers between devices  11 us (20%)
  local copies, waits for them, and re-layouts  1.99 us (4%)
  waiting for transfers between devices  0.83 us (1%)
    all_to_all x1, blocking collectives, shards(): lax.all_to_all(chip_sum.reshape(chips, width // devices, params * width),...  21.4 us
    pallas_call x1, Pallas kernels, local_parts(): pl.pallas_call(kernel, out_shape=jax.ShapeDtypeStruct((params, width, wid...  6.61 us
    ppermute x1, starting transfers between devices, shards(): taken = lax.ppermute(with_far(local, folds, far, False), AXIS, near_pairs)  6.07 us
    pallas_call x1, Pallas kernels, fold_far(): pl.pallas_call(kernel, out_shape=jax.ShapeDtypeStruct(shape, turned.dtype...  5.39 us
    ppermute x2, starting transfers between devices, shards(): lax.ppermute(near, AXIS, near_pairs)  4.24 us
    pallas_call x1, Pallas kernels, pick_far(): pl.pallas_call(kernel, out_shape=(jax.ShapeDtypeStruct(own.shape, own.dty...  2.8 us
    unnamed x11, local copies, waits for them, and re-layouts  1.99 us
    pallas_call x1, Pallas kernels, pick_near(): pl.pallas_call(kernel, out_shape=[jax.ShapeDtypeStruct((halo, size, span)...  1.71 us
  transfers between devices with their start and end apart: 4, of which 1 were waited for; matrix products, arithmetic and copies ran while one was open for 0% of the time, Pallas kernels for 29%

profile of v2, /device:TPU:0, one launch (start us, length us, event | category | flops | bytes accessed | tf_op | source)
XLA Modules:
  0.0 55.7 jit_solution(7025574982699568349)
XLA Ops:
  0.0 2.8 %shard_map.46 = (bf16[16,128,512]{2,1,0:T(8,128)(2,1)S(1)}, bf16[8,128,512]{2,1,0:T(8,128)(2,1)}) custom-call(s32[1,16]{1,0:T(1,128)} %sends_hbm.3, bf16[16,128,512]{2,1,0:T(8,128)(2,1)} %bitcast.2), custom_call_target="tpu_custom_call" | custom-call | bytes 655360 | tf_op jit(solution)/shard_map/pallas_call | solution.py:57
  2.8 0.0 copy-start
  2.8 0.7 %collective-permute-start.2 = (bf16[8,128,512]{2,1,0:T(8,128)(2,1)}, bf16[8,128,512]{2,1,0:T(8,128)(2,1)S(1)}, u32[]{:S(2)}, u32[]{:S(2)}) collective-permute-start(bf16[8,128,512]{2,1,0:T(8,128)(2,1)} %get-tuple-element.12), channel_id=1, source_target_pairs={{1,2},{2,1},{3,4},{4,3},{5,6},{6,5},{7,8},{8,7},{9,10},{10,9},{11,... | collective-permute-start | bytes 3145736 | tf_op jit(solution)/shard_map/ppermute | solution.py:292
  3.6 1.7 %shard_map.48 = (bf16[8,128,256]{2,1,0:T(8,128)(2,1)}, bf16[8,128,256]{2,1,0:T(8,128)(2,1)}) custom-call(s32[1,16]{1,0:T(1,128)} %sends_hbm.3, bf16[16,128,512]{2,1,0:T(8,128)(2,1)S(1)} %get-tuple-element.9.own_ref), custom_call_target="tpu_custom_call" | custom-call | bytes 262144 | tf_op jit(solution)/shard_map/pallas_call | solution.py:92
  5.3 4.2 %collective-permute-start = (bf16[8,128,256]{2,1,0:T(8,128)(2,1)}, bf16[8,128,256]{2,1,0:T(8,128)(2,1)}, u32[]{:S(2)}, u32[]{:S(2)}) collective-permute-start(bf16[8,128,256]{2,1,0:T(8,128)(2,1)} %get-tuple-element.10), channel_id=1, source_target_pairs={{0,1},{1,0},{2,3},{3,2},{4,5},{5,4},{6,7},{7,6},{8,9},{9,8},{10,11... | collective-permute-start | bytes 1572872 | tf_op jit(solution)/shard_map/ppermute | solution.py:293
  9.5 0.0 copy-start.4
  9.5 0.0 collective-permute-start.1
  9.5 0.0 copy-done
  9.5 1.5 %shard_map.47.turned_ref = bf16[512,2048]{1,0:T(8,128)(2,1)S(1)} custom-call(bf16[16,128,512]{2,1,0:T(8,128)(2,1)S(1)} %get-tuple-element.9.own_ref), custom_call_target="tpu_custom_call" | custom-call | bytes 524288 | tf_op jit(solution)/shard_map/pallas_call | solution.py:123
  11.0 0.0 copy-done.4
  11.0 0.1 copy.5.columns_ref
  11.1 0.0 copy-start.2
  11.1 1.9 %copy-done.2 = bf16[2,16,3,128,128]{4,3,2,1,0:T(8,128)(2,1)S(1)} copy-done((bf16[2,16,3,128,128]{4,3,2,1,0:T(8,128)(2,1)S(1)}, bf16[2,16,3,128,128]{4,3,2,1,0:T(8,128)(2,1)}, u32[]{:S(2)}) %copy-start.2) | copy-done | bytes 3145752
  13.0 0.0 copy-start.1
  13.0 0.0 copy-start.3
  13.0 5.4 %shard_map.50.folds_ref = bf16[2,512,1024]{2,1,0:T(8,128)(2,1)S(1)} custom-call(s32[2,16,2]{2,1,0:T(8,128)S(1)} %copy.5.columns_ref, bf16[512,2048]{1,0:T(8,128)(2,1)S(1)} %shard_map.47.turned_ref, bf16[2,16,3,128,128]{4,3,2,1,0:T(8,128)(2,1)S(1)} %copy-done.2), custom_call_target="tpu_custom_call" | custom-call | flops 67108864 | bytes 655360 | tf_op jit(solution)/shard_map/pallas_call | solution.py:172
  18.4 0.0 collective-permute-done.refs_0_
  18.4 0.0 collective-permute-done.1.refs_1_
  18.4 0.0 copy-done.1
  18.4 0.0 copy-done.3
  18.4 6.6 %shard_map.49.local_ref = f32[2,512,512]{2,1,0:T(8,128)S(1)} custom-call(s32[2,16,2]{2,1,0:T(8,128)S(1)} %copy.5.columns_ref, bf16[512,2048]{1,0:T(8,128)(2,1)S(1)} %shard_map.47.turned_ref, bf16[16,128,512]{2,1,0:T(8,128)(2,1)S(1)} %copy-done.1, bf16[2,16,3,128,128]{4,3,2,1,0:T(8,128)(2,1)S(1)} %copy-done.3, ...), custom_call_target="tpu_custom_call" | custom-call | flops 469762048 | bytes 1441792 | tf_op jit(solution)/shard_map/pallas_call | solution.py:224
  25.0 0.0 collective-permute-done.2.far_ref
  25.1 0.7 %shard_map.52 = bf16[256,1024]{1,0:T(8,128)(2,1)S(1)} custom-call(f32[2,512,512]{2,1,0:T(8,128)S(1)} %shard_map.49.local_ref, bf16[2,512,1024]{2,1,0:T(8,128)(2,1)S(1)} %shard_map.50.folds_ref, bf16[8,128,512]{2,1,0:T(8,128)(2,1)S(1)} %collective-permute-done.2.far_ref), custom_call_target="tpu_custom_call" | custom-call | flops 67108864 | bytes 393216 | tf_op jit(solution)/shard_map/pallas_call | solution.py:256
  25.8 6.1 %collective-permute-start.3 = (bf16[256,1024]{1,0:T(8,128)(2,1)S(1)}, bf16[256,1024]{1,0:T(8,128)(2,1)S(1)}, u32[]{:S(2)}, u32[]{:S(2)}) collective-permute-start(bf16[256,1024]{1,0:T(8,128)(2,1)S(1)} %shard_map.52), channel_id=1, source_target_pairs={{0,1},{1,0},{2,3},{3,2},{4,5},{5,4},{6,7},{7,6},{8,9},{9,8},{10,11... | collective-permute-start | bytes 1572872 | tf_op jit(solution)/shard_map/ppermute | solution.py:299
  31.8 0.7 %shard_map.51 = f32[256,1024]{1,0:T(8,128)S(1)} custom-call(f32[2,512,512]{2,1,0:T(8,128)S(1)} %shard_map.49.local_ref, bf16[2,512,1024]{2,1,0:T(8,128)(2,1)S(1)} %shard_map.50.folds_ref, bf16[8,128,512]{2,1,0:T(8,128)(2,1)S(1)} %collective-permute-done.2.far_ref), custom_call_target="tpu_custom_call" | custom-call | flops 67108864 | bytes 393216 | tf_op jit(solution)/shard_map/pallas_call | solution.py:256
  32.5 0.8 %collective-permute-done.3 = bf16[256,1024]{1,0:T(8,128)(2,1)S(1)} collective-permute-done((bf16[256,1024]{1,0:T(8,128)(2,1)S(1)}, bf16[256,1024]{1,0:T(8,128)(2,1)S(1)}, u32[]{:S(2)}, u32[]{:S(2)}) %collective-permute-start.3) | collective-permute-done | bytes 524320 | tf_op jit(solution)/shard_map/ppermute | solution.py:299
  33.4 0.1 add_convert_fusion
  33.5 21.4 %all_to_all.5.parts_ref = bf16[8,32,1024]{2,1,0:T(8,128)(2,1)S(1)} all-to-all(bf16[8,32,1024]{2,1,0:T(8,128)(2,1)S(1)} %bitcast.3), channel_id=1, replica_groups={{0,4,8,12,2,6,10,14},{1,5,9,13,3,7,11,15},{16,20,24,28,18,22,26,30},{17..., dimensions={0} | all-to-all | bytes 1048576 | tf_op jit(solution)/shard_map/all_to_all | solution.py:302
  54.9 0.7 %shard_map.53 = f32[32,1024]{1,0:T(8,128)} custom-call(bf16[8,32,1024]{2,1,0:T(8,128)(2,1)S(1)} %all_to_all.5.parts_ref), custom_call_target="tpu_custom_call" | custom-call | bytes 65536 | tf_op jit(solution)/shard_map/pallas_call | solution.py:273
Async XLA Ops:
  2.8 6.7 %copy-start = (bf16[16,128,512]{2,1,0:T(8,128)(2,1)}, bf16[16,128,512]{2,1,0:T(8,128)(2,1)S(1)}, u32[]{:S(2)}) copy-start(bf16[16,128,512]{2,1,0:T(8,128)(2,1)S(1)} %get-tuple-element.9.own_ref) | copy-start | bytes 6291460
  2.8 22.2 %collective-permute-start.2 = (bf16[8,128,512]{2,1,0:T(8,128)(2,1)}, bf16[8,128,512]{2,1,0:T(8,128)(2,1)S(1)}, u32[]{:S(2)}, u32[]{:S(2)}) collective-permute-start(bf16[8,128,512]{2,1,0:T(8,128)(2,1)} %get-tuple-element.12), channel_id=1, source_target_pairs={{1,2},{2,1},{3,4},{4,3},{5,6},{6,5},{7,8},{8,7},{9,10},{10,9},{11,... | collective-permute-start | bytes 3145736 | tf_op jit(solution)/shard_map/ppermute | solution.py:292
  5.3 13.1 %collective-permute-start = (bf16[8,128,256]{2,1,0:T(8,128)(2,1)}, bf16[8,128,256]{2,1,0:T(8,128)(2,1)}, u32[]{:S(2)}, u32[]{:S(2)}) collective-permute-start(bf16[8,128,256]{2,1,0:T(8,128)(2,1)} %get-tuple-element.10), channel_id=1, source_target_pairs={{0,1},{1,0},{2,3},{3,2},{4,5},{5,4},{6,7},{7,6},{8,9},{9,8},{10,11... | collective-permute-start | bytes 1572872 | tf_op jit(solution)/shard_map/ppermute | solution.py:293
  9.5 1.5 %copy-start.4 = (s32[2,16,2]{1,2,0:T(2,128)S(1)}, s32[2,16,2]{1,2,0:T(2,128)}, u32[]{:S(2)}) copy-start(s32[2,16,2]{1,2,0:T(2,128)} %param.6) | copy-start | bytes 772
  9.5 8.9 %collective-permute-start.1 = (bf16[8,128,256]{2,1,0:T(8,128)(2,1)}, bf16[8,128,256]{2,1,0:T(8,128)(2,1)}, u32[]{:S(2)}, u32[]{:S(2)}) collective-permute-start(bf16[8,128,256]{2,1,0:T(8,128)(2,1)} %get-tuple-element.11), channel_id=1, source_target_pairs={{0,1},{1,0},{2,3},{3,2},{4,5},{5,4},{6,7},{7,6},{8,9},{9,8},{10,11... | collective-permute-start | bytes 1572872 | tf_op jit(solution)/shard_map/ppermute | solution.py:293
  11.1 1.9 %copy-start.2 = (bf16[2,16,3,128,128]{4,3,2,1,0:T(8,128)(2,1)S(1)}, bf16[2,16,3,128,128]{4,3,2,1,0:T(8,128)(2,1)}, u32[]{:S(2)}) copy-start(bf16[2,16,3,128,128]{4,3,2,1,0:T(8,128)(2,1)} %blocks_ref.3) | copy-start | bytes 9437188
  13.0 5.4 %copy-start.1 = (bf16[16,128,512]{2,1,0:T(8,128)(2,1)S(1)}, bf16[16,128,512]{2,1,0:T(8,128)(2,1)}, u32[]{:S(2)}) copy-start(bf16[16,128,512]{2,1,0:T(8,128)(2,1)} %copy-done) | copy-start | bytes 6291460
  13.0 5.4 %copy-start.3 = (bf16[2,16,3,128,128]{4,3,2,1,0:T(8,128)(2,1)S(1)}, bf16[2,16,3,128,128]{4,3,2,1,0:T(8,128)(2,1)}, u32[]{:S(2)}) copy-start(bf16[2,16,3,128,128]{4,3,2,1,0:T(8,128)(2,1)} %blocks_ref.3) | copy-start | bytes 9437188
  25.8 7.6 %collective-permute-start.3 = (bf16[256,1024]{1,0:T(8,128)(2,1)S(1)}, bf16[256,1024]{1,0:T(8,128)(2,1)S(1)}, u32[]{:S(2)}, u32[]{:S(2)}) collective-permute-start(bf16[256,1024]{1,0:T(8,128)(2,1)S(1)} %shard_map.52), channel_id=1, source_target_pairs={{0,1},{1,0},{2,3},{3,2},{4,5},{5,4},{6,7},{7,6},{8,9},{9,8},{10,11... | collective-permute-start | bytes 1572872 | tf_op jit(solution)/shard_map/ppermute | solution.py:299

commit v3 on v2

--- a/solution.py
+++ b/solution.py
@@ -26,7 +26,7 @@
 
 
 def chip_order(chips):
-    return list(range(0, chips, 2)) + list(range(1, chips, 2))
+    return list(range(chips - 1, -1, -1))
 
 
 def halves(width):

time: 55.9 us -> 54.1 us (0.968)
  blocking collectives: 21.4 us -> 19.6 us
  starting transfers between devices: 11 us -> 12.6 us
  Pallas kernels: 20.1 us -> 18.6 us
    all_to_all x1, blocking collectives: 21.4 us -> 19.6 us  [shards(): lax.all_to_all(chip_sum.reshape(chips, width // devices, params * width),...]
    ppermute x1, starting transfers between devices: 6.07 us -> 7.63 us  [shards(): taken = lax.ppermute(with_far(local, folds, far, False), AXIS, near_pairs)]
    pallas_call x1, Pallas kernels: 5.39 us -> 3.83 us  [fold_far(): pl.pallas_call(kernel, out_shape=jax.ShapeDtypeStruct(shape, turned.dtype...]
  transfers between devices with their start and end apart: 4 -> 4, of which waited for: 1 -> 1; matrix products, arithmetic and copies ran while one was open for 0% -> 0% of each run, Pallas kernels for 29% -> 27%
where the time goes in v3:
time: 54.1 us; the launch traced here: 53.9 us
  blocking collectives  19.6 us (36%)
  Pallas kernels  18.6 us (34%)
  starting transfers between devices  12.6 us (23%)
  local copies, waits for them, and re-layouts  1.99 us (4%)
  waiting for transfers between devices  0.83 us (2%)
    all_to_all x1, blocking collectives, shards(): lax.all_to_all(chip_sum.reshape(chips, width // devices, params * width),...  19.6 us
    ppermute x1, starting transfers between devices, shards(): taken = lax.ppermute(with_far(local, folds, far, False), AXIS, near_pairs)  7.63 us
    pallas_call x1, Pallas kernels, local_parts(): pl.pallas_call(kernel, out_shape=jax.ShapeDtypeStruct((params, width, wid...  6.61 us
    ppermute x2, starting transfers between devices, shards(): lax.ppermute(near, AXIS, near_pairs)  4.24 us
    pallas_call x1, Pallas kernels, fold_far(): pl.pallas_call(kernel, out_shape=jax.ShapeDtypeStruct(shape, turned.dtype...  3.83 us
    pallas_call x1, Pallas kernels, pick_far(): pl.pallas_call(kernel, out_shape=(jax.ShapeDtypeStruct(own.shape, own.dty...  2.8 us
    unnamed x11, local copies, waits for them, and re-layouts  1.99 us
    pallas_call x1, Pallas kernels, pick_near(): pl.pallas_call(kernel, out_shape=[jax.ShapeDtypeStruct((halo, size, span)...  1.71 us
  transfers between devices with their start and end apart: 4, of which 1 were waited for; matrix products, arithmetic and copies ran while one was open for 0% of the time, Pallas kernels for 27%

profile of v3, /device:TPU:0, one launch (start us, length us, event | category | flops | bytes accessed | tf_op | source)
XLA Modules:
  0.0 53.9 jit_solution(4335938504770031461)
XLA Ops:
  0.0 2.8 %shard_map.46 = (bf16[16,128,512]{2,1,0:T(8,128)(2,1)S(1)}, bf16[8,128,512]{2,1,0:T(8,128)(2,1)}) custom-call(s32[1,16]{1,0:T(1,128)} %sends_hbm.3, bf16[16,128,512]{2,1,0:T(8,128)(2,1)} %bitcast.2), custom_call_target="tpu_custom_call" | custom-call | bytes 655360 | tf_op jit(solution)/shard_map/pallas_call | solution.py:57
  2.8 0.0 copy-start
  2.8 0.7 %collective-permute-start.2 = (bf16[8,128,512]{2,1,0:T(8,128)(2,1)}, bf16[8,128,512]{2,1,0:T(8,128)(2,1)S(1)}, u32[]{:S(2)}, u32[]{:S(2)}) collective-permute-start(bf16[8,128,512]{2,1,0:T(8,128)(2,1)} %get-tuple-element.12), channel_id=1, source_target_pairs={{1,2},{2,1},{3,4},{4,3},{5,6},{6,5},{7,8},{8,7},{9,10},{10,9},{11,... | collective-permute-start | bytes 3145736 | tf_op jit(solution)/shard_map/ppermute | solution.py:292
  3.6 1.7 %shard_map.48 = (bf16[8,128,256]{2,1,0:T(8,128)(2,1)}, bf16[8,128,256]{2,1,0:T(8,128)(2,1)}) custom-call(s32[1,16]{1,0:T(1,128)} %sends_hbm.3, bf16[16,128,512]{2,1,0:T(8,128)(2,1)S(1)} %get-tuple-element.9.own_ref), custom_call_target="tpu_custom_call" | custom-call | bytes 262144 | tf_op jit(solution)/shard_map/pallas_call | solution.py:92
  5.3 4.2 %collective-permute-start = (bf16[8,128,256]{2,1,0:T(8,128)(2,1)}, bf16[8,128,256]{2,1,0:T(8,128)(2,1)}, u32[]{:S(2)}, u32[]{:S(2)}) collective-permute-start(bf16[8,128,256]{2,1,0:T(8,128)(2,1)} %get-tuple-element.10), channel_id=1, source_target_pairs={{0,1},{1,0},{2,3},{3,2},{4,5},{5,4},{6,7},{7,6},{8,9},{9,8},{10,11... | collective-permute-start | bytes 1572872 | tf_op jit(solution)/shard_map/ppermute | solution.py:293
  9.5 0.0 copy-start.4
  9.5 0.0 collective-permute-start.1
  9.5 0.0 copy-done
  9.5 1.5 %shard_map.47.turned_ref = bf16[512,2048]{1,0:T(8,128)(2,1)S(1)} custom-call(bf16[16,128,512]{2,1,0:T(8,128)(2,1)S(1)} %get-tuple-element.9.own_ref), custom_call_target="tpu_custom_call" | custom-call | bytes 524288 | tf_op jit(solution)/shard_map/pallas_call | solution.py:123
  11.0 0.0 copy-done.4
  11.0 0.1 copy.5.columns_ref
  11.1 0.0 copy-start.2
  11.1 1.9 %copy-done.2 = bf16[2,16,3,128,128]{4,3,2,1,0:T(8,128)(2,1)S(1)} copy-done((bf16[2,16,3,128,128]{4,3,2,1,0:T(8,128)(2,1)S(1)}, bf16[2,16,3,128,128]{4,3,2,1,0:T(8,128)(2,1)}, u32[]{:S(2)}) %copy-start.2) | copy-done | bytes 3145752
  13.0 0.0 copy-start.1
  13.0 0.0 copy-start.3
  13.0 3.8 %shard_map.50.folds_ref = bf16[2,512,1024]{2,1,0:T(8,128)(2,1)S(1)} custom-call(s32[2,16,2]{2,1,0:T(8,128)S(1)} %copy.5.columns_ref, bf16[512,2048]{1,0:T(8,128)(2,1)S(1)} %shard_map.47.turned_ref, bf16[2,16,3,128,128]{4,3,2,1,0:T(8,128)(2,1)S(1)} %copy-done.2), custom_call_target="tpu_custom_call" | custom-call | flops 67108864 | bytes 655360 | tf_op jit(solution)/shard_map/pallas_call | solution.py:172
  16.8 0.0 collective-permute-done.refs_0_
  16.8 0.0 collective-permute-done.1.refs_1_
  16.8 0.0 copy-done.1
  16.9 0.0 copy-done.3
  16.9 6.6 %shard_map.49.local_ref = f32[2,512,512]{2,1,0:T(8,128)S(1)} custom-call(s32[2,16,2]{2,1,0:T(8,128)S(1)} %copy.5.columns_ref, bf16[512,2048]{1,0:T(8,128)(2,1)S(1)} %shard_map.47.turned_ref, bf16[16,128,512]{2,1,0:T(8,128)(2,1)S(1)} %copy-done.1, bf16[2,16,3,128,128]{4,3,2,1,0:T(8,128)(2,1)S(1)} %copy-done.3, ...), custom_call_target="tpu_custom_call" | custom-call | flops 469762048 | bytes 1441792 | tf_op jit(solution)/shard_map/pallas_call | solution.py:224
  23.5 0.0 collective-permute-done.2.far_ref
  23.5 0.7 %shard_map.52 = bf16[256,1024]{1,0:T(8,128)(2,1)S(1)} custom-call(f32[2,512,512]{2,1,0:T(8,128)S(1)} %shard_map.49.local_ref, bf16[2,512,1024]{2,1,0:T(8,128)(2,1)S(1)} %shard_map.50.folds_ref, bf16[8,128,512]{2,1,0:T(8,128)(2,1)S(1)} %collective-permute-done.2.far_ref), custom_call_target="tpu_custom_call" | custom-call | flops 67108864 | bytes 393216 | tf_op jit(solution)/shard_map/pallas_call | solution.py:256
  24.2 7.6 %collective-permute-start.3 = (bf16[256,1024]{1,0:T(8,128)(2,1)S(1)}, bf16[256,1024]{1,0:T(8,128)(2,1)S(1)}, u32[]{:S(2)}, u32[]{:S(2)}) collective-permute-start(bf16[256,1024]{1,0:T(8,128)(2,1)S(1)} %shard_map.52), channel_id=1, source_target_pairs={{0,1},{1,0},{2,3},{3,2},{4,5},{5,4},{6,7},{7,6},{8,9},{9,8},{10,11... | collective-permute-start | bytes 1572872 | tf_op jit(solution)/shard_map/ppermute | solution.py:299
  31.8 0.7 %shard_map.51 = f32[256,1024]{1,0:T(8,128)S(1)} custom-call(f32[2,512,512]{2,1,0:T(8,128)S(1)} %shard_map.49.local_ref, bf16[2,512,1024]{2,1,0:T(8,128)(2,1)S(1)} %shard_map.50.folds_ref, bf16[8,128,512]{2,1,0:T(8,128)(2,1)S(1)} %collective-permute-done.2.far_ref), custom_call_target="tpu_custom_call" | custom-call | flops 67108864 | bytes 393216 | tf_op jit(solution)/shard_map/pallas_call | solution.py:256
  32.5 0.8 %collective-permute-done.3 = bf16[256,1024]{1,0:T(8,128)(2,1)S(1)} collective-permute-done((bf16[256,1024]{1,0:T(8,128)(2,1)S(1)}, bf16[256,1024]{1,0:T(8,128)(2,1)S(1)}, u32[]{:S(2)}, u32[]{:S(2)}) %collective-permute-start.3) | collective-permute-done | bytes 524320 | tf_op jit(solution)/shard_map/ppermute | solution.py:299
  33.4 0.1 add_convert_fusion
  33.5 19.6 %all_to_all.5.parts_ref = bf16[8,32,1024]{2,1,0:T(8,128)(2,1)S(1)} all-to-all(bf16[8,32,1024]{2,1,0:T(8,128)(2,1)S(1)} %bitcast.3), channel_id=1, replica_groups={{14,12,10,8,6,4,2,0},{15,13,11,9,7,5,3,1},{30,28,26,24,22,20,18,16},{31..., dimensions={0} | all-to-all | bytes 1048576 | tf_op jit(solution)/shard_map/all_to_all | solution.py:302
  53.1 0.7 %shard_map.53 = f32[32,1024]{1,0:T(8,128)} custom-call(bf16[8,32,1024]{2,1,0:T(8,128)(2,1)S(1)} %all_to_all.5.parts_ref), custom_call_target="tpu_custom_call" | custom-call | bytes 65536 | tf_op jit(solution)/shard_map/pallas_call | solution.py:273
Async XLA Ops:
  2.8 6.7 %copy-start = (bf16[16,128,512]{2,1,0:T(8,128)(2,1)}, bf16[16,128,512]{2,1,0:T(8,128)(2,1)S(1)}, u32[]{:S(2)}) copy-start(bf16[16,128,512]{2,1,0:T(8,128)(2,1)S(1)} %get-tuple-element.9.own_ref) | copy-start | bytes 6291460
  2.8 20.7 %collective-permute-start.2 = (bf16[8,128,512]{2,1,0:T(8,128)(2,1)}, bf16[8,128,512]{2,1,0:T(8,128)(2,1)S(1)}, u32[]{:S(2)}, u32[]{:S(2)}) collective-permute-start(bf16[8,128,512]{2,1,0:T(8,128)(2,1)} %get-tuple-element.12), channel_id=1, source_target_pairs={{1,2},{2,1},{3,4},{4,3},{5,6},{6,5},{7,8},{8,7},{9,10},{10,9},{11,... | collective-permute-start | bytes 3145736 | tf_op jit(solution)/shard_map/ppermute | solution.py:292
  5.3 11.6 %collective-permute-start = (bf16[8,128,256]{2,1,0:T(8,128)(2,1)}, bf16[8,128,256]{2,1,0:T(8,128)(2,1)}, u32[]{:S(2)}, u32[]{:S(2)}) collective-permute-start(bf16[8,128,256]{2,1,0:T(8,128)(2,1)} %get-tuple-element.10), channel_id=1, source_target_pairs={{0,1},{1,0},{2,3},{3,2},{4,5},{5,4},{6,7},{7,6},{8,9},{9,8},{10,11... | collective-permute-start | bytes 1572872 | tf_op jit(solution)/shard_map/ppermute | solution.py:293
  9.5 1.5 %copy-start.4 = (s32[2,16,2]{1,2,0:T(2,128)S(1)}, s32[2,16,2]{1,2,0:T(2,128)}, u32[]{:S(2)}) copy-start(s32[2,16,2]{1,2,0:T(2,128)} %param.6) | copy-start | bytes 772
  9.5 7.3 %collective-permute-start.1 = (bf16[8,128,256]{2,1,0:T(8,128)(2,1)}, bf16[8,128,256]{2,1,0:T(8,128)(2,1)}, u32[]{:S(2)}, u32[]{:S(2)}) collective-permute-start(bf16[8,128,256]{2,1,0:T(8,128)(2,1)} %get-tuple-element.11), channel_id=1, source_target_pairs={{0,1},{1,0},{2,3},{3,2},{4,5},{5,4},{6,7},{7,6},{8,9},{9,8},{10,11... | collective-permute-start | bytes 1572872 | tf_op jit(solution)/shard_map/ppermute | solution.py:293
  11.1 1.9 %copy-start.2 = (bf16[2,16,3,128,128]{4,3,2,1,0:T(8,128)(2,1)S(1)}, bf16[2,16,3,128,128]{4,3,2,1,0:T(8,128)(2,1)}, u32[]{:S(2)}) copy-start(bf16[2,16,3,128,128]{4,3,2,1,0:T(8,128)(2,1)} %blocks_ref.3) | copy-start | bytes 9437188
  13.0 3.9 %copy-start.1 = (bf16[16,128,512]{2,1,0:T(8,128)(2,1)S(1)}, bf16[16,128,512]{2,1,0:T(8,128)(2,1)}, u32[]{:S(2)}) copy-start(bf16[16,128,512]{2,1,0:T(8,128)(2,1)} %copy-done) | copy-start | bytes 6291460
  13.0 3.9 %copy-start.3 = (bf16[2,16,3,128,128]{4,3,2,1,0:T(8,128)(2,1)S(1)}, bf16[2,16,3,128,128]{4,3,2,1,0:T(8,128)(2,1)}, u32[]{:S(2)}) copy-start(bf16[2,16,3,128,128]{4,3,2,1,0:T(8,128)(2,1)} %blocks_ref.3) | copy-start | bytes 9437188
  24.2 9.2 %collective-permute-start.3 = (bf16[256,1024]{1,0:T(8,128)(2,1)S(1)}, bf16[256,1024]{1,0:T(8,128)(2,1)S(1)}, u32[]{:S(2)}, u32[]{:S(2)}) collective-permute-start(bf16[256,1024]{1,0:T(8,128)(2,1)S(1)} %shard_map.52), channel_id=1, source_target_pairs={{0,1},{1,0},{2,3},{3,2},{4,5},{5,4},{6,7},{7,6},{8,9},{9,8},{10,11... | collective-permute-start | bytes 1572872 | tf_op jit(solution)/shard_map/ppermute | solution.py:299

commit v4 on v3

--- a/solution.py
+++ b/solution.py
@@ -26,7 +26,8 @@
 
 
 def chip_order(chips):
-    return list(range(chips - 1, -1, -1))
+    ends = zip(range(chips - 1, -1, -1), range(chips))
+    return [chip for pair in ends for chip in pair][:chips]
 
 
 def halves(width):

time: 54.1 us -> 53.5 us (0.989)
  starting transfers between devices: 12.6 us -> 11.7 us
  Pallas kernels: 18.6 us -> 19.4 us
  blocking collectives: 19.6 us -> 19 us
    ppermute x1, starting transfers between devices: 7.63 us -> 6.76 us  [shards(): taken = lax.ppermute(with_far(local, folds, far, False), AXIS, near_pairs)]
    pallas_call x1, Pallas kernels: 3.83 us -> 4.7 us  [fold_far(): pl.pallas_call(kernel, out_shape=jax.ShapeDtypeStruct(shape, turned.dtype...]
    all_to_all x1, blocking collectives: 19.6 us -> 19 us  [shards(): lax.all_to_all(chip_sum.reshape(chips, width // devices, params * width),...]
  transfers between devices with their start and end apart: 4 -> 4, of which waited for: 1 -> 1; matrix products, arithmetic and copies ran while one was open for 0% -> 0% of each run, Pallas kernels for 27% -> 29%
where the time goes in v4:
time: 53.5 us; the launch traced here: 53.2 us
  Pallas kernels  19.4 us (36%)
  blocking collectives  19 us (36%)
  starting transfers between devices  11.7 us (22%)
  local copies, waits for them, and re-layouts  1.99 us (4%)
  waiting for transfers between devices  0.83 us (2%)
    all_to_all x1, blocking collectives, shards(): lax.all_to_all(chip_sum.reshape(chips, width // devices, params * width),...  19 us
    ppermute x1, starting transfers between devices, shards(): taken = lax.ppermute(with_far(local, folds, far, False), AXIS, near_pairs)  6.76 us
    pallas_call x1, Pallas kernels, local_parts(): pl.pallas_call(kernel, out_shape=jax.ShapeDtypeStruct((params, width, wid...  6.61 us
    pallas_call x1, Pallas kernels, fold_far(): pl.pallas_call(kernel, out_shape=jax.ShapeDtypeStruct(shape, turned.dtype...  4.7 us
    ppermute x2, starting transfers between devices, shards(): lax.ppermute(near, AXIS, near_pairs)  4.24 us
    pallas_call x1, Pallas kernels, pick_far(): pl.pallas_call(kernel, out_shape=(jax.ShapeDtypeStruct(own.shape, own.dty...  2.8 us
    unnamed x11, local copies, waits for them, and re-layouts  1.99 us
    pallas_call x1, Pallas kernels, pick_near(): pl.pallas_call(kernel, out_shape=[jax.ShapeDtypeStruct((halo, size, span)...  1.71 us
  transfers between devices with their start and end apart: 4, of which 1 were waited for; matrix products, arithmetic and copies ran while one was open for 0% of the time, Pallas kernels for 29%

profile of v4, /device:TPU:0, one launch (start us, length us, event | category | flops | bytes accessed | tf_op | source)
XLA Modules:
  0.0 53.2 jit_solution(7019995224985923970)
XLA Ops:
  0.0 2.8 %shard_map.46 = (bf16[16,128,512]{2,1,0:T(8,128)(2,1)S(1)}, bf16[8,128,512]{2,1,0:T(8,128)(2,1)}) custom-call(s32[1,16]{1,0:T(1,128)} %sends_hbm.3, bf16[16,128,512]{2,1,0:T(8,128)(2,1)} %bitcast.2), custom_call_target="tpu_custom_call" | custom-call | bytes 655360 | tf_op jit(solution)/shard_map/pallas_call | solution.py:58
  2.8 0.0 copy-start
  2.8 0.7 %collective-permute-start.2 = (bf16[8,128,512]{2,1,0:T(8,128)(2,1)}, bf16[8,128,512]{2,1,0:T(8,128)(2,1)S(1)}, u32[]{:S(2)}, u32[]{:S(2)}) collective-permute-start(bf16[8,128,512]{2,1,0:T(8,128)(2,1)} %get-tuple-element.12), channel_id=1, source_target_pairs={{1,2},{2,1},{3,4},{4,3},{5,6},{6,5},{7,8},{8,7},{9,10},{10,9},{11,... | collective-permute-start | bytes 3145736 | tf_op jit(solution)/shard_map/ppermute | solution.py:293
  3.6 1.7 %shard_map.48 = (bf16[8,128,256]{2,1,0:T(8,128)(2,1)}, bf16[8,128,256]{2,1,0:T(8,128)(2,1)}) custom-call(s32[1,16]{1,0:T(1,128)} %sends_hbm.3, bf16[16,128,512]{2,1,0:T(8,128)(2,1)S(1)} %get-tuple-element.9.own_ref), custom_call_target="tpu_custom_call" | custom-call | bytes 262144 | tf_op jit(solution)/shard_map/pallas_call | solution.py:93
  5.3 4.2 %collective-permute-start = (bf16[8,128,256]{2,1,0:T(8,128)(2,1)}, bf16[8,128,256]{2,1,0:T(8,128)(2,1)}, u32[]{:S(2)}, u32[]{:S(2)}) collective-permute-start(bf16[8,128,256]{2,1,0:T(8,128)(2,1)} %get-tuple-element.10), channel_id=1, source_target_pairs={{0,1},{1,0},{2,3},{3,2},{4,5},{5,4},{6,7},{7,6},{8,9},{9,8},{10,11... | collective-permute-start | bytes 1572872 | tf_op jit(solution)/shard_map/ppermute | solution.py:294
  9.5 0.0 copy-start.4
  9.5 0.0 collective-permute-start.1
  9.5 0.0 copy-done
  9.5 1.5 %shard_map.47.turned_ref = bf16[512,2048]{1,0:T(8,128)(2,1)S(1)} custom-call(bf16[16,128,512]{2,1,0:T(8,128)(2,1)S(1)} %get-tuple-element.9.own_ref), custom_call_target="tpu_custom_call" | custom-call | bytes 524288 | tf_op jit(solution)/shard_map/pallas_call | solution.py:124
  11.0 0.0 copy-done.4
  11.0 0.1 copy.5.columns_ref
  11.1 0.0 copy-start.2
  11.1 1.9 %copy-done.2 = bf16[2,16,3,128,128]{4,3,2,1,0:T(8,128)(2,1)S(1)} copy-done((bf16[2,16,3,128,128]{4,3,2,1,0:T(8,128)(2,1)S(1)}, bf16[2,16,3,128,128]{4,3,2,1,0:T(8,128)(2,1)}, u32[]{:S(2)}) %copy-start.2) | copy-done | bytes 3145752
  13.0 0.0 copy-start.1
  13.0 0.0 copy-start.3
  13.0 4.7 %shard_map.50.folds_ref = bf16[2,512,1024]{2,1,0:T(8,128)(2,1)S(1)} custom-call(s32[2,16,2]{2,1,0:T(8,128)S(1)} %copy.5.columns_ref, bf16[512,2048]{1,0:T(8,128)(2,1)S(1)} %shard_map.47.turned_ref, bf16[2,16,3,128,128]{4,3,2,1,0:T(8,128)(2,1)S(1)} %copy-done.2), custom_call_target="tpu_custom_call" | custom-call | flops 67108864 | bytes 655360 | tf_op jit(solution)/shard_map/pallas_call | solution.py:173
  17.7 0.0 collective-permute-done.refs_0_
  17.7 0.0 collective-permute-done.1.refs_1_
  17.7 0.0 copy-done.1
  17.7 0.0 copy-done.3
  17.7 6.6 %shard_map.49.local_ref = f32[2,512,512]{2,1,0:T(8,128)S(1)} custom-call(s32[2,16,2]{2,1,0:T(8,128)S(1)} %copy.5.columns_ref, bf16[512,2048]{1,0:T(8,128)(2,1)S(1)} %shard_map.47.turned_ref, bf16[16,128,512]{2,1,0:T(8,128)(2,1)S(1)} %copy-done.1, bf16[2,16,3,128,128]{4,3,2,1,0:T(8,128)(2,1)S(1)} %copy-done.3, ...), custom_call_target="tpu_custom_call" | custom-call | flops 469762048 | bytes 1441792 | tf_op jit(solution)/shard_map/pallas_call | solution.py:225
  24.4 0.0 collective-permute-done.2.far_ref
  24.4 0.7 %shard_map.52 = bf16[256,1024]{1,0:T(8,128)(2,1)S(1)} custom-call(f32[2,512,512]{2,1,0:T(8,128)S(1)} %shard_map.49.local_ref, bf16[2,512,1024]{2,1,0:T(8,128)(2,1)S(1)} %shard_map.50.folds_ref, bf16[8,128,512]{2,1,0:T(8,128)(2,1)S(1)} %collective-permute-done.2.far_ref), custom_call_target="tpu_custom_call" | custom-call | flops 67108864 | bytes 393216 | tf_op jit(solution)/shard_map/pallas_call | solution.py:257
  25.1 6.8 %collective-permute-start.3 = (bf16[256,1024]{1,0:T(8,128)(2,1)S(1)}, bf16[256,1024]{1,0:T(8,128)(2,1)S(1)}, u32[]{:S(2)}, u32[]{:S(2)}) collective-permute-start(bf16[256,1024]{1,0:T(8,128)(2,1)S(1)} %shard_map.52), channel_id=1, source_target_pairs={{0,1},{1,0},{2,3},{3,2},{4,5},{5,4},{6,7},{7,6},{8,9},{9,8},{10,11... | collective-permute-start | bytes 1572872 | tf_op jit(solution)/shard_map/ppermute | solution.py:300
  31.8 0.7 %shard_map.51 = f32[256,1024]{1,0:T(8,128)S(1)} custom-call(f32[2,512,512]{2,1,0:T(8,128)S(1)} %shard_map.49.local_ref, bf16[2,512,1024]{2,1,0:T(8,128)(2,1)S(1)} %shard_map.50.folds_ref, bf16[8,128,512]{2,1,0:T(8,128)(2,1)S(1)} %collective-permute-done.2.far_ref), custom_call_target="tpu_custom_call" | custom-call | flops 67108864 | bytes 393216 | tf_op jit(solution)/shard_map/pallas_call | solution.py:257
  32.5 0.8 %collective-permute-done.3 = bf16[256,1024]{1,0:T(8,128)(2,1)S(1)} collective-permute-done((bf16[256,1024]{1,0:T(8,128)(2,1)S(1)}, bf16[256,1024]{1,0:T(8,128)(2,1)S(1)}, u32[]{:S(2)}, u32[]{:S(2)}) %collective-permute-start.3) | collective-permute-done | bytes 524320 | tf_op jit(solution)/shard_map/ppermute | solution.py:300
  33.4 0.1 add_convert_fusion
  33.5 19.0 %all_to_all.5.parts_ref = bf16[8,32,1024]{2,1,0:T(8,128)(2,1)S(1)} all-to-all(bf16[8,32,1024]{2,1,0:T(8,128)(2,1)S(1)} %bitcast.3), channel_id=1, replica_groups={{14,0,12,2,10,4,8,6},{15,1,13,3,11,5,9,7},{30,16,28,18,26,20,24,22},{31..., dimensions={0} | all-to-all | bytes 1048576 | tf_op jit(solution)/shard_map/all_to_all | solution.py:303
  52.5 0.7 %shard_map.53 = f32[32,1024]{1,0:T(8,128)} custom-call(bf16[8,32,1024]{2,1,0:T(8,128)(2,1)S(1)} %all_to_all.5.parts_ref), custom_call_target="tpu_custom_call" | custom-call | bytes 65536 | tf_op jit(solution)/shard_map/pallas_call | solution.py:274
Async XLA Ops:
  2.8 6.7 %copy-start = (bf16[16,128,512]{2,1,0:T(8,128)(2,1)}, bf16[16,128,512]{2,1,0:T(8,128)(2,1)S(1)}, u32[]{:S(2)}) copy-start(bf16[16,128,512]{2,1,0:T(8,128)(2,1)S(1)} %get-tuple-element.9.own_ref) | copy-start | bytes 6291460
  2.8 21.5 %collective-permute-start.2 = (bf16[8,128,512]{2,1,0:T(8,128)(2,1)}, bf16[8,128,512]{2,1,0:T(8,128)(2,1)S(1)}, u32[]{:S(2)}, u32[]{:S(2)}) collective-permute-start(bf16[8,128,512]{2,1,0:T(8,128)(2,1)} %get-tuple-element.12), channel_id=1, source_target_pairs={{1,2},{2,1},{3,4},{4,3},{5,6},{6,5},{7,8},{8,7},{9,10},{10,9},{11,... | collective-permute-start | bytes 3145736 | tf_op jit(solution)/shard_map/ppermute | solution.py:293
  5.3 12.4 %collective-permute-start = (bf16[8,128,256]{2,1,0:T(8,128)(2,1)}, bf16[8,128,256]{2,1,0:T(8,128)(2,1)}, u32[]{:S(2)}, u32[]{:S(2)}) collective-permute-start(bf16[8,128,256]{2,1,0:T(8,128)(2,1)} %get-tuple-element.10), channel_id=1, source_target_pairs={{0,1},{1,0},{2,3},{3,2},{4,5},{5,4},{6,7},{7,6},{8,9},{9,8},{10,11... | collective-permute-start | bytes 1572872 | tf_op jit(solution)/shard_map/ppermute | solution.py:294
  9.5 1.5 %copy-start.4 = (s32[2,16,2]{1,2,0:T(2,128)S(1)}, s32[2,16,2]{1,2,0:T(2,128)}, u32[]{:S(2)}) copy-start(s32[2,16,2]{1,2,0:T(2,128)} %param.6) | copy-start | bytes 772
  9.5 8.2 %collective-permute-start.1 = (bf16[8,128,256]{2,1,0:T(8,128)(2,1)}, bf16[8,128,256]{2,1,0:T(8,128)(2,1)}, u32[]{:S(2)}, u32[]{:S(2)}) collective-permute-start(bf16[8,128,256]{2,1,0:T(8,128)(2,1)} %get-tuple-element.11), channel_id=1, source_target_pairs={{0,1},{1,0},{2,3},{3,2},{4,5},{5,4},{6,7},{7,6},{8,9},{9,8},{10,11... | collective-permute-start | bytes 1572872 | tf_op jit(solution)/shard_map/ppermute | solution.py:294
  11.1 1.9 %copy-start.2 = (bf16[2,16,3,128,128]{4,3,2,1,0:T(8,128)(2,1)S(1)}, bf16[2,16,3,128,128]{4,3,2,1,0:T(8,128)(2,1)}, u32[]{:S(2)}) copy-start(bf16[2,16,3,128,128]{4,3,2,1,0:T(8,128)(2,1)} %blocks_ref.3) | copy-start | bytes 9437188
  13.0 4.7 %copy-start.1 = (bf16[16,128,512]{2,1,0:T(8,128)(2,1)S(1)}, bf16[16,128,512]{2,1,0:T(8,128)(2,1)}, u32[]{:S(2)}) copy-start(bf16[16,128,512]{2,1,0:T(8,128)(2,1)} %copy-done) | copy-start | bytes 6291460
  13.0 4.7 %copy-start.3 = (bf16[2,16,3,128,128]{4,3,2,1,0:T(8,128)(2,1)S(1)}, bf16[2,16,3,128,128]{4,3,2,1,0:T(8,128)(2,1)}, u32[]{:S(2)}) copy-start(bf16[2,16,3,128,128]{4,3,2,1,0:T(8,128)(2,1)} %blocks_ref.3) | copy-start | bytes 9437188
  25.1 8.3 %collective-permute-start.3 = (bf16[256,1024]{1,0:T(8,128)(2,1)S(1)}, bf16[256,1024]{1,0:T(8,128)(2,1)S(1)}, u32[]{:S(2)}, u32[]{:S(2)}) collective-permute-start(bf16[256,1024]{1,0:T(8,128)(2,1)S(1)} %shard_map.52), channel_id=1, source_target_pairs={{0,1},{1,0},{2,3},{3,2},{4,5},{5,4},{6,7},{7,6},{8,9},{9,8},{10,11... | collective-permute-start | bytes 1572872 | tf_op jit(solution)/shard_map/ppermute | solution.py:300

commit v5 on v4

--- a/solution.py
+++ b/solution.py
@@ -25,8 +25,9 @@
     return both
 
 
-def chip_order(chips):
-    ends = zip(range(chips - 1, -1, -1), range(chips))
+def chip_order(chips, core):
+    up, down = range(chips), range(chips - 1, -1, -1)
+    ends = zip(up, down) if core else zip(down, up)
     return [chip for pair in ends for chip in pair][:chips]
 
 
@@ -104,11 +105,11 @@
 def transposed(own, devices):
     count, size, width = own.shape
     chips, rows = devices // 2, width // devices
-    order = chip_order(chips)
+    orders = [chip_order(chips, core) for core in range(2)]
     if rows % 16:
         turned = own.reshape(count * size, width).T.reshape(chips, 2, rows, count * size)
-        turned = turned[jnp.array(order)]
-        return turned.transpose(1, 0, 2, 3).reshape(width, count * size)
+        turned = jnp.stack([turned[jnp.array(orders[core]), core] for core in range(2)])
+        return turned.reshape(width, count * size)
 
     def kernel(own_ref, out_ref):
         @pl.loop(0, count)
@@ -117,7 +118,7 @@
             turned = own_ref[block].T
             for device in range(devices):
                 chip, core = divmod(device, 2)
-                out_ref[pl.ds((core * chips + order.index(chip)) * rows, rows), cols] = (
+                out_ref[pl.ds((core * chips + orders[core].index(chip)) * rows, rows), cols] = (
                     turned[device * rows : (device + 1) * rows]
                 )
 
@@ -303,7 +304,7 @@
     parts = lax.all_to_all(
         chip_sum.reshape(chips, width // devices, params * width), AXIS,
         split_axis=0, concat_axis=0, tiled=True,
-        axis_index_groups=[[2 * chip + core for chip in chip_order(chips)] for core in range(2)],
+        axis_index_groups=[[2 * chip + core for chip in chip_order(chips, core)] for core in range(2)],
     )
     return add_chips(parts)
 

time: 53.5 us -> 54.2 us (1.013)
  no operation moved by 1% of the time
where the time goes in v5:
time: 54.2 us; the launch traced here: 53.6 us
  Pallas kernels  19.8 us (37%)
  blocking collectives  19.3 us (36%)
  starting transfers between devices  11.4 us (21%)
  local copies, waits for them, and re-layouts  1.99 us (4%)
  waiting for transfers between devices  0.83 us (2%)
    all_to_all x1, blocking collectives, shards(): lax.all_to_all(chip_sum.reshape(chips, width // devices, params * width),...  19.3 us
    pallas_call x1, Pallas kernels, local_parts(): pl.pallas_call(kernel, out_shape=jax.ShapeDtypeStruct((params, width, wid...  6.61 us
    ppermute x1, starting transfers between devices, shards(): taken = lax.ppermute(with_far(local, folds, far, False), AXIS, near_pairs)  6.41 us
    pallas_call x1, Pallas kernels, fold_far(): pl.pallas_call(kernel, out_shape=jax.ShapeDtypeStruct(shape, turned.dtype...  5.04 us
    ppermute x2, starting transfers between devices, shards(): lax.ppermute(near, AXIS, near_pairs)  4.24 us
    pallas_call x1, Pallas kernels, pick_far(): pl.pallas_call(kernel, out_shape=(jax.ShapeDtypeStruct(own.shape, own.dty...  2.8 us
    unnamed x11, local copies, waits for them, and re-layouts  1.99 us
    pallas_call x1, Pallas kernels, pick_near(): pl.pallas_call(kernel, out_shape=[jax.ShapeDtypeStruct((halo, size, span)...  1.71 us
  transfers between devices with their start and end apart: 4, of which 1 were waited for; matrix products, arithmetic and copies ran while one was open for 0% of the time, Pallas kernels for 29%

profile of v5, /device:TPU:0, one launch (start us, length us, event | category | flops | bytes accessed | tf_op | source)
XLA Modules:
  0.0 53.6 jit_solution(10620728997970577756)
XLA Ops:
  0.0 2.8 %shard_map.46 = (bf16[16,128,512]{2,1,0:T(8,128)(2,1)S(1)}, bf16[8,128,512]{2,1,0:T(8,128)(2,1)}) custom-call(s32[1,16]{1,0:T(1,128)} %sends_hbm.3, bf16[16,128,512]{2,1,0:T(8,128)(2,1)} %bitcast.2), custom_call_target="tpu_custom_call" | custom-call | bytes 655360 | tf_op jit(solution)/shard_map/pallas_call | solution.py:59
  2.8 0.0 copy-start
  2.8 0.7 %collective-permute-start.2 = (bf16[8,128,512]{2,1,0:T(8,128)(2,1)}, bf16[8,128,512]{2,1,0:T(8,128)(2,1)S(1)}, u32[]{:S(2)}, u32[]{:S(2)}) collective-permute-start(bf16[8,128,512]{2,1,0:T(8,128)(2,1)} %get-tuple-element.12), channel_id=1, source_target_pairs={{1,2},{2,1},{3,4},{4,3},{5,6},{6,5},{7,8},{8,7},{9,10},{10,9},{11,... | collective-permute-start | bytes 3145736 | tf_op jit(solution)/shard_map/ppermute | solution.py:294
  3.6 1.7 %shard_map.48 = (bf16[8,128,256]{2,1,0:T(8,128)(2,1)}, bf16[8,128,256]{2,1,0:T(8,128)(2,1)}) custom-call(s32[1,16]{1,0:T(1,128)} %sends_hbm.3, bf16[16,128,512]{2,1,0:T(8,128)(2,1)S(1)} %get-tuple-element.9.own_ref), custom_call_target="tpu_custom_call" | custom-call | bytes 262144 | tf_op jit(solution)/shard_map/pallas_call | solution.py:94
  5.3 4.2 %collective-permute-start = (bf16[8,128,256]{2,1,0:T(8,128)(2,1)}, bf16[8,128,256]{2,1,0:T(8,128)(2,1)}, u32[]{:S(2)}, u32[]{:S(2)}) collective-permute-start(bf16[8,128,256]{2,1,0:T(8,128)(2,1)} %get-tuple-element.10), channel_id=1, source_target_pairs={{0,1},{1,0},{2,3},{3,2},{4,5},{5,4},{6,7},{7,6},{8,9},{9,8},{10,11... | collective-permute-start | bytes 1572872 | tf_op jit(solution)/shard_map/ppermute | solution.py:295
  9.5 0.0 copy-start.4
  9.5 0.0 collective-permute-start.1
  9.5 0.0 copy-done
  9.5 1.5 %shard_map.47.turned_ref = bf16[512,2048]{1,0:T(8,128)(2,1)S(1)} custom-call(bf16[16,128,512]{2,1,0:T(8,128)(2,1)S(1)} %get-tuple-element.9.own_ref), custom_call_target="tpu_custom_call" | custom-call | bytes 524288 | tf_op jit(solution)/shard_map/pallas_call | solution.py:125
  11.0 0.0 copy-done.4
  11.0 0.1 copy.5.columns_ref
  11.1 0.0 copy-start.2
  11.1 1.9 %copy-done.2 = bf16[2,16,3,128,128]{4,3,2,1,0:T(8,128)(2,1)S(1)} copy-done((bf16[2,16,3,128,128]{4,3,2,1,0:T(8,128)(2,1)S(1)}, bf16[2,16,3,128,128]{4,3,2,1,0:T(8,128)(2,1)}, u32[]{:S(2)}) %copy-start.2) | copy-done | bytes 3145752
  13.0 0.0 copy-start.1
  13.0 0.0 copy-start.3
  13.0 5.0 %shard_map.50.folds_ref = bf16[2,512,1024]{2,1,0:T(8,128)(2,1)S(1)} custom-call(s32[2,16,2]{2,1,0:T(8,128)S(1)} %copy.5.columns_ref, bf16[512,2048]{1,0:T(8,128)(2,1)S(1)} %shard_map.47.turned_ref, bf16[2,16,3,128,128]{4,3,2,1,0:T(8,128)(2,1)S(1)} %copy-done.2), custom_call_target="tpu_custom_call" | custom-call | flops 67108864 | bytes 655360 | tf_op jit(solution)/shard_map/pallas_call | solution.py:174
  18.0 0.0 collective-permute-done.refs_0_
  18.1 0.0 collective-permute-done.1.refs_1_
  18.1 0.0 copy-done.1
  18.1 0.0 copy-done.3
  18.1 6.6 %shard_map.49.local_ref = f32[2,512,512]{2,1,0:T(8,128)S(1)} custom-call(s32[2,16,2]{2,1,0:T(8,128)S(1)} %copy.5.columns_ref, bf16[512,2048]{1,0:T(8,128)(2,1)S(1)} %shard_map.47.turned_ref, bf16[16,128,512]{2,1,0:T(8,128)(2,1)S(1)} %copy-done.1, bf16[2,16,3,128,128]{4,3,2,1,0:T(8,128)(2,1)S(1)} %copy-done.3, ...), custom_call_target="tpu_custom_call" | custom-call | flops 469762048 | bytes 1441792 | tf_op jit(solution)/shard_map/pallas_call | solution.py:226
  24.7 0.0 collective-permute-done.2.far_ref
  24.7 0.7 %shard_map.52 = bf16[256,1024]{1,0:T(8,128)(2,1)S(1)} custom-call(f32[2,512,512]{2,1,0:T(8,128)S(1)} %shard_map.49.local_ref, bf16[2,512,1024]{2,1,0:T(8,128)(2,1)S(1)} %shard_map.50.folds_ref, bf16[8,128,512]{2,1,0:T(8,128)(2,1)S(1)} %collective-permute-done.2.far_ref), custom_call_target="tpu_custom_call" | custom-call | flops 67108864 | bytes 393216 | tf_op jit(solution)/shard_map/pallas_call | solution.py:258
  25.4 6.4 %collective-permute-start.3 = (bf16[256,1024]{1,0:T(8,128)(2,1)S(1)}, bf16[256,1024]{1,0:T(8,128)(2,1)S(1)}, u32[]{:S(2)}, u32[]{:S(2)}) collective-permute-start(bf16[256,1024]{1,0:T(8,128)(2,1)S(1)} %shard_map.52), channel_id=1, source_target_pairs={{0,1},{1,0},{2,3},{3,2},{4,5},{5,4},{6,7},{7,6},{8,9},{9,8},{10,11... | collective-permute-start | bytes 1572872 | tf_op jit(solution)/shard_map/ppermute | solution.py:301
  31.8 0.7 %shard_map.51 = f32[256,1024]{1,0:T(8,128)S(1)} custom-call(f32[2,512,512]{2,1,0:T(8,128)S(1)} %shard_map.49.local_ref, bf16[2,512,1024]{2,1,0:T(8,128)(2,1)S(1)} %shard_map.50.folds_ref, bf16[8,128,512]{2,1,0:T(8,128)(2,1)S(1)} %collective-permute-done.2.far_ref), custom_call_target="tpu_custom_call" | custom-call | flops 67108864 | bytes 393216 | tf_op jit(solution)/shard_map/pallas_call | solution.py:258
  32.5 0.8 %collective-permute-done.3 = bf16[256,1024]{1,0:T(8,128)(2,1)S(1)} collective-permute-done((bf16[256,1024]{1,0:T(8,128)(2,1)S(1)}, bf16[256,1024]{1,0:T(8,128)(2,1)S(1)}, u32[]{:S(2)}, u32[]{:S(2)}) %collective-permute-start.3) | collective-permute-done | bytes 524320 | tf_op jit(solution)/shard_map/ppermute | solution.py:301
  33.4 0.1 add_convert_fusion
  33.5 19.3 %all_to_all.5.parts_ref = bf16[8,32,1024]{2,1,0:T(8,128)(2,1)S(1)} all-to-all(bf16[8,32,1024]{2,1,0:T(8,128)(2,1)S(1)} %bitcast.3), channel_id=1, replica_groups={{14,0,12,2,10,4,8,6},{1,15,3,13,5,11,7,9},{30,16,28,18,26,20,24,22},{17..., dimensions={0} | all-to-all | bytes 1048576 | tf_op jit(solution)/shard_map/all_to_all | solution.py:304
  52.8 0.7 %shard_map.53 = f32[32,1024]{1,0:T(8,128)} custom-call(bf16[8,32,1024]{2,1,0:T(8,128)(2,1)S(1)} %all_to_all.5.parts_ref), custom_call_target="tpu_custom_call" | custom-call | bytes 65536 | tf_op jit(solution)/shard_map/pallas_call | solution.py:275
Async XLA Ops:
  2.8 6.7 %copy-start = (bf16[16,128,512]{2,1,0:T(8,128)(2,1)}, bf16[16,128,512]{2,1,0:T(8,128)(2,1)S(1)}, u32[]{:S(2)}) copy-start(bf16[16,128,512]{2,1,0:T(8,128)(2,1)S(1)} %get-tuple-element.9.own_ref) | copy-start | bytes 6291460
  2.8 21.9 %collective-permute-start.2 = (bf16[8,128,512]{2,1,0:T(8,128)(2,1)}, bf16[8,128,512]{2,1,0:T(8,128)(2,1)S(1)}, u32[]{:S(2)}, u32[]{:S(2)}) collective-permute-start(bf16[8,128,512]{2,1,0:T(8,128)(2,1)} %get-tuple-element.12), channel_id=1, source_target_pairs={{1,2},{2,1},{3,4},{4,3},{5,6},{6,5},{7,8},{8,7},{9,10},{10,9},{11,... | collective-permute-start | bytes 3145736 | tf_op jit(solution)/shard_map/ppermute | solution.py:294
  5.3 12.8 %collective-permute-start = (bf16[8,128,256]{2,1,0:T(8,128)(2,1)}, bf16[8,128,256]{2,1,0:T(8,128)(2,1)}, u32[]{:S(2)}, u32[]{:S(2)}) collective-permute-start(bf16[8,128,256]{2,1,0:T(8,128)(2,1)} %get-tuple-element.10), channel_id=1, source_target_pairs={{0,1},{1,0},{2,3},{3,2},{4,5},{5,4},{6,7},{7,6},{8,9},{9,8},{10,11... | collective-permute-start | bytes 1572872 | tf_op jit(solution)/shard_map/ppermute | solution.py:295
  9.5 1.5 %copy-start.4 = (s32[2,16,2]{1,2,0:T(2,128)S(1)}, s32[2,16,2]{1,2,0:T(2,128)}, u32[]{:S(2)}) copy-start(s32[2,16,2]{1,2,0:T(2,128)} %param.6) | copy-start | bytes 772
  9.5 8.6 %collective-permute-start.1 = (bf16[8,128,256]{2,1,0:T(8,128)(2,1)}, bf16[8,128,256]{2,1,0:T(8,128)(2,1)}, u32[]{:S(2)}, u32[]{:S(2)}) collective-permute-start(bf16[8,128,256]{2,1,0:T(8,128)(2,1)} %get-tuple-element.11), channel_id=1, source_target_pairs={{0,1},{1,0},{2,3},{3,2},{4,5},{5,4},{6,7},{7,6},{8,9},{9,8},{10,11... | collective-permute-start | bytes 1572872 | tf_op jit(solution)/shard_map/ppermute | solution.py:295
  11.1 1.9 %copy-start.2 = (bf16[2,16,3,128,128]{4,3,2,1,0:T(8,128)(2,1)S(1)}, bf16[2,16,3,128,128]{4,3,2,1,0:T(8,128)(2,1)}, u32[]{:S(2)}) copy-start(bf16[2,16,3,128,128]{4,3,2,1,0:T(8,128)(2,1)} %blocks_ref.3) | copy-start | bytes 9437188
  13.0 5.1 %copy-start.1 = (bf16[16,128,512]{2,1,0:T(8,128)(2,1)S(1)}, bf16[16,128,512]{2,1,0:T(8,128)(2,1)}, u32[]{:S(2)}) copy-start(bf16[16,128,512]{2,1,0:T(8,128)(2,1)} %copy-done) | copy-start | bytes 6291460
  13.0 5.1 %copy-start.3 = (bf16[2,16,3,128,128]{4,3,2,1,0:T(8,128)(2,1)S(1)}, bf16[2,16,3,128,128]{4,3,2,1,0:T(8,128)(2,1)}, u32[]{:S(2)}) copy-start(bf16[2,16,3,128,128]{4,3,2,1,0:T(8,128)(2,1)} %blocks_ref.3) | copy-start | bytes 9437188
  25.4 8.0 %collective-permute-start.3 = (bf16[256,1024]{1,0:T(8,128)(2,1)S(1)}, bf16[256,1024]{1,0:T(8,128)(2,1)S(1)}, u32[]{:S(2)}, u32[]{:S(2)}) collective-permute-start(bf16[256,1024]{1,0:T(8,128)(2,1)S(1)} %shard_map.52), channel_id=1, source_target_pairs={{0,1},{1,0},{2,3},{3,2},{4,5},{5,4},{6,7},{7,6},{8,9},{9,8},{10,11... | collective-permute-start | bytes 1572872 | tf_op jit(solution)/shard_map/ppermute | solution.py:301

commit v6 on v3

--- a/solution.py
+++ b/solution.py
@@ -26,7 +26,10 @@
 
 
 def chip_order(chips):
-    return list(range(chips - 1, -1, -1))
+    half = chips // 2
+    pairs_of = zip(range(chips - 1, half - 1, -1), range(chips - half - 1, -1, -1))
+    order = [chip for pair in pairs_of for chip in pair]
+    return order + [chip for chip in range(chips) if chip not in order]
 
 
 def halves(width):

time: 54.1 us -> 54.1 us (level)
  starting transfers between devices: 12.6 us -> 10.7 us
  Pallas kernels: 18.6 us -> 20.5 us
    ppermute x1, starting transfers between devices: 7.63 us -> 5.72 us  [shards(): taken = lax.ppermute(with_far(local, folds, far, False), AXIS, near_pairs)]
    pallas_call x1, Pallas kernels: 3.83 us -> 5.74 us  [fold_far(): pl.pallas_call(kernel, out_shape=jax.ShapeDtypeStruct(shape, turned.dtype...]
  transfers between devices with their start and end apart: 4 -> 4, of which waited for: 1 -> 1; matrix products, arithmetic and copies ran while one was open for 0% -> 0% of each run, Pallas kernels for 27% -> 30%
where the time goes in v6:
time: 54.1 us; the launch traced here: 53.9 us
  Pallas kernels  20.5 us (38%)
  blocking collectives  19.6 us (36%)
  starting transfers between devices  10.7 us (20%)
  local copies, waits for them, and re-layouts  1.99 us (4%)
  waiting for transfers between devices  0.83 us (2%)
    all_to_all x1, blocking collectives, shards(): lax.all_to_all(chip_sum.reshape(chips, width // devices, params * width),...  19.6 us
    pallas_call x1, Pallas kernels, local_parts(): pl.pallas_call(kernel, out_shape=jax.ShapeDtypeStruct((params, width, wid...  6.61 us
    pallas_call x1, Pallas kernels, fold_far(): pl.pallas_call(kernel, out_shape=jax.ShapeDtypeStruct(shape, turned.dtype...  5.74 us
    ppermute x1, starting transfers between devices, shards(): taken = lax.ppermute(with_far(local, folds, far, False), AXIS, near_pairs)  5.72 us
    ppermute x2, starting transfers between devices, shards(): lax.ppermute(near, AXIS, near_pairs)  4.24 us
    pallas_call x1, Pallas kernels, pick_far(): pl.pallas_call(kernel, out_shape=(jax.ShapeDtypeStruct(own.shape, own.dty...  2.8 us
    unnamed x11, local copies, waits for them, and re-layouts  1.99 us
    pallas_call x1, Pallas kernels, pick_near(): pl.pallas_call(kernel, out_shape=[jax.ShapeDtypeStruct((halo, size, span)...  1.71 us
  transfers between devices with their start and end apart: 4, of which 1 were waited for; matrix products, arithmetic and copies ran while one was open for 0% of the time, Pallas kernels for 30%

profile of v6, /device:TPU:0, one launch (start us, length us, event | category | flops | bytes accessed | tf_op | source)
XLA Modules:
  0.0 53.9 jit_solution(5935318077850975297)
XLA Ops:
  0.0 2.8 %shard_map.46 = (bf16[16,128,512]{2,1,0:T(8,128)(2,1)S(1)}, bf16[8,128,512]{2,1,0:T(8,128)(2,1)}) custom-call(s32[1,16]{1,0:T(1,128)} %sends_hbm.3, bf16[16,128,512]{2,1,0:T(8,128)(2,1)} %bitcast.2), custom_call_target="tpu_custom_call" | custom-call | bytes 655360 | tf_op jit(solution)/shard_map/pallas_call | solution.py:60
  2.8 0.0 copy-start
  2.8 0.7 %collective-permute-start.2 = (bf16[8,128,512]{2,1,0:T(8,128)(2,1)}, bf16[8,128,512]{2,1,0:T(8,128)(2,1)S(1)}, u32[]{:S(2)}, u32[]{:S(2)}) collective-permute-start(bf16[8,128,512]{2,1,0:T(8,128)(2,1)} %get-tuple-element.12), channel_id=1, source_target_pairs={{1,2},{2,1},{3,4},{4,3},{5,6},{6,5},{7,8},{8,7},{9,10},{10,9},{11,... | collective-permute-start | bytes 3145736 | tf_op jit(solution)/shard_map/ppermute | solution.py:295
  3.6 1.7 %shard_map.48 = (bf16[8,128,256]{2,1,0:T(8,128)(2,1)}, bf16[8,128,256]{2,1,0:T(8,128)(2,1)}) custom-call(s32[1,16]{1,0:T(1,128)} %sends_hbm.3, bf16[16,128,512]{2,1,0:T(8,128)(2,1)S(1)} %get-tuple-element.9.own_ref), custom_call_target="tpu_custom_call" | custom-call | bytes 262144 | tf_op jit(solution)/shard_map/pallas_call | solution.py:95
  5.3 4.2 %collective-permute-start = (bf16[8,128,256]{2,1,0:T(8,128)(2,1)}, bf16[8,128,256]{2,1,0:T(8,128)(2,1)}, u32[]{:S(2)}, u32[]{:S(2)}) collective-permute-start(bf16[8,128,256]{2,1,0:T(8,128)(2,1)} %get-tuple-element.10), channel_id=1, source_target_pairs={{0,1},{1,0},{2,3},{3,2},{4,5},{5,4},{6,7},{7,6},{8,9},{9,8},{10,11... | collective-permute-start | bytes 1572872 | tf_op jit(solution)/shard_map/ppermute | solution.py:296
  9.5 0.0 copy-start.4
  9.5 0.0 collective-permute-start.1
  9.5 0.0 copy-done
  9.5 1.5 %shard_map.47.turned_ref = bf16[512,2048]{1,0:T(8,128)(2,1)S(1)} custom-call(bf16[16,128,512]{2,1,0:T(8,128)(2,1)S(1)} %get-tuple-element.9.own_ref), custom_call_target="tpu_custom_call" | custom-call | bytes 524288 | tf_op jit(solution)/shard_map/pallas_call | solution.py:126
  11.0 0.0 copy-done.4
  11.0 0.1 copy.5.columns_ref
  11.1 0.0 copy-start.2
  11.1 1.9 %copy-done.2 = bf16[2,16,3,128,128]{4,3,2,1,0:T(8,128)(2,1)S(1)} copy-done((bf16[2,16,3,128,128]{4,3,2,1,0:T(8,128)(2,1)S(1)}, bf16[2,16,3,128,128]{4,3,2,1,0:T(8,128)(2,1)}, u32[]{:S(2)}) %copy-start.2) | copy-done | bytes 3145752
  13.0 0.0 copy-start.1
  13.0 0.0 copy-start.3
  13.0 5.7 %shard_map.50.folds_ref = bf16[2,512,1024]{2,1,0:T(8,128)(2,1)S(1)} custom-call(s32[2,16,2]{2,1,0:T(8,128)S(1)} %copy.5.columns_ref, bf16[512,2048]{1,0:T(8,128)(2,1)S(1)} %shard_map.47.turned_ref, bf16[2,16,3,128,128]{4,3,2,1,0:T(8,128)(2,1)S(1)} %copy-done.2), custom_call_target="tpu_custom_call" | custom-call | flops 67108864 | bytes 655360 | tf_op jit(solution)/shard_map/pallas_call | solution.py:175
  18.7 0.0 collective-permute-done.refs_0_
  18.7 0.0 collective-permute-done.1.refs_1_
  18.8 0.0 copy-done.1
  18.8 0.0 copy-done.3
  18.8 6.6 %shard_map.49.local_ref = f32[2,512,512]{2,1,0:T(8,128)S(1)} custom-call(s32[2,16,2]{2,1,0:T(8,128)S(1)} %copy.5.columns_ref, bf16[512,2048]{1,0:T(8,128)(2,1)S(1)} %shard_map.47.turned_ref, bf16[16,128,512]{2,1,0:T(8,128)(2,1)S(1)} %copy-done.1, bf16[2,16,3,128,128]{4,3,2,1,0:T(8,128)(2,1)S(1)} %copy-done.3, ...), custom_call_target="tpu_custom_call" | custom-call | flops 469762048 | bytes 1441792 | tf_op jit(solution)/shard_map/pallas_call | solution.py:227
  25.4 0.0 collective-permute-done.2.far_ref
  25.4 0.7 %shard_map.52 = bf16[256,1024]{1,0:T(8,128)(2,1)S(1)} custom-call(f32[2,512,512]{2,1,0:T(8,128)S(1)} %shard_map.49.local_ref, bf16[2,512,1024]{2,1,0:T(8,128)(2,1)S(1)} %shard_map.50.folds_ref, bf16[8,128,512]{2,1,0:T(8,128)(2,1)S(1)} %collective-permute-done.2.far_ref), custom_call_target="tpu_custom_call" | custom-call | flops 67108864 | bytes 393216 | tf_op jit(solution)/shard_map/pallas_call | solution.py:259
  26.1 5.7 %collective-permute-start.3 = (bf16[256,1024]{1,0:T(8,128)(2,1)S(1)}, bf16[256,1024]{1,0:T(8,128)(2,1)S(1)}, u32[]{:S(2)}, u32[]{:S(2)}) collective-permute-start(bf16[256,1024]{1,0:T(8,128)(2,1)S(1)} %shard_map.52), channel_id=1, source_target_pairs={{0,1},{1,0},{2,3},{3,2},{4,5},{5,4},{6,7},{7,6},{8,9},{9,8},{10,11... | collective-permute-start | bytes 1572872 | tf_op jit(solution)/shard_map/ppermute | solution.py:302
  31.8 0.7 %shard_map.51 = f32[256,1024]{1,0:T(8,128)S(1)} custom-call(f32[2,512,512]{2,1,0:T(8,128)S(1)} %shard_map.49.local_ref, bf16[2,512,1024]{2,1,0:T(8,128)(2,1)S(1)} %shard_map.50.folds_ref, bf16[8,128,512]{2,1,0:T(8,128)(2,1)S(1)} %collective-permute-done.2.far_ref), custom_call_target="tpu_custom_call" | custom-call | flops 67108864 | bytes 393216 | tf_op jit(solution)/shard_map/pallas_call | solution.py:259
  32.5 0.8 %collective-permute-done.3 = bf16[256,1024]{1,0:T(8,128)(2,1)S(1)} collective-permute-done((bf16[256,1024]{1,0:T(8,128)(2,1)S(1)}, bf16[256,1024]{1,0:T(8,128)(2,1)S(1)}, u32[]{:S(2)}, u32[]{:S(2)}) %collective-permute-start.3) | collective-permute-done | bytes 524320 | tf_op jit(solution)/shard_map/ppermute | solution.py:302
  33.4 0.1 add_convert_fusion
  33.5 19.6 %all_to_all.5.parts_ref = bf16[8,32,1024]{2,1,0:T(8,128)(2,1)S(1)} all-to-all(bf16[8,32,1024]{2,1,0:T(8,128)(2,1)S(1)} %bitcast.3), channel_id=1, replica_groups={{14,6,12,4,10,2,8,0},{15,7,13,5,11,3,9,1},{30,22,28,20,26,18,24,16},{31..., dimensions={0} | all-to-all | bytes 1048576 | tf_op jit(solution)/shard_map/all_to_all | solution.py:305
  53.1 0.7 %shard_map.53 = f32[32,1024]{1,0:T(8,128)} custom-call(bf16[8,32,1024]{2,1,0:T(8,128)(2,1)S(1)} %all_to_all.5.parts_ref), custom_call_target="tpu_custom_call" | custom-call | bytes 65536 | tf_op jit(solution)/shard_map/pallas_call | solution.py:276
Async XLA Ops:
  2.8 6.7 %copy-start = (bf16[16,128,512]{2,1,0:T(8,128)(2,1)}, bf16[16,128,512]{2,1,0:T(8,128)(2,1)S(1)}, u32[]{:S(2)}) copy-start(bf16[16,128,512]{2,1,0:T(8,128)(2,1)S(1)} %get-tuple-element.9.own_ref) | copy-start | bytes 6291460
  2.8 22.6 %collective-permute-start.2 = (bf16[8,128,512]{2,1,0:T(8,128)(2,1)}, bf16[8,128,512]{2,1,0:T(8,128)(2,1)S(1)}, u32[]{:S(2)}, u32[]{:S(2)}) collective-permute-start(bf16[8,128,512]{2,1,0:T(8,128)(2,1)} %get-tuple-element.12), channel_id=1, source_target_pairs={{1,2},{2,1},{3,4},{4,3},{5,6},{6,5},{7,8},{8,7},{9,10},{10,9},{11,... | collective-permute-start | bytes 3145736 | tf_op jit(solution)/shard_map/ppermute | solution.py:295
  5.3 13.5 %collective-permute-start = (bf16[8,128,256]{2,1,0:T(8,128)(2,1)}, bf16[8,128,256]{2,1,0:T(8,128)(2,1)}, u32[]{:S(2)}, u32[]{:S(2)}) collective-permute-start(bf16[8,128,256]{2,1,0:T(8,128)(2,1)} %get-tuple-element.10), channel_id=1, source_target_pairs={{0,1},{1,0},{2,3},{3,2},{4,5},{5,4},{6,7},{7,6},{8,9},{9,8},{10,11... | collective-permute-start | bytes 1572872 | tf_op jit(solution)/shard_map/ppermute | solution.py:296
  9.5 1.5 %copy-start.4 = (s32[2,16,2]{1,2,0:T(2,128)S(1)}, s32[2,16,2]{1,2,0:T(2,128)}, u32[]{:S(2)}) copy-start(s32[2,16,2]{1,2,0:T(2,128)} %param.6) | copy-start | bytes 772
  9.5 9.3 %collective-permute-start.1 = (bf16[8,128,256]{2,1,0:T(8,128)(2,1)}, bf16[8,128,256]{2,1,0:T(8,128)(2,1)}, u32[]{:S(2)}, u32[]{:S(2)}) collective-permute-start(bf16[8,128,256]{2,1,0:T(8,128)(2,1)} %get-tuple-element.11), channel_id=1, source_target_pairs={{0,1},{1,0},{2,3},{3,2},{4,5},{5,4},{6,7},{7,6},{8,9},{9,8},{10,11... | collective-permute-start | bytes 1572872 | tf_op jit(solution)/shard_map/ppermute | solution.py:296
  11.1 1.9 %copy-start.2 = (bf16[2,16,3,128,128]{4,3,2,1,0:T(8,128)(2,1)S(1)}, bf16[2,16,3,128,128]{4,3,2,1,0:T(8,128)(2,1)}, u32[]{:S(2)}) copy-start(bf16[2,16,3,128,128]{4,3,2,1,0:T(8,128)(2,1)} %blocks_ref.3) | copy-start | bytes 9437188
  13.0 5.8 %copy-start.1 = (bf16[16,128,512]{2,1,0:T(8,128)(2,1)S(1)}, bf16[16,128,512]{2,1,0:T(8,128)(2,1)}, u32[]{:S(2)}) copy-start(bf16[16,128,512]{2,1,0:T(8,128)(2,1)} %copy-done) | copy-start | bytes 6291460
  13.0 5.8 %copy-start.3 = (bf16[2,16,3,128,128]{4,3,2,1,0:T(8,128)(2,1)S(1)}, bf16[2,16,3,128,128]{4,3,2,1,0:T(8,128)(2,1)}, u32[]{:S(2)}) copy-start(bf16[2,16,3,128,128]{4,3,2,1,0:T(8,128)(2,1)} %blocks_ref.3) | copy-start | bytes 9437188
  26.1 7.3 %collective-permute-start.3 = (bf16[256,1024]{1,0:T(8,128)(2,1)S(1)}, bf16[256,1024]{1,0:T(8,128)(2,1)S(1)}, u32[]{:S(2)}, u32[]{:S(2)}) collective-permute-start(bf16[256,1024]{1,0:T(8,128)(2,1)S(1)} %shard_map.52), channel_id=1, source_target_pairs={{0,1},{1,0},{2,3},{3,2},{4,5},{5,4},{6,7},{7,6},{8,9},{9,8},{10,11... | collective-permute-start | bytes 1572872 | tf_op jit(solution)/shard_map/ppermute | solution.py:302

commit v7 on v3

--- a/solution.py
+++ b/solution.py
@@ -26,7 +26,10 @@
 
 
 def chip_order(chips):
-    return list(range(chips - 1, -1, -1))
+    low = [chip ^ 1 for chip in range(chips)] if chips % 2 == 0 else list(range(chips))
+    ends = zip(range(chips - 1, -1, -1), low)
+    order = [chip for pair in ends for chip in pair][:chips]
+    return order if len(set(order)) == chips else list(range(chips))
 
 
 def halves(width):

time: 54.1 us -> 53.8 us (level)
  starting transfers between devices: 12.6 us -> 11 us
  Pallas kernels: 18.6 us -> 20.1 us
    ppermute x1, starting transfers between devices: 7.63 us -> 6.06 us  [shards(): taken = lax.ppermute(with_far(local, folds, far, False), AXIS, near_pairs)]
    pallas_call x1, Pallas kernels: 3.83 us -> 5.39 us  [fold_far(): pl.pallas_call(kernel, out_shape=jax.ShapeDtypeStruct(shape, turned.dtype...]
  transfers between devices with their start and end apart: 4 -> 4, of which waited for: 1 -> 1; matrix products, arithmetic and copies ran while one was open for 0% -> 0% of each run, Pallas kernels for 27% -> 30%
where the time goes in v7:
time: 53.8 us; the launch traced here: 53.5 us
  Pallas kernels  20.1 us (37%)
  blocking collectives  19.3 us (36%)
  starting transfers between devices  11 us (20%)
  local copies, waits for them, and re-layouts  1.99 us (4%)
  waiting for transfers between devices  0.83 us (2%)
    all_to_all x1, blocking collectives, shards(): lax.all_to_all(chip_sum.reshape(chips, width // devices, params * width),...  19.3 us
    pallas_call x1, Pallas kernels, local_parts(): pl.pallas_call(kernel, out_shape=jax.ShapeDtypeStruct((params, width, wid...  6.62 us
    ppermute x1, starting transfers between devices, shards(): taken = lax.ppermute(with_far(local, folds, far, False), AXIS, near_pairs)  6.06 us
    pallas_call x1, Pallas kernels, fold_far(): pl.pallas_call(kernel, out_shape=jax.ShapeDtypeStruct(shape, turned.dtype...  5.39 us
    ppermute x2, starting transfers between devices, shards(): lax.ppermute(near, AXIS, near_pairs)  4.24 us
    pallas_call x1, Pallas kernels, pick_far(): pl.pallas_call(kernel, out_shape=(jax.ShapeDtypeStruct(own.shape, own.dty...  2.8 us
    unnamed x11, local copies, waits for them, and re-layouts  1.99 us
    pallas_call x1, Pallas kernels, pick_near(): pl.pallas_call(kernel, out_shape=[jax.ShapeDtypeStruct((halo, size, span)...  1.71 us
  transfers between devices with their start and end apart: 4, of which 1 were waited for; matrix products, arithmetic and copies ran while one was open for 0% of the time, Pallas kernels for 30%

profile of v7, /device:TPU:0, one launch (start us, length us, event | category | flops | bytes accessed | tf_op | source)
XLA Modules:
  0.0 53.5 jit_solution(5533594098168344341)
XLA Ops:
  0.0 2.8 %shard_map.46 = (bf16[16,128,512]{2,1,0:T(8,128)(2,1)S(1)}, bf16[8,128,512]{2,1,0:T(8,128)(2,1)}) custom-call(s32[1,16]{1,0:T(1,128)} %sends_hbm.3, bf16[16,128,512]{2,1,0:T(8,128)(2,1)} %bitcast.2), custom_call_target="tpu_custom_call" | custom-call | bytes 655360 | tf_op jit(solution)/shard_map/pallas_call | solution.py:60
  2.8 0.0 copy-start
  2.8 0.7 %collective-permute-start.2 = (bf16[8,128,512]{2,1,0:T(8,128)(2,1)}, bf16[8,128,512]{2,1,0:T(8,128)(2,1)S(1)}, u32[]{:S(2)}, u32[]{:S(2)}) collective-permute-start(bf16[8,128,512]{2,1,0:T(8,128)(2,1)} %get-tuple-element.12), channel_id=1, source_target_pairs={{1,2},{2,1},{3,4},{4,3},{5,6},{6,5},{7,8},{8,7},{9,10},{10,9},{11,... | collective-permute-start | bytes 3145736 | tf_op jit(solution)/shard_map/ppermute | solution.py:295
  3.6 1.7 %shard_map.48 = (bf16[8,128,256]{2,1,0:T(8,128)(2,1)}, bf16[8,128,256]{2,1,0:T(8,128)(2,1)}) custom-call(s32[1,16]{1,0:T(1,128)} %sends_hbm.3, bf16[16,128,512]{2,1,0:T(8,128)(2,1)S(1)} %get-tuple-element.9.own_ref), custom_call_target="tpu_custom_call" | custom-call | bytes 262144 | tf_op jit(solution)/shard_map/pallas_call | solution.py:95
  5.3 4.2 %collective-permute-start = (bf16[8,128,256]{2,1,0:T(8,128)(2,1)}, bf16[8,128,256]{2,1,0:T(8,128)(2,1)}, u32[]{:S(2)}, u32[]{:S(2)}) collective-permute-start(bf16[8,128,256]{2,1,0:T(8,128)(2,1)} %get-tuple-element.10), channel_id=1, source_target_pairs={{0,1},{1,0},{2,3},{3,2},{4,5},{5,4},{6,7},{7,6},{8,9},{9,8},{10,11... | collective-permute-start | bytes 1572872 | tf_op jit(solution)/shard_map/ppermute | solution.py:296
  9.5 0.0 copy-start.4
  9.5 0.0 collective-permute-start.1
  9.5 0.0 copy-done
  9.5 1.5 %shard_map.47.turned_ref = bf16[512,2048]{1,0:T(8,128)(2,1)S(1)} custom-call(bf16[16,128,512]{2,1,0:T(8,128)(2,1)S(1)} %get-tuple-element.9.own_ref), custom_call_target="tpu_custom_call" | custom-call | bytes 524288 | tf_op jit(solution)/shard_map/pallas_call | solution.py:126
  11.0 0.0 copy-done.4
  11.0 0.1 copy.5.columns_ref
  11.1 0.0 copy-start.2
  11.1 1.9 %copy-done.2 = bf16[2,16,3,128,128]{4,3,2,1,0:T(8,128)(2,1)S(1)} copy-done((bf16[2,16,3,128,128]{4,3,2,1,0:T(8,128)(2,1)S(1)}, bf16[2,16,3,128,128]{4,3,2,1,0:T(8,128)(2,1)}, u32[]{:S(2)}) %copy-start.2) | copy-done | bytes 3145752
  13.0 0.0 copy-start.1
  13.0 0.0 copy-start.3
  13.0 5.4 %shard_map.50.folds_ref = bf16[2,512,1024]{2,1,0:T(8,128)(2,1)S(1)} custom-call(s32[2,16,2]{2,1,0:T(8,128)S(1)} %copy.5.columns_ref, bf16[512,2048]{1,0:T(8,128)(2,1)S(1)} %shard_map.47.turned_ref, bf16[2,16,3,128,128]{4,3,2,1,0:T(8,128)(2,1)S(1)} %copy-done.2), custom_call_target="tpu_custom_call" | custom-call | flops 67108864 | bytes 655360 | tf_op jit(solution)/shard_map/pallas_call | solution.py:175
  18.4 0.0 collective-permute-done.refs_0_
  18.4 0.0 collective-permute-done.1.refs_1_
  18.4 0.0 copy-done.1
  18.4 0.0 copy-done.3
  18.4 6.6 %shard_map.49.local_ref = f32[2,512,512]{2,1,0:T(8,128)S(1)} custom-call(s32[2,16,2]{2,1,0:T(8,128)S(1)} %copy.5.columns_ref, bf16[512,2048]{1,0:T(8,128)(2,1)S(1)} %shard_map.47.turned_ref, bf16[16,128,512]{2,1,0:T(8,128)(2,1)S(1)} %copy-done.1, bf16[2,16,3,128,128]{4,3,2,1,0:T(8,128)(2,1)S(1)} %copy-done.3, ...), custom_call_target="tpu_custom_call" | custom-call | flops 469762048 | bytes 1441792 | tf_op jit(solution)/shard_map/pallas_call | solution.py:227
  25.0 0.0 collective-permute-done.2.far_ref
  25.1 0.7 %shard_map.52 = bf16[256,1024]{1,0:T(8,128)(2,1)S(1)} custom-call(f32[2,512,512]{2,1,0:T(8,128)S(1)} %shard_map.49.local_ref, bf16[2,512,1024]{2,1,0:T(8,128)(2,1)S(1)} %shard_map.50.folds_ref, bf16[8,128,512]{2,1,0:T(8,128)(2,1)S(1)} %collective-permute-done.2.far_ref), custom_call_target="tpu_custom_call" | custom-call | flops 67108864 | bytes 393216 | tf_op jit(solution)/shard_map/pallas_call | solution.py:259
  25.8 6.1 %collective-permute-start.3 = (bf16[256,1024]{1,0:T(8,128)(2,1)S(1)}, bf16[256,1024]{1,0:T(8,128)(2,1)S(1)}, u32[]{:S(2)}, u32[]{:S(2)}) collective-permute-start(bf16[256,1024]{1,0:T(8,128)(2,1)S(1)} %shard_map.52), channel_id=1, source_target_pairs={{0,1},{1,0},{2,3},{3,2},{4,5},{5,4},{6,7},{7,6},{8,9},{9,8},{10,11... | collective-permute-start | bytes 1572872 | tf_op jit(solution)/shard_map/ppermute | solution.py:302
  31.8 0.7 %shard_map.51 = f32[256,1024]{1,0:T(8,128)S(1)} custom-call(f32[2,512,512]{2,1,0:T(8,128)S(1)} %shard_map.49.local_ref, bf16[2,512,1024]{2,1,0:T(8,128)(2,1)S(1)} %shard_map.50.folds_ref, bf16[8,128,512]{2,1,0:T(8,128)(2,1)S(1)} %collective-permute-done.2.far_ref), custom_call_target="tpu_custom_call" | custom-call | flops 67108864 | bytes 393216 | tf_op jit(solution)/shard_map/pallas_call | solution.py:259
  32.5 0.8 %collective-permute-done.3 = bf16[256,1024]{1,0:T(8,128)(2,1)S(1)} collective-permute-done((bf16[256,1024]{1,0:T(8,128)(2,1)S(1)}, bf16[256,1024]{1,0:T(8,128)(2,1)S(1)}, u32[]{:S(2)}, u32[]{:S(2)}) %collective-permute-start.3) | collective-permute-done | bytes 524320 | tf_op jit(solution)/shard_map/ppermute | solution.py:302
  33.4 0.1 add_convert_fusion
  33.5 19.3 %all_to_all.5.parts_ref = bf16[8,32,1024]{2,1,0:T(8,128)(2,1)S(1)} all-to-all(bf16[8,32,1024]{2,1,0:T(8,128)(2,1)S(1)} %bitcast.3), channel_id=1, replica_groups={{14,2,12,0,10,6,8,4},{15,3,13,1,11,7,9,5},{30,18,28,16,26,22,24,20},{31..., dimensions={0} | all-to-all | bytes 1048576 | tf_op jit(solution)/shard_map/all_to_all | solution.py:305
  52.8 0.7 %shard_map.53 = f32[32,1024]{1,0:T(8,128)} custom-call(bf16[8,32,1024]{2,1,0:T(8,128)(2,1)S(1)} %all_to_all.5.parts_ref), custom_call_target="tpu_custom_call" | custom-call | bytes 65536 | tf_op jit(solution)/shard_map/pallas_call | solution.py:276
Async XLA Ops:
  2.8 6.7 %copy-start = (bf16[16,128,512]{2,1,0:T(8,128)(2,1)}, bf16[16,128,512]{2,1,0:T(8,128)(2,1)S(1)}, u32[]{:S(2)}) copy-start(bf16[16,128,512]{2,1,0:T(8,128)(2,1)S(1)} %get-tuple-element.9.own_ref) | copy-start | bytes 6291460
  2.8 22.2 %collective-permute-start.2 = (bf16[8,128,512]{2,1,0:T(8,128)(2,1)}, bf16[8,128,512]{2,1,0:T(8,128)(2,1)S(1)}, u32[]{:S(2)}, u32[]{:S(2)}) collective-permute-start(bf16[8,128,512]{2,1,0:T(8,128)(2,1)} %get-tuple-element.12), channel_id=1, source_target_pairs={{1,2},{2,1},{3,4},{4,3},{5,6},{6,5},{7,8},{8,7},{9,10},{10,9},{11,... | collective-permute-start | bytes 3145736 | tf_op jit(solution)/shard_map/ppermute | solution.py:295
  5.3 13.1 %collective-permute-start = (bf16[8,128,256]{2,1,0:T(8,128)(2,1)}, bf16[8,128,256]{2,1,0:T(8,128)(2,1)}, u32[]{:S(2)}, u32[]{:S(2)}) collective-permute-start(bf16[8,128,256]{2,1,0:T(8,128)(2,1)} %get-tuple-element.10), channel_id=1, source_target_pairs={{0,1},{1,0},{2,3},{3,2},{4,5},{5,4},{6,7},{7,6},{8,9},{9,8},{10,11... | collective-permute-start | bytes 1572872 | tf_op jit(solution)/shard_map/ppermute | solution.py:296
  9.5 1.5 %copy-start.4 = (s32[2,16,2]{1,2,0:T(2,128)S(1)}, s32[2,16,2]{1,2,0:T(2,128)}, u32[]{:S(2)}) copy-start(s32[2,16,2]{1,2,0:T(2,128)} %param.6) | copy-start | bytes 772
  9.5 8.9 %collective-permute-start.1 = (bf16[8,128,256]{2,1,0:T(8,128)(2,1)}, bf16[8,128,256]{2,1,0:T(8,128)(2,1)}, u32[]{:S(2)}, u32[]{:S(2)}) collective-permute-start(bf16[8,128,256]{2,1,0:T(8,128)(2,1)} %get-tuple-element.11), channel_id=1, source_target_pairs={{0,1},{1,0},{2,3},{3,2},{4,5},{5,4},{6,7},{7,6},{8,9},{9,8},{10,11... | collective-permute-start | bytes 1572872 | tf_op jit(solution)/shard_map/ppermute | solution.py:296
  11.1 1.9 %copy-start.2 = (bf16[2,16,3,128,128]{4,3,2,1,0:T(8,128)(2,1)S(1)}, bf16[2,16,3,128,128]{4,3,2,1,0:T(8,128)(2,1)}, u32[]{:S(2)}) copy-start(bf16[2,16,3,128,128]{4,3,2,1,0:T(8,128)(2,1)} %blocks_ref.3) | copy-start | bytes 9437188
  13.0 5.4 %copy-start.1 = (bf16[16,128,512]{2,1,0:T(8,128)(2,1)S(1)}, bf16[16,128,512]{2,1,0:T(8,128)(2,1)}, u32[]{:S(2)}) copy-start(bf16[16,128,512]{2,1,0:T(8,128)(2,1)} %copy-done) | copy-start | bytes 6291460
  13.0 5.4 %copy-start.3 = (bf16[2,16,3,128,128]{4,3,2,1,0:T(8,128)(2,1)S(1)}, bf16[2,16,3,128,128]{4,3,2,1,0:T(8,128)(2,1)}, u32[]{:S(2)}) copy-start(bf16[2,16,3,128,128]{4,3,2,1,0:T(8,128)(2,1)} %blocks_ref.3) | copy-start | bytes 9437188
  25.8 7.6 %collective-permute-start.3 = (bf16[256,1024]{1,0:T(8,128)(2,1)S(1)}, bf16[256,1024]{1,0:T(8,128)(2,1)S(1)}, u32[]{:S(2)}, u32[]{:S(2)}) collective-permute-start(bf16[256,1024]{1,0:T(8,128)(2,1)S(1)} %shard_map.52), channel_id=1, source_target_pairs={{0,1},{1,0},{2,3},{3,2},{4,5},{5,4},{6,7},{7,6},{8,9},{9,8},{10,11... | collective-permute-start | bytes 1572872 | tf_op jit(solution)/shard_map/ppermute | solution.py:302

commit v8 on v4

--- a/solution.py
+++ b/solution.py
@@ -35,70 +35,40 @@
     return [(0, width)] if half % LANES else [(0, half), (half, half)]
 
 
-def pick_far(own, sends):
+def pick_blocks(own, sends):
     count, size, width = own.shape
     halo = sends.shape[1] // 2
-
-    def kernel(sends_hbm, own_hbm, own_ref, far_ref, sends_ref, list_sem, sems):
-        lists = pltpu.make_async_copy(sends_hbm, sends_ref, list_sem)
+    ranges = halves(width)
+
+    def kernel(sends_hbm, own_hbm, own_ref, *refs):
+        far_refs, near_refs = refs[: len(ranges)], refs[len(ranges) : 2 * len(ranges)]
+        sends_ref, sems = refs[2 * len(ranges) :]
+        lists = pltpu.make_async_copy(sends_hbm, sends_ref, sems.at[0])
+        load = pltpu.make_async_copy(own_hbm, own_ref, sems.at[1])
         lists.start()
-        loads = [
-            pltpu.make_async_copy(own_hbm.at[block], own_ref.at[block], sems.at[block])
-            for block in range(count)
-        ]
-        for load in loads:
-            load.start()
+        load.start()
         lists.wait()
-        for load in loads:
-            load.wait()
-        first = lax.rem(lax.axis_index(AXIS), 2) * halo
-        for place in range(halo):
-            far_ref[place] = own_ref[sends_ref[0, first + place]]
-
-    return pl.pallas_call(
-        kernel,
-        out_shape=(
-            jax.ShapeDtypeStruct(own.shape, own.dtype),
-            jax.ShapeDtypeStruct((halo, size, width), own.dtype),
-        ),
+        load.wait()
+        odd = lax.rem(lax.axis_index(AXIS), 2)
+        for which, out_refs in ((odd, far_refs), (1 - odd, near_refs)):
+            for place in range(halo):
+                block = sends_ref[0, which * halo + place]
+                for part, out_ref in zip(ranges, out_refs):
+                    out_ref[place] = own_ref[block, :, pl.ds(*part)]
+
+    return pl.pallas_call(
+        kernel,
+        out_shape=[jax.ShapeDtypeStruct(own.shape, own.dtype)]
+        + [jax.ShapeDtypeStruct((halo, size, span), own.dtype) for _, span in ranges] * 2,
         in_specs=[pl.BlockSpec(memory_space=pltpu.HBM)] * 2,
-        out_specs=(VMEM,) * 2,
-        scratch_shapes=[
-            pltpu.SMEM(sends.shape, sends.dtype),
-            pltpu.SemaphoreType.DMA(()),
-            pltpu.SemaphoreType.DMA((count,)),
-        ],
-        compiler_params=PARAMETERS,
-        cost_estimate=cost(0, 5 * own.size),
+        out_specs=[VMEM] * (1 + 2 * len(ranges)),
+        scratch_shapes=[pltpu.SMEM(sends.shape, sends.dtype), pltpu.SemaphoreType.DMA((2,))],
+        compiler_params=PARAMETERS,
+        cost_estimate=cost(0, 6 * own.size),
     )(
         pltpu.with_memory_space_constraint(sends, pltpu.HBM),
         pltpu.with_memory_space_constraint(own, pltpu.HBM),
     )
-
-
-def pick_near(own, sends):
-    _, size, width = own.shape
-    halo = sends.shape[1] // 2
-    ranges = halves(width)
-
-    def kernel(sends_hbm, own_ref, *refs):
-        near_refs, sends_ref = refs[:-1], refs[-1]
-        pltpu.sync_copy(sends_hbm, sends_ref)
-        first = (1 - lax.rem(lax.axis_index(AXIS), 2)) * halo
-        for place in range(halo):
-            block = sends_ref[0, first + place]
-            for part, near_ref in zip(ranges, near_refs):
-                near_ref[place] = own_ref[block, :, pl.ds(*part)]
-
-    return pl.pallas_call(
-        kernel,
-        out_shape=[jax.ShapeDtypeStruct((halo, size, span), own.dtype) for _, span in ranges],
-        in_specs=[pl.BlockSpec(memory_space=pltpu.HBM), VMEM],
-        out_specs=[VMEM] * len(ranges),
-        scratch_shapes=[pltpu.SMEM(sends.shape, sends.dtype)],
-        compiler_params=PARAMETERS,
-        cost_estimate=cost(0, 2 * own.size),
-    )(pltpu.with_memory_space_constraint(sends, pltpu.HBM), own)
 
 
 def transposed(own, devices):
@@ -239,7 +209,7 @@
     )(columns, turned, own, blocks, *nears)
 
 
-def with_far(local, folds, far, mine):
+def with_far(local, folds, far, mine, start):
     params, width, depth = folds.shape
     half, span = width // 2, far.shape[2]
 
@@ -248,7 +218,7 @@
         rows = pl.ds(pl.multiple_of((odd if mine else 1 - odd) * half, half), half)
         right = far_ref[...].reshape(depth, span)
         for param in range(params):
-            total = local_ref[param, rows] + jnp.dot(
+            total = local_ref[param, rows, pl.ds(start, span)] + jnp.dot(
                 folds_ref[param, rows], right, preferred_element_type=jnp.float32
             )
             out_ref[:, pl.ds(param * span, span)] = total.astype(out_ref.dtype)
@@ -267,13 +237,22 @@
     )(local, folds, far)
 
 
-def add_chips(parts):
+def add_chips(parts, params):
+    _, rows, columns = parts.shape
+    width = columns // params
+    ranges = halves(width)
+
     def kernel(parts_ref, out_ref):
-        out_ref[...] = jnp.sum(parts_ref[...].astype(jnp.float32), axis=0)
-
-    return pl.pallas_call(
-        kernel,
-        out_shape=jax.ShapeDtypeStruct(parts.shape[1:], jnp.float32),
+        total = jnp.sum(parts_ref[...].astype(jnp.float32), axis=0)
+        at = 0
+        for start, span in ranges:
+            for param in range(params):
+                out_ref[:, pl.ds(param * width + start, span)] = total[:, at : at + span]
+                at += span
+
+    return pl.pallas_call(
+        kernel,
+        out_shape=jax.ShapeDtypeStruct((rows, columns), jnp.float32),
         in_specs=[VMEM],
         out_specs=VMEM,
         compiler_params=PARAMETERS,
@@ -289,23 +268,28 @@
     chips = devices // 2
     near_pairs, far_pairs = pairs(devices, 0), pairs(devices, 1)
 
-    own, far = pick_far(basis.reshape(count, size, width), sends)
-    far = lax.ppermute(far, AXIS, far_pairs)
-    nears = [lax.ppermute(near, AXIS, near_pairs) for near in pick_near(own, sends)]
+    ranges = halves(width)
+    own, *listed = pick_blocks(basis.reshape(count, size, width), sends)
+    fars = [lax.ppermute(far, AXIS, far_pairs) for far in listed[: len(ranges)]]
+    nears = [lax.ppermute(near, AXIS, near_pairs) for near in listed[len(ranges) :]]
 
     turned = transposed(own, devices)
     folds = fold_far(turned, blocks, columns, halo)
     local = local_parts(turned, own, nears, blocks, columns)
 
-    taken = lax.ppermute(with_far(local, folds, far, False), AXIS, near_pairs)
-    keep = with_far(local, folds, far, True)
+    taken, keep = [], []
+    for (start, _), far in zip(ranges, fars):
+        give = with_far(local, folds, far, False, start)
+        taken.append(lax.ppermute(give, AXIS, near_pairs))
+        keep.append(with_far(local, folds, far, True, start))
+    taken, keep = jnp.concatenate(taken, axis=1), jnp.concatenate(keep, axis=1)
     chip_sum = (keep + taken.astype(jnp.float32)).astype(jnp.bfloat16)
     parts = lax.all_to_all(
         chip_sum.reshape(chips, width // devices, params * width), AXIS,
         split_axis=0, concat_axis=0, tiled=True,
         axis_index_groups=[[2 * chip + core for chip in chip_order(chips)] for core in range(2)],
     )
-    return add_chips(parts)
+    return add_chips(parts, params)
 
 
 def solution(mesh):

time: 53.5 us -> 53.7 us (level)
  starting transfers between devices: 11.7 us -> 14.7 us
  local copies, waits for them, and re-layouts: 1.99 us -> 0.49 us
  Pallas kernels: 19.4 us -> 18.7 us
  waiting for transfers between devices: 0.83 us -> 0.28 us
    ppermute x2 -> x4, starting transfers between devices: 7.49 us -> 14.1 us  [the longest x2 12.7 us: shards(): taken.append(lax.ppermute(give, AXIS, near_pairs))]
    ppermute x2, starting transfers between devices: 4.24 us -> 0.6 us  [shards(): lax.ppermute(near, AXIS, near_pairs)]
    unnamed x11 -> x5, local copies, waits for them, and re-layouts: 1.99 us -> 0.49 us
    pallas_call x3 -> x2, Pallas kernels: 5.23 us -> 3.82 us  [the longest x1 3.1 us: pick_blocks(): pl.pallas_call(kernel, out_shape=[jax.ShapeDtypeStruct(own.shape, own.dty...]
    ppermute x2 -> x4, waiting for transfers between devices: 0.83 us -> 0.28 us  [the longest x2 0.27 us: shards(): taken.append(lax.ppermute(give, AXIS, near_pairs))]
    pallas_call x2 -> x4, Pallas kernels: 1.41 us -> 1.74 us  [with_far(): pl.pallas_call(kernel, out_shape=jax.ShapeDtypeStruct((half, columns), jn...]
  transfers between devices with their start and end apart: 4 -> 6, of which waited for: 1 -> 1; matrix products, arithmetic and copies ran while one was open for 0% -> 0% of each run, Pallas kernels for 29% -> 28%
where the time goes in v8:
time: 53.7 us; the launch traced here: 53.5 us
  blocking collectives  19 us (35%)
  Pallas kernels  18.7 us (35%)
  starting transfers between devices  14.7 us (27%)
    all_to_all x1, blocking collectives, shards(): lax.all_to_all(chip_sum.reshape(chips, width // devices, params * width),...  19 us
    ppermute x2, starting transfers between devices, shards(): taken.append(lax.ppermute(give, AXIS, near_pairs))  12.7 us
    pallas_call x1, Pallas kernels, local_parts(): pl.pallas_call(kernel, out_shape=jax.ShapeDtypeStruct((params, width, wid...  6.61 us
    pallas_call x1, Pallas kernels, fold_far(): pl.pallas_call(kernel, out_shape=jax.ShapeDtypeStruct(shape, turned.dtype...  5.05 us
    pallas_call x1, Pallas kernels, pick_blocks(): pl.pallas_call(kernel, out_shape=[jax.ShapeDtypeStruct(own.shape, own.dty...  3.1 us
    pallas_call x4, Pallas kernels, with_far(): pl.pallas_call(kernel, out_shape=jax.ShapeDtypeStruct((half, columns), jn...  1.74 us
    pallas_call x1, Pallas kernels, transposed(): pl.pallas_call(kernel, out_shape=jax.ShapeDtypeStruct((width, count * siz...  1.48 us
    ppermute x2, starting transfers between devices, shards(): fars = [lax.ppermute(far, AXIS, far_pairs) for far in listed[:len(ranges)]]  1.38 us
  transfers between devices with their start and end apart: 6, of which 1 were waited for; matrix products, arithmetic and copies ran while one was open for 0% of the time, Pallas kernels for 28%

profile of v8, /device:TPU:0, one launch (start us, length us, event | category | flops | bytes accessed | tf_op | source)
XLA Modules:
  0.0 53.5 jit_solution(14692977466012517008)
XLA Ops:
  0.0 0.0 copy-start.1
  0.0 3.1 %shard_map.46 = (bf16[16,128,512]{2,1,0:T(8,128)(2,1)S(1)}, bf16[8,128,256]{2,1,0:T(8,128)(2,1)}, bf16[8,128,256]{2,1,0:T(8,128)(2,1)}, bf16[8,128,256]{2,1,0:T(8,128)(2,1)}, bf16[8,128,256]{2,1,0:T(8,128)(2,1)}) custom-call(s32[1,16]{1,0:T(1,128)} %sends_hbm.1, bf16[16,128,512]{2,1,0:T(8,128)(2,1)} %bitcast.7), custom_call_target="tpu_custom_call" | custom-call | bytes 786432 | tf_op jit(solution)/shard_map/pallas_call | solution.py:59
  3.1 0.5 collective-permute-start
  3.6 0.1 collective-permute-start.1
  3.7 0.7 %collective-permute-start.2 = (bf16[8,128,256]{2,1,0:T(8,128)(2,1)}, bf16[8,128,256]{2,1,0:T(8,128)(2,1)S(1)}, u32[]{:S(2)}, u32[]{:S(2)}) collective-permute-start(bf16[8,128,256]{2,1,0:T(8,128)(2,1)} %get-tuple-element.13), channel_id=1, source_target_pairs={{1,2},{2,1},{3,4},{4,3},{5,6},{6,5},{7,8},{8,7},{9,10},{10,9},{11,... | collective-permute-start | bytes 1572872 | tf_op jit(solution)/shard_map/ppermute | solution.py:273
  4.4 0.7 %collective-permute-start.3 = (bf16[8,128,256]{2,1,0:T(8,128)(2,1)}, bf16[8,128,256]{2,1,0:T(8,128)(2,1)S(1)}, u32[]{:S(2)}, u32[]{:S(2)}) collective-permute-start(bf16[8,128,256]{2,1,0:T(8,128)(2,1)} %get-tuple-element.14), channel_id=1, source_target_pairs={{1,2},{2,1},{3,4},{4,3},{5,6},{6,5},{7,8},{8,7},{9,10},{10,9},{11,... | collective-permute-start | bytes 1572872 | tf_op jit(solution)/shard_map/ppermute | solution.py:273
  5.1 0.0 copy-done.1
  5.1 0.1 copy.5.columns_ref
  5.2 0.0 copy-start
  5.2 1.5 %shard_map.47.turned_ref = bf16[512,2048]{1,0:T(8,128)(2,1)S(1)} custom-call(bf16[16,128,512]{2,1,0:T(8,128)(2,1)S(1)} %get-tuple-element.10.own_ref), custom_call_target="tpu_custom_call" | custom-call | bytes 524288 | tf_op jit(solution)/shard_map/pallas_call | solution.py:94
  6.7 0.4 copy-done
  7.1 5.0 %shard_map.49.folds_ref = bf16[2,512,1024]{2,1,0:T(8,128)(2,1)S(1)} custom-call(s32[2,16,2]{2,1,0:T(8,128)S(1)} %copy.5.columns_ref, bf16[512,2048]{1,0:T(8,128)(2,1)S(1)} %shard_map.47.turned_ref, bf16[2,16,3,128,128]{4,3,2,1,0:T(8,128)(2,1)S(1)} %copy-done), custom_call_target="tpu_custom_call" | custom-call | flops 67108864 | bytes 655360 | tf_op jit(solution)/shard_map/pallas_call | solution.py:143
  12.1 0.0 collective-permute-done.refs_0_
  12.2 0.0 collective-permute-done.1.refs_1_
  12.2 6.6 %shard_map.48.local_ref = f32[2,512,512]{2,1,0:T(8,128)S(1)} custom-call(s32[2,16,2]{2,1,0:T(8,128)S(1)} %copy.5.columns_ref, bf16[512,2048]{1,0:T(8,128)(2,1)S(1)} %shard_map.47.turned_ref, bf16[16,128,512]{2,1,0:T(8,128)(2,1)S(1)} %get-tuple-element.10.own_ref, bf16[2,16,3,128,128]{4,3,2,1,0:T(8,128)(2,1)S(1)} %copy-done, ...), custom_call_target="tpu_custom_call" | custom-call | flops 469762048 | bytes 1441792 | tf_op jit(solution)/shard_map/pallas_call | solution.py:195
  18.8 0.0 collective-permute-done.2.far_ref
  18.8 0.4 shard_map.52
  19.2 7.6 %collective-permute-start.4 = (bf16[256,512]{1,0:T(8,128)(2,1)S(1)}, bf16[256,512]{1,0:T(8,128)(2,1)S(1)}, u32[]{:S(2)}, u32[]{:S(2)}) collective-permute-start(bf16[256,512]{1,0:T(8,128)(2,1)S(1)} %shard_map.52), channel_id=1, source_target_pairs={{0,1},{1,0},{2,3},{3,2},{4,5},{5,4},{6,7},{7,6},{8,9},{9,8},{10,11... | collective-permute-start | bytes 786440 | tf_op jit(solution)/shard_map/ppermute | solution.py:283
  26.8 0.0 collective-permute-done.3.far_ref
  26.8 0.4 shard_map.53
  27.2 5.2 %collective-permute-start.5 = (bf16[256,512]{1,0:T(8,128)(2,1)S(1)}, bf16[256,512]{1,0:T(8,128)(2,1)S(1)}, u32[]{:S(2)}, u32[]{:S(2)}) collective-permute-start(bf16[256,512]{1,0:T(8,128)(2,1)S(1)} %shard_map.53), channel_id=1, source_target_pairs={{0,1},{1,0},{2,3},{3,2},{4,5},{5,4},{6,7},{7,6},{8,9},{9,8},{10,11... | collective-permute-start | bytes 786440 | tf_op jit(solution)/shard_map/ppermute | solution.py:283
  32.4 0.4 shard_map.51
  32.9 0.4 shard_map.50
  33.3 0.0 collective-permute-done.4
  33.3 0.3 collective-permute-done.5
  33.6 0.1 fusion
  33.7 19.0 %all_to_all.5.parts_ref = bf16[8,32,1024]{2,1,0:T(8,128)(2,1)S(1)} all-to-all(bf16[8,32,1024]{2,1,0:T(8,128)(2,1)S(1)} %fusion), channel_id=1, replica_groups={{14,0,12,2,10,4,8,6},{15,1,13,3,11,5,9,7},{30,16,28,18,26,20,24,22},{31..., dimensions={0} | all-to-all | bytes 1048576 | tf_op jit(solution)/shard_map/all_to_all | solution.py:287
  52.7 0.7 %shard_map.54 = f32[32,1024]{1,0:T(8,128)} custom-call(bf16[8,32,1024]{2,1,0:T(8,128)(2,1)S(1)} %all_to_all.5.parts_ref), custom_call_target="tpu_custom_call" | custom-call | bytes 65536 | tf_op jit(solution)/shard_map/pallas_call | solution.py:253
Async XLA Ops:
  0.0 5.1 %copy-start.1 = (s32[2,16,2]{1,2,0:T(2,128)S(1)}, s32[2,16,2]{1,2,0:T(2,128)}, u32[]{:S(2)}) copy-start(s32[2,16,2]{1,2,0:T(2,128)} %param.6) | copy-start | bytes 772
  3.1 9.0 %collective-permute-start = (bf16[8,128,256]{2,1,0:T(8,128)(2,1)}, bf16[8,128,256]{2,1,0:T(8,128)(2,1)}, u32[]{:S(2)}, u32[]{:S(2)}) collective-permute-start(bf16[8,128,256]{2,1,0:T(8,128)(2,1)} %get-tuple-element.11), channel_id=1, source_target_pairs={{0,1},{1,0},{2,3},{3,2},{4,5},{5,4},{6,7},{7,6},{8,9},{9,8},{10,11... | collective-permute-start | bytes 1572872 | tf_op jit(solution)/shard_map/ppermute | solution.py:274
  3.6 8.5 %collective-permute-start.1 = (bf16[8,128,256]{2,1,0:T(8,128)(2,1)}, bf16[8,128,256]{2,1,0:T(8,128)(2,1)}, u32[]{:S(2)}, u32[]{:S(2)}) collective-permute-start(bf16[8,128,256]{2,1,0:T(8,128)(2,1)} %get-tuple-element.12), channel_id=1, source_target_pairs={{0,1},{1,0},{2,3},{3,2},{4,5},{5,4},{6,7},{7,6},{8,9},{9,8},{10,11... | collective-permute-start | bytes 1572872 | tf_op jit(solution)/shard_map/ppermute | solution.py:274
  3.7 15.1 %collective-permute-start.2 = (bf16[8,128,256]{2,1,0:T(8,128)(2,1)}, bf16[8,128,256]{2,1,0:T(8,128)(2,1)S(1)}, u32[]{:S(2)}, u32[]{:S(2)}) collective-permute-start(bf16[8,128,256]{2,1,0:T(8,128)(2,1)} %get-tuple-element.13), channel_id=1, source_target_pairs={{1,2},{2,1},{3,4},{4,3},{5,6},{6,5},{7,8},{8,7},{9,10},{10,9},{11,... | collective-permute-start | bytes 1572872 | tf_op jit(solution)/shard_map/ppermute | solution.py:273
  4.4 22.4 %collective-permute-start.3 = (bf16[8,128,256]{2,1,0:T(8,128)(2,1)}, bf16[8,128,256]{2,1,0:T(8,128)(2,1)S(1)}, u32[]{:S(2)}, u32[]{:S(2)}) collective-permute-start(bf16[8,128,256]{2,1,0:T(8,128)(2,1)} %get-tuple-element.14), channel_id=1, source_target_pairs={{1,2},{2,1},{3,4},{4,3},{5,6},{6,5},{7,8},{8,7},{9,10},{10,9},{11,... | collective-permute-start | bytes 1572872 | tf_op jit(solution)/shard_map/ppermute | solution.py:273
  5.2 1.9 %copy-start = (bf16[2,16,3,128,128]{4,3,2,1,0:T(8,128)(2,1)S(1)}, bf16[2,16,3,128,128]{4,3,2,1,0:T(8,128)(2,1)}, u32[]{:S(2)}) copy-start(bf16[2,16,3,128,128]{4,3,2,1,0:T(8,128)(2,1)} %blocks_ref.3) | copy-start | bytes 9437188
  19.2 14.1 %collective-permute-start.4 = (bf16[256,512]{1,0:T(8,128)(2,1)S(1)}, bf16[256,512]{1,0:T(8,128)(2,1)S(1)}, u32[]{:S(2)}, u32[]{:S(2)}) collective-permute-start(bf16[256,512]{1,0:T(8,128)(2,1)S(1)} %shard_map.52), channel_id=1, source_target_pairs={{0,1},{1,0},{2,3},{3,2},{4,5},{5,4},{6,7},{7,6},{8,9},{9,8},{10,11... | collective-permute-start | bytes 786440 | tf_op jit(solution)/shard_map/ppermute | solution.py:283
  27.2 6.3 %collective-permute-start.5 = (bf16[256,512]{1,0:T(8,128)(2,1)S(1)}, bf16[256,512]{1,0:T(8,128)(2,1)S(1)}, u32[]{:S(2)}, u32[]{:S(2)}) collective-permute-start(bf16[256,512]{1,0:T(8,128)(2,1)S(1)} %shard_map.53), channel_id=1, source_target_pairs={{0,1},{1,0},{2,3},{3,2},{4,5},{5,4},{6,7},{7,6},{8,9},{9,8},{10,11... | collective-permute-start | bytes 786440 | tf_op jit(solution)/shard_map/ppermute | solution.py:283

commit v9 on v3

--- a/solution.py
+++ b/solution.py
@@ -26,7 +26,9 @@
 
 
 def chip_order(chips):
-    return list(range(chips - 1, -1, -1))
+    high = [(chips - 1 - place) ^ 1 for place in range(chips)]
+    order = [chip for pair in zip(high, range(chips)) for chip in pair][:chips]
+    return order if len(set(order)) == chips else list(range(chips))
 
 
 def halves(width):
@@ -38,18 +40,13 @@
     count, size, width = own.shape
     halo = sends.shape[1] // 2
 
-    def kernel(sends_hbm, own_hbm, own_ref, far_ref, sends_ref, list_sem, sems):
+    def kernel(sends_hbm, own_hbm, own_ref, far_ref, sends_ref, list_sem, load_sem):
         lists = pltpu.make_async_copy(sends_hbm, sends_ref, list_sem)
         lists.start()
-        loads = [
-            pltpu.make_async_copy(own_hbm.at[block], own_ref.at[block], sems.at[block])
-            for block in range(count)
-        ]
-        for load in loads:
-            load.start()
+        load = pltpu.make_async_copy(own_hbm, own_ref, load_sem)
+        load.start()
         lists.wait()
-        for load in loads:
-            load.wait()
+        load.wait()
         first = lax.rem(lax.axis_index(AXIS), 2) * halo
         for place in range(halo):
             far_ref[place] = own_ref[sends_ref[0, first + place]]
@@ -65,7 +62,7 @@
         scratch_shapes=[
             pltpu.SMEM(sends.shape, sends.dtype),
             pltpu.SemaphoreType.DMA(()),
-            pltpu.SemaphoreType.DMA((count,)),
+            pltpu.SemaphoreType.DMA(()),
         ],
         compiler_params=PARAMETERS,
         cost_estimate=cost(0, 5 * own.size),

time: 54.1 us -> 53.8 us (level)
  starting transfers between devices: 12.6 us -> 11.4 us
  Pallas kernels: 18.6 us -> 19.6 us
    ppermute x1, starting transfers between devices: 7.63 us -> 6.41 us  [shards(): taken = lax.ppermute(with_far(local, folds, far, False), AXIS, near_pairs)]
    pallas_call x1, Pallas kernels: 3.83 us -> 5.05 us  [fold_far(): pl.pallas_call(kernel, out_shape=jax.ShapeDtypeStruct(shape, turned.dtype...]
  transfers between devices with their start and end apart: 4 -> 4, of which waited for: 1 -> 1; matrix products, arithmetic and copies ran while one was open for 0% -> 0% of each run, Pallas kernels for 27% -> 29%
where the time goes in v9:
time: 53.8 us; the launch traced here: 53.6 us
  Pallas kernels  19.6 us (36%)
  blocking collectives  19.5 us (36%)
  starting transfers between devices  11.4 us (21%)
  local copies, waits for them, and re-layouts  1.99 us (4%)
  waiting for transfers between devices  0.83 us (2%)
    all_to_all x1, blocking collectives, shards(): lax.all_to_all(chip_sum.reshape(chips, width // devices, params * width),...  19.5 us
    pallas_call x1, Pallas kernels, local_parts(): pl.pallas_call(kernel, out_shape=jax.ShapeDtypeStruct((params, width, wid...  6.62 us
    ppermute x1, starting transfers between devices, shards(): taken = lax.ppermute(with_far(local, folds, far, False), AXIS, near_pairs)  6.41 us
    pallas_call x1, Pallas kernels, fold_far(): pl.pallas_call(kernel, out_shape=jax.ShapeDtypeStruct(shape, turned.dtype...  5.05 us
    ppermute x2, starting transfers between devices, shards(): lax.ppermute(near, AXIS, near_pairs)  4.24 us
    pallas_call x1, Pallas kernels, pick_far(): pl.pallas_call(kernel, out_shape=(jax.ShapeDtypeStruct(own.shape, own.dty...  2.66 us
    unnamed x11, local copies, waits for them, and re-layouts  1.99 us
    pallas_call x1, Pallas kernels, pick_near(): pl.pallas_call(kernel, out_shape=[jax.ShapeDtypeStruct((halo, size, span)...  1.71 us
  transfers between devices with their start and end apart: 4, of which 1 were waited for; matrix products, arithmetic and copies ran while one was open for 0% of the time, Pallas kernels for 29%

profile of v9, /device:TPU:0, one launch (start us, length us, event | category | flops | bytes accessed | tf_op | source)
XLA Modules:
  0.0 53.6 jit_solution(16390273874179516413)
XLA Ops:
  0.0 2.7 %shard_map.46 = (bf16[16,128,512]{2,1,0:T(8,128)(2,1)S(1)}, bf16[8,128,512]{2,1,0:T(8,128)(2,1)}) custom-call(s32[1,16]{1,0:T(1,128)} %sends_hbm.3, bf16[16,128,512]{2,1,0:T(8,128)(2,1)} %bitcast.2), custom_call_target="tpu_custom_call" | custom-call | bytes 655360 | tf_op jit(solution)/shard_map/pallas_call | solution.py:54
  2.7 0.0 copy-start
  2.7 0.7 %collective-permute-start.2 = (bf16[8,128,512]{2,1,0:T(8,128)(2,1)}, bf16[8,128,512]{2,1,0:T(8,128)(2,1)S(1)}, u32[]{:S(2)}, u32[]{:S(2)}) collective-permute-start(bf16[8,128,512]{2,1,0:T(8,128)(2,1)} %get-tuple-element.12), channel_id=1, source_target_pairs={{1,2},{2,1},{3,4},{4,3},{5,6},{6,5},{7,8},{8,7},{9,10},{10,9},{11,... | collective-permute-start | bytes 3145736 | tf_op jit(solution)/shard_map/ppermute | solution.py:289
  3.4 1.7 %shard_map.48 = (bf16[8,128,256]{2,1,0:T(8,128)(2,1)}, bf16[8,128,256]{2,1,0:T(8,128)(2,1)}) custom-call(s32[1,16]{1,0:T(1,128)} %sends_hbm.3, bf16[16,128,512]{2,1,0:T(8,128)(2,1)S(1)} %get-tuple-element.9.own_ref), custom_call_target="tpu_custom_call" | custom-call | bytes 262144 | tf_op jit(solution)/shard_map/pallas_call | solution.py:89
  5.1 4.2 %collective-permute-start = (bf16[8,128,256]{2,1,0:T(8,128)(2,1)}, bf16[8,128,256]{2,1,0:T(8,128)(2,1)}, u32[]{:S(2)}, u32[]{:S(2)}) collective-permute-start(bf16[8,128,256]{2,1,0:T(8,128)(2,1)} %get-tuple-element.10), channel_id=1, source_target_pairs={{0,1},{1,0},{2,3},{3,2},{4,5},{5,4},{6,7},{7,6},{8,9},{9,8},{10,11... | collective-permute-start | bytes 1572872 | tf_op jit(solution)/shard_map/ppermute | solution.py:290
  9.4 0.0 copy-start.4
  9.4 0.0 collective-permute-start.1
  9.4 0.0 copy-done
  9.4 1.5 %shard_map.47.turned_ref = bf16[512,2048]{1,0:T(8,128)(2,1)S(1)} custom-call(bf16[16,128,512]{2,1,0:T(8,128)(2,1)S(1)} %get-tuple-element.9.own_ref), custom_call_target="tpu_custom_call" | custom-call | bytes 524288 | tf_op jit(solution)/shard_map/pallas_call | solution.py:120
  10.9 0.0 copy-done.4
  10.9 0.1 copy.5.columns_ref
  11.0 0.0 copy-start.2
  11.0 1.9 %copy-done.2 = bf16[2,16,3,128,128]{4,3,2,1,0:T(8,128)(2,1)S(1)} copy-done((bf16[2,16,3,128,128]{4,3,2,1,0:T(8,128)(2,1)S(1)}, bf16[2,16,3,128,128]{4,3,2,1,0:T(8,128)(2,1)}, u32[]{:S(2)}) %copy-start.2) | copy-done | bytes 3145752
  12.8 0.0 copy-start.1
  12.9 0.0 copy-start.3
  12.9 5.0 %shard_map.50.folds_ref = bf16[2,512,1024]{2,1,0:T(8,128)(2,1)S(1)} custom-call(s32[2,16,2]{2,1,0:T(8,128)S(1)} %copy.5.columns_ref, bf16[512,2048]{1,0:T(8,128)(2,1)S(1)} %shard_map.47.turned_ref, bf16[2,16,3,128,128]{4,3,2,1,0:T(8,128)(2,1)S(1)} %copy-done.2), custom_call_target="tpu_custom_call" | custom-call | flops 67108864 | bytes 655360 | tf_op jit(solution)/shard_map/pallas_call | solution.py:169
  17.9 0.0 collective-permute-done.refs_0_
  17.9 0.0 collective-permute-done.1.refs_1_
  17.9 0.0 copy-done.1
  17.9 0.0 copy-done.3
  17.9 6.6 %shard_map.49.local_ref = f32[2,512,512]{2,1,0:T(8,128)S(1)} custom-call(s32[2,16,2]{2,1,0:T(8,128)S(1)} %copy.5.columns_ref, bf16[512,2048]{1,0:T(8,128)(2,1)S(1)} %shard_map.47.turned_ref, bf16[16,128,512]{2,1,0:T(8,128)(2,1)S(1)} %copy-done.1, bf16[2,16,3,128,128]{4,3,2,1,0:T(8,128)(2,1)S(1)} %copy-done.3, ...), custom_call_target="tpu_custom_call" | custom-call | flops 469762048 | bytes 1441792 | tf_op jit(solution)/shard_map/pallas_call | solution.py:221
  24.6 0.0 collective-permute-done.2.far_ref
  24.6 0.7 %shard_map.52 = bf16[256,1024]{1,0:T(8,128)(2,1)S(1)} custom-call(f32[2,512,512]{2,1,0:T(8,128)S(1)} %shard_map.49.local_ref, bf16[2,512,1024]{2,1,0:T(8,128)(2,1)S(1)} %shard_map.50.folds_ref, bf16[8,128,512]{2,1,0:T(8,128)(2,1)S(1)} %collective-permute-done.2.far_ref), custom_call_target="tpu_custom_call" | custom-call | flops 67108864 | bytes 393216 | tf_op jit(solution)/shard_map/pallas_call | solution.py:253
  25.3 6.4 %collective-permute-start.3 = (bf16[256,1024]{1,0:T(8,128)(2,1)S(1)}, bf16[256,1024]{1,0:T(8,128)(2,1)S(1)}, u32[]{:S(2)}, u32[]{:S(2)}) collective-permute-start(bf16[256,1024]{1,0:T(8,128)(2,1)S(1)} %shard_map.52), channel_id=1, source_target_pairs={{0,1},{1,0},{2,3},{3,2},{4,5},{5,4},{6,7},{7,6},{8,9},{9,8},{10,11... | collective-permute-start | bytes 1572872 | tf_op jit(solution)/shard_map/ppermute | solution.py:296
  31.7 0.7 %shard_map.51 = f32[256,1024]{1,0:T(8,128)S(1)} custom-call(f32[2,512,512]{2,1,0:T(8,128)S(1)} %shard_map.49.local_ref, bf16[2,512,1024]{2,1,0:T(8,128)(2,1)S(1)} %shard_map.50.folds_ref, bf16[8,128,512]{2,1,0:T(8,128)(2,1)S(1)} %collective-permute-done.2.far_ref), custom_call_target="tpu_custom_call" | custom-call | flops 67108864 | bytes 393216 | tf_op jit(solution)/shard_map/pallas_call | solution.py:253
  32.4 0.8 %collective-permute-done.3 = bf16[256,1024]{1,0:T(8,128)(2,1)S(1)} collective-permute-done((bf16[256,1024]{1,0:T(8,128)(2,1)S(1)}, bf16[256,1024]{1,0:T(8,128)(2,1)S(1)}, u32[]{:S(2)}, u32[]{:S(2)}) %collective-permute-start.3) | collective-permute-done | bytes 524320 | tf_op jit(solution)/shard_map/ppermute | solution.py:296
  33.2 0.1 add_convert_fusion
  33.4 19.5 %all_to_all.5.parts_ref = bf16[8,32,1024]{2,1,0:T(8,128)(2,1)S(1)} all-to-all(bf16[8,32,1024]{2,1,0:T(8,128)(2,1)S(1)} %bitcast.3), channel_id=1, replica_groups={{12,0,14,2,8,4,10,6},{13,1,15,3,9,5,11,7},{28,16,30,18,24,20,26,22},{29..., dimensions={0} | all-to-all | bytes 1048576 | tf_op jit(solution)/shard_map/all_to_all | solution.py:299
  52.9 0.7 %shard_map.53 = f32[32,1024]{1,0:T(8,128)} custom-call(bf16[8,32,1024]{2,1,0:T(8,128)(2,1)S(1)} %all_to_all.5.parts_ref), custom_call_target="tpu_custom_call" | custom-call | bytes 65536 | tf_op jit(solution)/shard_map/pallas_call | solution.py:270
Async XLA Ops:
  2.7 6.7 %copy-start = (bf16[16,128,512]{2,1,0:T(8,128)(2,1)}, bf16[16,128,512]{2,1,0:T(8,128)(2,1)S(1)}, u32[]{:S(2)}) copy-start(bf16[16,128,512]{2,1,0:T(8,128)(2,1)S(1)} %get-tuple-element.9.own_ref) | copy-start | bytes 6291460
  2.7 21.9 %collective-permute-start.2 = (bf16[8,128,512]{2,1,0:T(8,128)(2,1)}, bf16[8,128,512]{2,1,0:T(8,128)(2,1)S(1)}, u32[]{:S(2)}, u32[]{:S(2)}) collective-permute-start(bf16[8,128,512]{2,1,0:T(8,128)(2,1)} %get-tuple-element.12), channel_id=1, source_target_pairs={{1,2},{2,1},{3,4},{4,3},{5,6},{6,5},{7,8},{8,7},{9,10},{10,9},{11,... | collective-permute-start | bytes 3145736 | tf_op jit(solution)/shard_map/ppermute | solution.py:289
  5.1 12.8 %collective-permute-start = (bf16[8,128,256]{2,1,0:T(8,128)(2,1)}, bf16[8,128,256]{2,1,0:T(8,128)(2,1)}, u32[]{:S(2)}, u32[]{:S(2)}) collective-permute-start(bf16[8,128,256]{2,1,0:T(8,128)(2,1)} %get-tuple-element.10), channel_id=1, source_target_pairs={{0,1},{1,0},{2,3},{3,2},{4,5},{5,4},{6,7},{7,6},{8,9},{9,8},{10,11... | collective-permute-start | bytes 1572872 | tf_op jit(solution)/shard_map/ppermute | solution.py:290
  9.4 1.5 %copy-start.4 = (s32[2,16,2]{1,2,0:T(2,128)S(1)}, s32[2,16,2]{1,2,0:T(2,128)}, u32[]{:S(2)}) copy-start(s32[2,16,2]{1,2,0:T(2,128)} %param.6) | copy-start | bytes 772
  9.4 8.6 %collective-permute-start.1 = (bf16[8,128,256]{2,1,0:T(8,128)(2,1)}, bf16[8,128,256]{2,1,0:T(8,128)(2,1)}, u32[]{:S(2)}, u32[]{:S(2)}) collective-permute-start(bf16[8,128,256]{2,1,0:T(8,128)(2,1)} %get-tuple-element.11), channel_id=1, source_target_pairs={{0,1},{1,0},{2,3},{3,2},{4,5},{5,4},{6,7},{7,6},{8,9},{9,8},{10,11... | collective-permute-start | bytes 1572872 | tf_op jit(solution)/shard_map/ppermute | solution.py:290
  11.0 1.9 %copy-start.2 = (bf16[2,16,3,128,128]{4,3,2,1,0:T(8,128)(2,1)S(1)}, bf16[2,16,3,128,128]{4,3,2,1,0:T(8,128)(2,1)}, u32[]{:S(2)}) copy-start(bf16[2,16,3,128,128]{4,3,2,1,0:T(8,128)(2,1)} %blocks_ref.3) | copy-start | bytes 9437188
  12.8 5.1 %copy-start.1 = (bf16[16,128,512]{2,1,0:T(8,128)(2,1)S(1)}, bf16[16,128,512]{2,1,0:T(8,128)(2,1)}, u32[]{:S(2)}) copy-start(bf16[16,128,512]{2,1,0:T(8,128)(2,1)} %copy-done) | copy-start | bytes 6291460
  12.9 5.1 %copy-start.3 = (bf16[2,16,3,128,128]{4,3,2,1,0:T(8,128)(2,1)S(1)}, bf16[2,16,3,128,128]{4,3,2,1,0:T(8,128)(2,1)}, u32[]{:S(2)}) copy-start(bf16[2,16,3,128,128]{4,3,2,1,0:T(8,128)(2,1)} %blocks_ref.3) | copy-start | bytes 9437188
  25.3 7.9 %collective-permute-start.3 = (bf16[256,1024]{1,0:T(8,128)(2,1)S(1)}, bf16[256,1024]{1,0:T(8,128)(2,1)S(1)}, u32[]{:S(2)}, u32[]{:S(2)}) collective-permute-start(bf16[256,1024]{1,0:T(8,128)(2,1)S(1)} %shard_map.52), channel_id=1, source_target_pairs={{0,1},{1,0},{2,3},{3,2},{4,5},{5,4},{6,7},{7,6},{8,9},{9,8},{10,11... | collective-permute-start | bytes 1572872 | tf_op jit(solution)/shard_map/ppermute | solution.py:296

commit v10 on v9

--- a/solution.py
+++ b/solution.py
@@ -26,9 +26,8 @@
 
 
 def chip_order(chips):
-    high = [(chips - 1 - place) ^ 1 for place in range(chips)]
-    order = [chip for pair in zip(high, range(chips)) for chip in pair][:chips]
-    return order if len(set(order)) == chips else list(range(chips))
+    ends = zip(range(chips - 1, -1, -1), range(chips))
+    return [chip for pair in ends for chip in pair][:chips]
 
 
 def halves(width):

time: 53.8 us -> 53.4 us (level)
  no operation moved by 1% of the time
where the time goes in v10:
time: 53.4 us; the launch traced here: 53.1 us
  Pallas kernels  19.3 us (36%)
  blocking collectives  19 us (36%)
  starting transfers between devices  11.7 us (22%)
  local copies, waits for them, and re-layouts  1.99 us (4%)
  waiting for transfers between devices  0.83 us (2%)
    all_to_all x1, blocking collectives, shards(): lax.all_to_all(chip_sum.reshape(chips, width // devices, params * width),...  19 us
    ppermute x1, starting transfers between devices, shards(): taken = lax.ppermute(with_far(local, folds, far, False), AXIS, near_pairs)  6.76 us
    pallas_call x1, Pallas kernels, local_parts(): pl.pallas_call(kernel, out_shape=jax.ShapeDtypeStruct((params, width, wid...  6.62 us
    pallas_call x1, Pallas kernels, fold_far(): pl.pallas_call(kernel, out_shape=jax.ShapeDtypeStruct(shape, turned.dtype...  4.7 us
    ppermute x2, starting transfers between devices, shards(): lax.ppermute(near, AXIS, near_pairs)  4.24 us
    pallas_call x1, Pallas kernels, pick_far(): pl.pallas_call(kernel, out_shape=(jax.ShapeDtypeStruct(own.shape, own.dty...  2.66 us
    unnamed x11, local copies, waits for them, and re-layouts  1.99 us
    pallas_call x1, Pallas kernels, pick_near(): pl.pallas_call(kernel, out_shape=[jax.ShapeDtypeStruct((halo, size, span)...  1.71 us
  transfers between devices with their start and end apart: 4, of which 1 were waited for; matrix products, arithmetic and copies ran while one was open for 0% of the time, Pallas kernels for 29%

profile of v10, /device:TPU:0, one launch (start us, length us, event | category | flops | bytes accessed | tf_op | source)
XLA Modules:
  0.0 53.1 jit_solution(3502030787597188640)
XLA Ops:
  0.0 2.7 %shard_map.46 = (bf16[16,128,512]{2,1,0:T(8,128)(2,1)S(1)}, bf16[8,128,512]{2,1,0:T(8,128)(2,1)}) custom-call(s32[1,16]{1,0:T(1,128)} %sends_hbm.3, bf16[16,128,512]{2,1,0:T(8,128)(2,1)} %bitcast.2), custom_call_target="tpu_custom_call" | custom-call | bytes 655360 | tf_op jit(solution)/shard_map/pallas_call | solution.py:53
  2.7 0.0 copy-start
  2.7 0.7 %collective-permute-start.2 = (bf16[8,128,512]{2,1,0:T(8,128)(2,1)}, bf16[8,128,512]{2,1,0:T(8,128)(2,1)S(1)}, u32[]{:S(2)}, u32[]{:S(2)}) collective-permute-start(bf16[8,128,512]{2,1,0:T(8,128)(2,1)} %get-tuple-element.12), channel_id=1, source_target_pairs={{1,2},{2,1},{3,4},{4,3},{5,6},{6,5},{7,8},{8,7},{9,10},{10,9},{11,... | collective-permute-start | bytes 3145736 | tf_op jit(solution)/shard_map/ppermute | solution.py:288
  3.4 1.7 %shard_map.48 = (bf16[8,128,256]{2,1,0:T(8,128)(2,1)}, bf16[8,128,256]{2,1,0:T(8,128)(2,1)}) custom-call(s32[1,16]{1,0:T(1,128)} %sends_hbm.3, bf16[16,128,512]{2,1,0:T(8,128)(2,1)S(1)} %get-tuple-element.9.own_ref), custom_call_target="tpu_custom_call" | custom-call | bytes 262144 | tf_op jit(solution)/shard_map/pallas_call | solution.py:88
  5.1 4.2 %collective-permute-start = (bf16[8,128,256]{2,1,0:T(8,128)(2,1)}, bf16[8,128,256]{2,1,0:T(8,128)(2,1)}, u32[]{:S(2)}, u32[]{:S(2)}) collective-permute-start(bf16[8,128,256]{2,1,0:T(8,128)(2,1)} %get-tuple-element.10), channel_id=1, source_target_pairs={{0,1},{1,0},{2,3},{3,2},{4,5},{5,4},{6,7},{7,6},{8,9},{9,8},{10,11... | collective-permute-start | bytes 1572872 | tf_op jit(solution)/shard_map/ppermute | solution.py:289
  9.4 0.0 copy-start.4
  9.4 0.0 collective-permute-start.1
  9.4 0.0 copy-done
  9.4 1.5 %shard_map.47.turned_ref = bf16[512,2048]{1,0:T(8,128)(2,1)S(1)} custom-call(bf16[16,128,512]{2,1,0:T(8,128)(2,1)S(1)} %get-tuple-element.9.own_ref), custom_call_target="tpu_custom_call" | custom-call | bytes 524288 | tf_op jit(solution)/shard_map/pallas_call | solution.py:119
  10.9 0.0 copy-done.4
  10.9 0.1 copy.5.columns_ref
  11.0 0.0 copy-start.2
  11.0 1.9 %copy-done.2 = bf16[2,16,3,128,128]{4,3,2,1,0:T(8,128)(2,1)S(1)} copy-done((bf16[2,16,3,128,128]{4,3,2,1,0:T(8,128)(2,1)S(1)}, bf16[2,16,3,128,128]{4,3,2,1,0:T(8,128)(2,1)}, u32[]{:S(2)}) %copy-start.2) | copy-done | bytes 3145752
  12.8 0.0 copy-start.1
  12.9 0.0 copy-start.3
  12.9 4.7 %shard_map.50.folds_ref = bf16[2,512,1024]{2,1,0:T(8,128)(2,1)S(1)} custom-call(s32[2,16,2]{2,1,0:T(8,128)S(1)} %copy.5.columns_ref, bf16[512,2048]{1,0:T(8,128)(2,1)S(1)} %shard_map.47.turned_ref, bf16[2,16,3,128,128]{4,3,2,1,0:T(8,128)(2,1)S(1)} %copy-done.2), custom_call_target="tpu_custom_call" | custom-call | flops 67108864 | bytes 655360 | tf_op jit(solution)/shard_map/pallas_call | solution.py:168
  17.6 0.0 collective-permute-done.refs_0_
  17.6 0.0 collective-permute-done.1.refs_1_
  17.6 0.0 copy-done.1
  17.6 0.0 copy-done.3
  17.6 6.6 %shard_map.49.local_ref = f32[2,512,512]{2,1,0:T(8,128)S(1)} custom-call(s32[2,16,2]{2,1,0:T(8,128)S(1)} %copy.5.columns_ref, bf16[512,2048]{1,0:T(8,128)(2,1)S(1)} %shard_map.47.turned_ref, bf16[16,128,512]{2,1,0:T(8,128)(2,1)S(1)} %copy-done.1, bf16[2,16,3,128,128]{4,3,2,1,0:T(8,128)(2,1)S(1)} %copy-done.3, ...), custom_call_target="tpu_custom_call" | custom-call | flops 469762048 | bytes 1441792 | tf_op jit(solution)/shard_map/pallas_call | solution.py:220
  24.2 0.0 collective-permute-done.2.far_ref
  24.2 0.7 %shard_map.52 = bf16[256,1024]{1,0:T(8,128)(2,1)S(1)} custom-call(f32[2,512,512]{2,1,0:T(8,128)S(1)} %shard_map.49.local_ref, bf16[2,512,1024]{2,1,0:T(8,128)(2,1)S(1)} %shard_map.50.folds_ref, bf16[8,128,512]{2,1,0:T(8,128)(2,1)S(1)} %collective-permute-done.2.far_ref), custom_call_target="tpu_custom_call" | custom-call | flops 67108864 | bytes 393216 | tf_op jit(solution)/shard_map/pallas_call | solution.py:252
  24.9 6.8 %collective-permute-start.3 = (bf16[256,1024]{1,0:T(8,128)(2,1)S(1)}, bf16[256,1024]{1,0:T(8,128)(2,1)S(1)}, u32[]{:S(2)}, u32[]{:S(2)}) collective-permute-start(bf16[256,1024]{1,0:T(8,128)(2,1)S(1)} %shard_map.52), channel_id=1, source_target_pairs={{0,1},{1,0},{2,3},{3,2},{4,5},{5,4},{6,7},{7,6},{8,9},{9,8},{10,11... | collective-permute-start | bytes 1572872 | tf_op jit(solution)/shard_map/ppermute | solution.py:295
  31.7 0.7 %shard_map.51 = f32[256,1024]{1,0:T(8,128)S(1)} custom-call(f32[2,512,512]{2,1,0:T(8,128)S(1)} %shard_map.49.local_ref, bf16[2,512,1024]{2,1,0:T(8,128)(2,1)S(1)} %shard_map.50.folds_ref, bf16[8,128,512]{2,1,0:T(8,128)(2,1)S(1)} %collective-permute-done.2.far_ref), custom_call_target="tpu_custom_call" | custom-call | flops 67108864 | bytes 393216 | tf_op jit(solution)/shard_map/pallas_call | solution.py:252
  32.4 0.8 %collective-permute-done.3 = bf16[256,1024]{1,0:T(8,128)(2,1)S(1)} collective-permute-done((bf16[256,1024]{1,0:T(8,128)(2,1)S(1)}, bf16[256,1024]{1,0:T(8,128)(2,1)S(1)}, u32[]{:S(2)}, u32[]{:S(2)}) %collective-permute-start.3) | collective-permute-done | bytes 524320 | tf_op jit(solution)/shard_map/ppermute | solution.py:295
  33.2 0.1 add_convert_fusion
  33.4 19.0 %all_to_all.5.parts_ref = bf16[8,32,1024]{2,1,0:T(8,128)(2,1)S(1)} all-to-all(bf16[8,32,1024]{2,1,0:T(8,128)(2,1)S(1)} %bitcast.3), channel_id=1, replica_groups={{14,0,12,2,10,4,8,6},{15,1,13,3,11,5,9,7},{30,16,28,18,26,20,24,22},{31..., dimensions={0} | all-to-all | bytes 1048576 | tf_op jit(solution)/shard_map/all_to_all | solution.py:298
  52.4 0.7 %shard_map.53 = f32[32,1024]{1,0:T(8,128)} custom-call(bf16[8,32,1024]{2,1,0:T(8,128)(2,1)S(1)} %all_to_all.5.parts_ref), custom_call_target="tpu_custom_call" | custom-call | bytes 65536 | tf_op jit(solution)/shard_map/pallas_call | solution.py:269
Async XLA Ops:
  2.7 6.7 %copy-start = (bf16[16,128,512]{2,1,0:T(8,128)(2,1)}, bf16[16,128,512]{2,1,0:T(8,128)(2,1)S(1)}, u32[]{:S(2)}) copy-start(bf16[16,128,512]{2,1,0:T(8,128)(2,1)S(1)} %get-tuple-element.9.own_ref) | copy-start | bytes 6291460
  2.7 21.5 %collective-permute-start.2 = (bf16[8,128,512]{2,1,0:T(8,128)(2,1)}, bf16[8,128,512]{2,1,0:T(8,128)(2,1)S(1)}, u32[]{:S(2)}, u32[]{:S(2)}) collective-permute-start(bf16[8,128,512]{2,1,0:T(8,128)(2,1)} %get-tuple-element.12), channel_id=1, source_target_pairs={{1,2},{2,1},{3,4},{4,3},{5,6},{6,5},{7,8},{8,7},{9,10},{10,9},{11,... | collective-permute-start | bytes 3145736 | tf_op jit(solution)/shard_map/ppermute | solution.py:288
  5.1 12.4 %collective-permute-start = (bf16[8,128,256]{2,1,0:T(8,128)(2,1)}, bf16[8,128,256]{2,1,0:T(8,128)(2,1)}, u32[]{:S(2)}, u32[]{:S(2)}) collective-permute-start(bf16[8,128,256]{2,1,0:T(8,128)(2,1)} %get-tuple-element.10), channel_id=1, source_target_pairs={{0,1},{1,0},{2,3},{3,2},{4,5},{5,4},{6,7},{7,6},{8,9},{9,8},{10,11... | collective-permute-start | bytes 1572872 | tf_op jit(solution)/shard_map/ppermute | solution.py:289
  9.4 1.5 %copy-start.4 = (s32[2,16,2]{1,2,0:T(2,128)S(1)}, s32[2,16,2]{1,2,0:T(2,128)}, u32[]{:S(2)}) copy-start(s32[2,16,2]{1,2,0:T(2,128)} %param.6) | copy-start | bytes 772
  9.4 8.2 %collective-permute-start.1 = (bf16[8,128,256]{2,1,0:T(8,128)(2,1)}, bf16[8,128,256]{2,1,0:T(8,128)(2,1)}, u32[]{:S(2)}, u32[]{:S(2)}) collective-permute-start(bf16[8,128,256]{2,1,0:T(8,128)(2,1)} %get-tuple-element.11), channel_id=1, source_target_pairs={{0,1},{1,0},{2,3},{3,2},{4,5},{5,4},{6,7},{7,6},{8,9},{9,8},{10,11... | collective-permute-start | bytes 1572872 | tf_op jit(solution)/shard_map/ppermute | solution.py:289
  11.0 1.9 %copy-start.2 = (bf16[2,16,3,128,128]{4,3,2,1,0:T(8,128)(2,1)S(1)}, bf16[2,16,3,128,128]{4,3,2,1,0:T(8,128)(2,1)}, u32[]{:S(2)}) copy-start(bf16[2,16,3,128,128]{4,3,2,1,0:T(8,128)(2,1)} %blocks_ref.3) | copy-start | bytes 9437188
  12.8 4.7 %copy-start.1 = (bf16[16,128,512]{2,1,0:T(8,128)(2,1)S(1)}, bf16[16,128,512]{2,1,0:T(8,128)(2,1)}, u32[]{:S(2)}) copy-start(bf16[16,128,512]{2,1,0:T(8,128)(2,1)} %copy-done) | copy-start | bytes 6291460
  12.9 4.7 %copy-start.3 = (bf16[2,16,3,128,128]{4,3,2,1,0:T(8,128)(2,1)S(1)}, bf16[2,16,3,128,128]{4,3,2,1,0:T(8,128)(2,1)}, u32[]{:S(2)}) copy-start(bf16[2,16,3,128,128]{4,3,2,1,0:T(8,128)(2,1)} %blocks_ref.3) | copy-start | bytes 9437188
  24.9 8.3 %collective-permute-start.3 = (bf16[256,1024]{1,0:T(8,128)(2,1)S(1)}, bf16[256,1024]{1,0:T(8,128)(2,1)S(1)}, u32[]{:S(2)}, u32[]{:S(2)}) collective-permute-start(bf16[256,1024]{1,0:T(8,128)(2,1)S(1)} %shard_map.52), channel_id=1, source_target_pairs={{0,1},{1,0},{2,3},{3,2},{4,5},{5,4},{6,7},{7,6},{8,9},{9,8},{10,11... | collective-permute-start | bytes 1572872 | tf_op jit(solution)/shard_map/ppermute | solution.py:295

commit v11 on v10

--- a/solution.py
+++ b/solution.py
@@ -26,8 +26,9 @@
 
 
 def chip_order(chips):
-    ends = zip(range(chips - 1, -1, -1), range(chips))
-    return [chip for pair in ends for chip in pair][:chips]
+    low = list(range(0, chips // 2, 2)) + list(range(1, chips // 2, 2))
+    order = [chip for place in low for chip in (chips - 1 - place, place)]
+    return order + [chip for chip in range(chips) if chip not in order]
 
 
 def halves(width):

time: 53.4 us -> 53 us (level)
  no operation moved by 1% of the time
where the time goes in v11:
time: 53 us; the launch traced here: 52.8 us
  Pallas kernels  19.5 us (37%)
  blocking collectives  18.6 us (35%)
  starting transfers between devices  11.5 us (22%)
  local copies, waits for them, and re-layouts  1.99 us (4%)
  waiting for transfers between devices  0.83 us (2%)
    all_to_all x1, blocking collectives, shards(): lax.all_to_all(chip_sum.reshape(chips, width // devices, params * width),...  18.6 us
    pallas_call x1, Pallas kernels, local_parts(): pl.pallas_call(kernel, out_shape=jax.ShapeDtypeStruct((params, width, wid...  6.62 us
    ppermute x1, starting transfers between devices, shards(): taken = lax.ppermute(with_far(local, folds, far, False), AXIS, near_pairs)  6.58 us
    pallas_call x1, Pallas kernels, fold_far(): pl.pallas_call(kernel, out_shape=jax.ShapeDtypeStruct(shape, turned.dtype...  4.87 us
    ppermute x2, starting transfers between devices, shards(): lax.ppermute(near, AXIS, near_pairs)  4.24 us
    pallas_call x1, Pallas kernels, pick_far(): pl.pallas_call(kernel, out_shape=(jax.ShapeDtypeStruct(own.shape, own.dty...  2.66 us
    unnamed x11, local copies, waits for them, and re-layouts  1.99 us
    pallas_call x1, Pallas kernels, pick_near(): pl.pallas_call(kernel, out_shape=[jax.ShapeDtypeStruct((halo, size, span)...  1.71 us
  transfers between devices with their start and end apart: 4, of which 1 were waited for; matrix products, arithmetic and copies ran while one was open for 0% of the time, Pallas kernels for 29%

profile of v11, /device:TPU:0, one launch (start us, length us, event | category | flops | bytes accessed | tf_op | source)
XLA Modules:
  0.0 52.8 jit_solution(14539431592104182042)
XLA Ops:
  0.0 2.7 %shard_map.46 = (bf16[16,128,512]{2,1,0:T(8,128)(2,1)S(1)}, bf16[8,128,512]{2,1,0:T(8,128)(2,1)}) custom-call(s32[1,16]{1,0:T(1,128)} %sends_hbm.3, bf16[16,128,512]{2,1,0:T(8,128)(2,1)} %bitcast.2), custom_call_target="tpu_custom_call" | custom-call | bytes 655360 | tf_op jit(solution)/shard_map/pallas_call | solution.py:54
  2.7 0.0 copy-start
  2.7 0.7 %collective-permute-start.2 = (bf16[8,128,512]{2,1,0:T(8,128)(2,1)}, bf16[8,128,512]{2,1,0:T(8,128)(2,1)S(1)}, u32[]{:S(2)}, u32[]{:S(2)}) collective-permute-start(bf16[8,128,512]{2,1,0:T(8,128)(2,1)} %get-tuple-element.12), channel_id=1, source_target_pairs={{1,2},{2,1},{3,4},{4,3},{5,6},{6,5},{7,8},{8,7},{9,10},{10,9},{11,... | collective-permute-start | bytes 3145736 | tf_op jit(solution)/shard_map/ppermute | solution.py:289
  3.4 1.7 %shard_map.48 = (bf16[8,128,256]{2,1,0:T(8,128)(2,1)}, bf16[8,128,256]{2,1,0:T(8,128)(2,1)}) custom-call(s32[1,16]{1,0:T(1,128)} %sends_hbm.3, bf16[16,128,512]{2,1,0:T(8,128)(2,1)S(1)} %get-tuple-element.9.own_ref), custom_call_target="tpu_custom_call" | custom-call | bytes 262144 | tf_op jit(solution)/shard_map/pallas_call | solution.py:89
  5.1 4.2 %collective-permute-start = (bf16[8,128,256]{2,1,0:T(8,128)(2,1)}, bf16[8,128,256]{2,1,0:T(8,128)(2,1)}, u32[]{:S(2)}, u32[]{:S(2)}) collective-permute-start(bf16[8,128,256]{2,1,0:T(8,128)(2,1)} %get-tuple-element.10), channel_id=1, source_target_pairs={{0,1},{1,0},{2,3},{3,2},{4,5},{5,4},{6,7},{7,6},{8,9},{9,8},{10,11... | collective-permute-start | bytes 1572872 | tf_op jit(solution)/shard_map/ppermute | solution.py:290
  9.4 0.0 copy-start.4
  9.4 0.0 collective-permute-start.1
  9.4 0.0 copy-done
  9.4 1.5 %shard_map.47.turned_ref = bf16[512,2048]{1,0:T(8,128)(2,1)S(1)} custom-call(bf16[16,128,512]{2,1,0:T(8,128)(2,1)S(1)} %get-tuple-element.9.own_ref), custom_call_target="tpu_custom_call" | custom-call | bytes 524288 | tf_op jit(solution)/shard_map/pallas_call | solution.py:120
  10.9 0.0 copy-done.4
  10.9 0.1 copy.5.columns_ref
  11.0 0.0 copy-start.2
  11.0 1.9 %copy-done.2 = bf16[2,16,3,128,128]{4,3,2,1,0:T(8,128)(2,1)S(1)} copy-done((bf16[2,16,3,128,128]{4,3,2,1,0:T(8,128)(2,1)S(1)}, bf16[2,16,3,128,128]{4,3,2,1,0:T(8,128)(2,1)}, u32[]{:S(2)}) %copy-start.2) | copy-done | bytes 3145752
  12.8 0.0 copy-start.1
  12.9 0.0 copy-start.3
  12.9 4.9 %shard_map.50.folds_ref = bf16[2,512,1024]{2,1,0:T(8,128)(2,1)S(1)} custom-call(s32[2,16,2]{2,1,0:T(8,128)S(1)} %copy.5.columns_ref, bf16[512,2048]{1,0:T(8,128)(2,1)S(1)} %shard_map.47.turned_ref, bf16[2,16,3,128,128]{4,3,2,1,0:T(8,128)(2,1)S(1)} %copy-done.2), custom_call_target="tpu_custom_call" | custom-call | flops 67108864 | bytes 655360 | tf_op jit(solution)/shard_map/pallas_call | solution.py:169
  17.7 0.0 collective-permute-done.refs_0_
  17.7 0.0 collective-permute-done.1.refs_1_
  17.8 0.0 copy-done.1
  17.8 0.0 copy-done.3
  17.8 6.6 %shard_map.49.local_ref = f32[2,512,512]{2,1,0:T(8,128)S(1)} custom-call(s32[2,16,2]{2,1,0:T(8,128)S(1)} %copy.5.columns_ref, bf16[512,2048]{1,0:T(8,128)(2,1)S(1)} %shard_map.47.turned_ref, bf16[16,128,512]{2,1,0:T(8,128)(2,1)S(1)} %copy-done.1, bf16[2,16,3,128,128]{4,3,2,1,0:T(8,128)(2,1)S(1)} %copy-done.3, ...), custom_call_target="tpu_custom_call" | custom-call | flops 469762048 | bytes 1441792 | tf_op jit(solution)/shard_map/pallas_call | solution.py:221
  24.4 0.0 collective-permute-done.2.far_ref
  24.4 0.7 %shard_map.52 = bf16[256,1024]{1,0:T(8,128)(2,1)S(1)} custom-call(f32[2,512,512]{2,1,0:T(8,128)S(1)} %shard_map.49.local_ref, bf16[2,512,1024]{2,1,0:T(8,128)(2,1)S(1)} %shard_map.50.folds_ref, bf16[8,128,512]{2,1,0:T(8,128)(2,1)S(1)} %collective-permute-done.2.far_ref), custom_call_target="tpu_custom_call" | custom-call | flops 67108864 | bytes 393216 | tf_op jit(solution)/shard_map/pallas_call | solution.py:253
  25.1 6.6 %collective-permute-start.3 = (bf16[256,1024]{1,0:T(8,128)(2,1)S(1)}, bf16[256,1024]{1,0:T(8,128)(2,1)S(1)}, u32[]{:S(2)}, u32[]{:S(2)}) collective-permute-start(bf16[256,1024]{1,0:T(8,128)(2,1)S(1)} %shard_map.52), channel_id=1, source_target_pairs={{0,1},{1,0},{2,3},{3,2},{4,5},{5,4},{6,7},{7,6},{8,9},{9,8},{10,11... | collective-permute-start | bytes 1572872 | tf_op jit(solution)/shard_map/ppermute | solution.py:296
  31.7 0.7 %shard_map.51 = f32[256,1024]{1,0:T(8,128)S(1)} custom-call(f32[2,512,512]{2,1,0:T(8,128)S(1)} %shard_map.49.local_ref, bf16[2,512,1024]{2,1,0:T(8,128)(2,1)S(1)} %shard_map.50.folds_ref, bf16[8,128,512]{2,1,0:T(8,128)(2,1)S(1)} %collective-permute-done.2.far_ref), custom_call_target="tpu_custom_call" | custom-call | flops 67108864 | bytes 393216 | tf_op jit(solution)/shard_map/pallas_call | solution.py:253
  32.4 0.8 %collective-permute-done.3 = bf16[256,1024]{1,0:T(8,128)(2,1)S(1)} collective-permute-done((bf16[256,1024]{1,0:T(8,128)(2,1)S(1)}, bf16[256,1024]{1,0:T(8,128)(2,1)S(1)}, u32[]{:S(2)}, u32[]{:S(2)}) %collective-permute-start.3) | collective-permute-done | bytes 524320 | tf_op jit(solution)/shard_map/ppermute | solution.py:296
  33.2 0.1 add_convert_fusion
  33.4 18.6 %all_to_all.5.parts_ref = bf16[8,32,1024]{2,1,0:T(8,128)(2,1)S(1)} all-to-all(bf16[8,32,1024]{2,1,0:T(8,128)(2,1)S(1)} %bitcast.3), channel_id=1, replica_groups={{14,0,10,4,12,2,8,6},{15,1,11,5,13,3,9,7},{30,16,26,20,28,18,24,22},{31..., dimensions={0} | all-to-all | bytes 1048576 | tf_op jit(solution)/shard_map/all_to_all | solution.py:299
  52.0 0.7 %shard_map.53 = f32[32,1024]{1,0:T(8,128)} custom-call(bf16[8,32,1024]{2,1,0:T(8,128)(2,1)S(1)} %all_to_all.5.parts_ref), custom_call_target="tpu_custom_call" | custom-call | bytes 65536 | tf_op jit(solution)/shard_map/pallas_call | solution.py:270
Async XLA Ops:
  2.7 6.7 %copy-start = (bf16[16,128,512]{2,1,0:T(8,128)(2,1)}, bf16[16,128,512]{2,1,0:T(8,128)(2,1)S(1)}, u32[]{:S(2)}) copy-start(bf16[16,128,512]{2,1,0:T(8,128)(2,1)S(1)} %get-tuple-element.9.own_ref) | copy-start | bytes 6291460
  2.7 21.7 %collective-permute-start.2 = (bf16[8,128,512]{2,1,0:T(8,128)(2,1)}, bf16[8,128,512]{2,1,0:T(8,128)(2,1)S(1)}, u32[]{:S(2)}, u32[]{:S(2)}) collective-permute-start(bf16[8,128,512]{2,1,0:T(8,128)(2,1)} %get-tuple-element.12), channel_id=1, source_target_pairs={{1,2},{2,1},{3,4},{4,3},{5,6},{6,5},{7,8},{8,7},{9,10},{10,9},{11,... | collective-permute-start | bytes 3145736 | tf_op jit(solution)/shard_map/ppermute | solution.py:289
  5.1 12.6 %collective-permute-start = (bf16[8,128,256]{2,1,0:T(8,128)(2,1)}, bf16[8,128,256]{2,1,0:T(8,128)(2,1)}, u32[]{:S(2)}, u32[]{:S(2)}) collective-permute-start(bf16[8,128,256]{2,1,0:T(8,128)(2,1)} %get-tuple-element.10), channel_id=1, source_target_pairs={{0,1},{1,0},{2,3},{3,2},{4,5},{5,4},{6,7},{7,6},{8,9},{9,8},{10,11... | collective-permute-start | bytes 1572872 | tf_op jit(solution)/shard_map/ppermute | solution.py:290
  9.4 1.5 %copy-start.4 = (s32[2,16,2]{1,2,0:T(2,128)S(1)}, s32[2,16,2]{1,2,0:T(2,128)}, u32[]{:S(2)}) copy-start(s32[2,16,2]{1,2,0:T(2,128)} %param.6) | copy-start | bytes 772
  9.4 8.4 %collective-permute-start.1 = (bf16[8,128,256]{2,1,0:T(8,128)(2,1)}, bf16[8,128,256]{2,1,0:T(8,128)(2,1)}, u32[]{:S(2)}, u32[]{:S(2)}) collective-permute-start(bf16[8,128,256]{2,1,0:T(8,128)(2,1)} %get-tuple-element.11), channel_id=1, source_target_pairs={{0,1},{1,0},{2,3},{3,2},{4,5},{5,4},{6,7},{7,6},{8,9},{9,8},{10,11... | collective-permute-start | bytes 1572872 | tf_op jit(solution)/shard_map/ppermute | solution.py:290
  11.0 1.9 %copy-start.2 = (bf16[2,16,3,128,128]{4,3,2,1,0:T(8,128)(2,1)S(1)}, bf16[2,16,3,128,128]{4,3,2,1,0:T(8,128)(2,1)}, u32[]{:S(2)}) copy-start(bf16[2,16,3,128,128]{4,3,2,1,0:T(8,128)(2,1)} %blocks_ref.3) | copy-start | bytes 9437188
  12.8 4.9 %copy-start.1 = (bf16[16,128,512]{2,1,0:T(8,128)(2,1)S(1)}, bf16[16,128,512]{2,1,0:T(8,128)(2,1)}, u32[]{:S(2)}) copy-start(bf16[16,128,512]{2,1,0:T(8,128)(2,1)} %copy-done) | copy-start | bytes 6291460
  12.9 4.9 %copy-start.3 = (bf16[2,16,3,128,128]{4,3,2,1,0:T(8,128)(2,1)S(1)}, bf16[2,16,3,128,128]{4,3,2,1,0:T(8,128)(2,1)}, u32[]{:S(2)}) copy-start(bf16[2,16,3,128,128]{4,3,2,1,0:T(8,128)(2,1)} %blocks_ref.3) | copy-start | bytes 9437188
  25.1 8.1 %collective-permute-start.3 = (bf16[256,1024]{1,0:T(8,128)(2,1)S(1)}, bf16[256,1024]{1,0:T(8,128)(2,1)S(1)}, u32[]{:S(2)}, u32[]{:S(2)}) collective-permute-start(bf16[256,1024]{1,0:T(8,128)(2,1)S(1)} %shard_map.52), channel_id=1, source_target_pairs={{0,1},{1,0},{2,3},{3,2},{4,5},{5,4},{6,7},{7,6},{8,9},{9,8},{10,11... | collective-permute-start | bytes 1572872 | tf_op jit(solution)/shard_map/ppermute | solution.py:296
